TPU v7x, 256 devices: a whole 4x4x8 slice. The times are simulated.
256 devices in a mesh: row: 4 (over y), col: 16 (over z, core), layer: 4 (over x).
Axes of the slice: x: 4, y: 4, z: 8, core: 2. Of those that a mesh axis runs over, the one named last changes fastest.
Arguments:
- density: bfloat16 [8192, 4, 2048], P('row', 'layer', 'col'), may hold values from -6 to 6
- response: bfloat16 [4, 2048, 8192], P('layer', 'row', 'col'), may hold values from -0.125 to 0.125
- density_mask: int32 [64, 4, 16], P('row', 'layer', 'col'), may hold values 0 or 1
- response_mask: int32 [4, 16, 64], P('layer', 'row', 'col'), may hold values 0 or 1
- result_mask: int32 [64, 64], P('row', 'col'), may hold values 0 or 1
Outputs:
- perturbed: bfloat16 [16, 16, 32, 8192], P(('row', 'layer'), 'col')
All inputs are finite; a program needn't handle non-finite values. No bound on the sum of `density_mask` or of `response_mask` or of `result_mask` on one device may be relied on, other than what follows from the above.
Results may differ from a plain program's by a relative error of at most 0.0042.
Values may be sent and summed in bfloat16 or wider, within the bound.
No kernel may reach another device: no remote copies, remote signals or barrier semaphores. Data moves between devices by JAX's collectives and lax.ppermute only.
A program may use at most 64 MiB of HBM per device.

v0:
```python
import jax
import jax.numpy as jnp
from jax import lax
from jax.experimental import pallas as pl
from jax.experimental.pallas import tpu as pltpu
from jax.sharding import PartitionSpec as P

NQ = 2
MQ = 2048 // NQ
TAIL = 16
BF = jnp.bfloat16
F32 = jnp.float32
VMEM = pltpu.VMEM
WHOLE = pl.BlockSpec(memory_space=pltpu.VMEM)
SCALARS = pl.BlockSpec(memory_space=pltpu.SMEM)
ANYWHERE = pl.BlockSpec(memory_space=pl.ANY)


def params(mib=48):
    return pltpu.CompilerParams(vmem_limit_bytes=mib * 1024 * 1024)


def cost(flops, moved):
    return pl.CostEstimate(flops=flops, bytes_accessed=moved, transcendentals=0)


def position():
    place = lax.axis_index("col")
    return lax.axis_index("row"), place // 2, place % 2, lax.axis_index("layer")


def rows_of(q):
    return MQ + TAIL if q == 0 else MQ


def prep_a_kernel(dm, a, rm, *rest):
    outs, spare = rest[:NQ], rest[NQ]
    per = 4 // NQ
    for q in range(NQ):
        for xb in range(4):
            for j in range(per):
                block = xb * 4 + q * per + j
                keep = dm[block].astype(F32)
                value = a[block * 128 : (block + 1) * 128, :].astype(F32) * keep
                at = (xb * per + j) * 128
                outs[q][at : at + 128, :] = value.astype(BF)
    spare[...] = jnp.zeros_like(spare)
    spare[0:4, 0:16] = rm[...].astype(F32)
    outs[0][MQ : MQ + TAIL, :] = spare[...].astype(BF)


def prep_a(a, dm, rm):
    return pl.pallas_call(
        prep_a_kernel,
        out_shape=[jax.ShapeDtypeStruct((rows_of(q), 128), BF) for q in range(NQ)],
        in_specs=[SCALARS, WHOLE, WHOLE],
        out_specs=[WHOLE] * NQ,
        scratch_shapes=[VMEM((TAIL, 128), F32)],
        compiler_params=params(),
        cost_estimate=cost(2048 * 128, 2 * 2048 * 128 * 2),
    )(dm, a, rm)


def prep_b_kernel(mask, b, out):
    for tb in range(4):
        for cb in range(4):
            keep = mask[tb, cb].astype(F32)
            block = b[tb * 128 : (tb + 1) * 128, cb * 128 : (cb + 1) * 128].astype(F32) * keep
            flipped = block.T.astype(BF)
            lanes = slice((tb // 2) * 128, (tb // 2 + 1) * 128)
            for e in range(2):
                out[(2 * cb + e) * 2 + tb % 2, :, lanes] = flipped[e * 64 : (e + 1) * 64, :]


def prep_b(b, mask):
    return pl.pallas_call(
        prep_b_kernel,
        out_shape=jax.ShapeDtypeStruct((16, 64, 256), BF),
        in_specs=[SCALARS, WHOLE],
        out_specs=WHOLE,
        compiler_params=params(),
        cost_estimate=cost(512 * 512, 2 * 512 * 512 * 2),
    )(mask, b)


def load_and_multiply(q, half, pieces, bs, a_full, b_full, sems, tails):
    y, z, core, _ = position()
    copies = []
    bands = (slice(0, 16), slice(0, 16), slice(0, 16), slice(0, 8), slice(8, 16))
    for s, back in enumerate((0, 1, 3, 2, 2)):
        y0 = lax.rem(y - back + 4, 4)
        copies.append(pltpu.make_async_copy(bs[s].at[:, half], b_full.at[y0, bands[s]], sems.at[8 + s]))
    for s in range(8):
        z0 = lax.rem(z - s + 8, 8)
        lanes = pl.ds(pl.multiple_of(z0 * 128, 128), 128)
        copies.append(pltpu.make_async_copy(pieces[s].at[0:MQ], a_full.at[:, lanes], sems.at[s]))
    if q == 0:
        for s in range(8):
            copies.append(pltpu.make_async_copy(pieces[s].at[MQ : MQ + TAIL], tails.at[s], sems.at[13 + s]))
    for copy in copies:
        copy.start()
    for copy in copies:
        copy.wait()
    total = None
    for y0 in range(4):
        term = lax.dot_general(
            a_full[:, y0 * 256 : (y0 + 1) * 256],
            b_full[y0].reshape(512, 256),
            (((1,), (1,)), ((), ())),
            preferred_element_type=F32,
        )
        total = term if total is None else total + term
    return total


def mask_rows(tails):
    _, z, core, _ = position()
    row = lax.broadcasted_iota(jnp.int32, (TAIL, 128), 0)
    lane = lax.broadcasted_iota(jnp.int32, (TAIL, 128), 1)
    wide = lax.broadcasted_iota(jnp.int32, (TAIL, 512), 1) // 32
    mask = jnp.zeros((TAIL, 512), F32)
    for s in range(8):
        z0 = lax.rem(z - s + 8, 8)
        values = tails[s].astype(F32)
        chosen = jnp.sum(jnp.where(row == z // 2, values, 0.0), axis=0, keepdims=True)
        column = jnp.sum(jnp.where(row == lane, chosen, 0.0), axis=1, keepdims=True)
        mask = jnp.where(wide == 2 * z0 + core, column, mask)
    return mask


def send_kernel(q, *refs):
    pieces, bs, out = refs[:8], refs[8:13], refs[13]
    a_full, b_full, tails, sems = refs[14:]
    core = position()[2]
    total = load_and_multiply(q, 1 - core, pieces, bs, a_full, b_full, sems, tails)
    out[0:MQ, :] = total.astype(BF)
    if q == 0:
        out[MQ : MQ + TAIL, :] = mask_rows(tails).astype(BF)


def scratches():
    return [
        VMEM((MQ, 1024), BF),
        VMEM((4, 16, 32, 256), BF),
        VMEM((8, TAIL, 128), BF),
        pltpu.SemaphoreType.DMA((21,)),
    ]


def send_half(q, pieces, bs):
    return pl.pallas_call(
        lambda *refs: send_kernel(q, *refs),
        out_shape=jax.ShapeDtypeStruct((rows_of(q), 512), BF),
        in_specs=[ANYWHERE] * 13,
        out_specs=WHOLE,
        scratch_shapes=scratches(),
        compiler_params=params(),
        cost_estimate=cost(2 * MQ * 1024 * 512, MQ * 1024 * 2 + 1024 * 1024),
    )(*pieces, *bs)


def keep_kernel(q, *refs):
    pieces, bs, received = refs[:8], refs[8:13], refs[13]
    own, outs = refs[14], refs[15:18]
    rest = refs[18:]
    if q == 0:
        mask, rest = rest[0], rest[1:]
    a_full, b_full, tails, sems, total = rest
    _, _, core, x = position()
    part = load_and_multiply(q, core, pieces, bs, a_full, b_full, sems, tails)
    total[...] = (part + received[0:MQ, :].astype(F32)).reshape(4, MQ // 4, 512)
    own[...] = total[x]
    for s in range(1, 4):
        outs[s - 1][...] = total[lax.rem(x + s, 4)].astype(BF)
    if q == 0:
        mask[...] = mask_rows(tails) + received[MQ : MQ + TAIL, :].astype(F32)


def keep_half(q, pieces, bs, received):
    part = (MQ // 4, 512)
    shapes = [jax.ShapeDtypeStruct(part, F32)] + [jax.ShapeDtypeStruct(part, BF)] * 3
    if q == 0:
        shapes.append(jax.ShapeDtypeStruct((TAIL, 512), F32))
    return pl.pallas_call(
        lambda *refs: keep_kernel(q, *refs),
        out_shape=shapes,
        in_specs=[ANYWHERE] * 13 + [WHOLE],
        out_specs=[WHOLE] * len(shapes),
        scratch_shapes=scratches() + [VMEM((4, MQ // 4, 512), F32)],
        compiler_params=params(),
        cost_estimate=cost(2 * MQ * 1024 * 512, MQ * 1024 * 2 + 2 * 1024 * 1024),
    )(*pieces, *bs, received)


def sum_kernel(*refs):
    mask, parts, out, flipped = refs[0], refs[1:-2], refs[-2], refs[-1]
    x = position()[3]
    for q in range(NQ):
        own, first, second, third = parts[4 * q : 4 * q + 4]
        for j in range(4 // NQ):
            block = q * (4 // NQ) + j
            rows = slice(j * 128, (j + 1) * 128)
            value = own[rows, :] + first[rows, :].astype(F32) + second[rows, :].astype(F32) + third[rows, :].astype(F32)
            value = value * mask[pl.ds(x * 4 + block, 1), :]
            out[block * 128 : (block + 1) * 128, :] = value.astype(BF)
            flipped[:, block * 128 : (block + 1) * 128] = value.T.astype(BF)


def sum_parts(mask, parts):
    return pl.pallas_call(
        sum_kernel,
        out_shape=[jax.ShapeDtypeStruct((512, 512), BF)] * 2,
        in_specs=[WHOLE] * (1 + len(parts)),
        out_specs=[WHOLE] * 2,
        compiler_params=params(),
        cost_estimate=cost(512 * 512 * 5, 512 * 512 * 14),
    )(mask, *parts)


def final_kernel(own, mirrored, out):
    group = lax.broadcasted_iota(jnp.int32, (32, 128), 1) // 32
    for k_high in range(4):
        for b_high in range(4):
            sources = [own[4 * k_high + k, :, b_high * 128 : (b_high + 1) * 128].astype(F32) for k in range(4)]
            for b in range(4):
                value = None
                for k in range(4):
                    shift = ((k - b) % 4) * 32
                    turned = pltpu.roll(sources[k], shift, 1) if shift else sources[k]
                    value = turned if value is None else jnp.where(group == k, turned, value)
                band = b_high * 4 + b
                value = value + mirrored[band, :, k_high * 128 : (k_high + 1) * 128].astype(F32)
                at = band * 512 + k_high * 128
                out[:, at : at + 128] = value.astype(BF)


def finish(own, mirrored):
    return pl.pallas_call(
        final_kernel,
        out_shape=jax.ShapeDtypeStruct((32, 8192), BF),
        in_specs=[WHOLE] * 2,
        out_specs=WHOLE,
        compiler_params=params(),
        cost_estimate=cost(32 * 8192 * 8, 3 * 32 * 8192 * 2),
    )(own, mirrored)


def turn_z(value, shift):
    pairs = [(2 * z + c, 2 * ((z + shift) % 8) + c) for z in range(8) for c in range(2)]
    return lax.ppermute(value, "col", pairs)


def turn(value, axis, shift):
    return lax.ppermute(value, axis, [(i, (i + shift) % 4) for i in range(4)])


def per_device(density, response, density_mask, response_mask, result_mask):
    chunks = prep_a(density.reshape(2048, 128), density_mask.reshape(16), result_mask.T)
    chunks, response = lax.optimization_barrier((chunks, response))
    b_send = prep_b(response.reshape(512, 512), response_mask.reshape(4, 4))

    b_own = lax.all_to_all(b_send, "col", 0, 0)
    behind, ahead = turn(b_own, "row", 1), turn(b_own, "row", -1)
    bs = [b_own, behind, ahead, turn(behind[:8], "row", 1), turn(ahead[8:], "row", -1)]
    bs = [value.reshape(-1, 2, 32, 256) for value in bs]

    gathered = [{0: chunk} for chunk in chunks]
    for step in range(1, 5):
        for q in range(NQ):
            got = gathered[q]
            if step < 4 or q % 2 == 0:
                got[step] = turn_z(got[step - 1], 1)
            if step < 4 or q % 2 == 1:
                got[8 - step] = turn_z(got[(9 - step) % 8], -1)

    parts = []
    mask = None
    for q in range(NQ):
        pieces = [gathered[q][s] for s in range(8)]
        other = send_half(q, pieces, bs)
        received = lax.ppermute(other, "col", [(i, i ^ 1) for i in range(16)])
        kept = keep_half(q, pieces, bs, received)
        if q == 0:
            mask = kept[4]
        parts += [kept[0]] + [turn(kept[s], "layer", s) for s in (1, 2, 3)]

    product, flipped = sum_parts(mask, parts)
    own = lax.all_to_all(product.reshape(16, 32, 512), "col", 0, 0)
    mirrored = lax.all_to_all(flipped.reshape(16, 32, 512), ("row", "layer"), 0, 0)
    return finish(own, mirrored).reshape(1, 1, 32, 8192)


def solution(mesh):
    placed = (
        P("row", "layer", "col"),
        P("layer", "row", "col"),
        P("row", "layer", "col"),
        P("layer", "row", "col"),
        P("row", "col"),
    )
    return jax.shard_map(
        per_device,
        mesh=mesh,
        in_specs=placed,
        out_specs=P(("row", "layer"), "col", None, None),
        check_vma=False,
    )
```

profile of v0, /device:TPU:1, one launch (start us, length us, event | category | flops | bytes accessed | tf_op | source)
XLA Modules:
  0.0 156.3 jit_solution(2326154835222467420)
XLA Ops:
  4.7 1.6 %shard_map.56 = bf16[16,64,256]{2,1,0:T(8,128)(2,1)} custom-call(s32[4,4]{1,0:T(4,128)S(1)} %bitcast.38, bf16[512,512]{1,0:T(8,128)(2,1)S(1)} %bitcast.34), custom_call_target="tpu_custom_call" | custom-call | flops 262144 | bytes 1048576 | tf_op jit(solution)/shard_map/pallas_call | solution.py:76
  6.3 10.0 %all-to-all-start = ((bf16[16,64,256]{2,1,0:T(8,128)(2,1)}), bf16[16,64,256]{2,1,0:T(8,128)(2,1)S(1)}, u32[]{:S(2)}, u32[]{:S(2)}) async-start(bf16[16,64,256]{2,1,0:T(8,128)(2,1)} %shard_map.56), calls=%async_computation | async-start | bytes 1048576 | tf_op jit(solution)/shard_map/all_to_all | solution.py:262
  16.3 2.6 %collective-permute-start.18 = (bf16[1024,128]{1,0:T(8,128)(2,1)S(1)}, bf16[1024,128]{1,0:T(8,128)(2,1)S(1)}, u32[]{:S(2)}, u32[]{:S(2)}) collective-permute-start(bf16[1024,128]{1,0:T(8,128)(2,1)S(1)} %get-tuple-element.30.refs_0_), channel_id=1, source_target_pairs={{0,56},{4,60},{8,0},{12,4},{16,8},{20,12},{24,16},{28,20},{32,24},... | collective-permute-start | bytes 786440 | tf_op jit(solution)/shard_map/ppermute | solution.py:250
  19.2 2.5 %collective-permute-start.4 = (bf16[1040,128]{1,0:T(8,128)(2,1)S(1)}, bf16[1040,128]{1,0:T(8,128)(2,1)S(1)}, u32[]{:S(2)}, u32[]{:S(2)}) collective-permute-start(bf16[1040,128]{1,0:T(8,128)(2,1)S(1)} %get-tuple-element.23.refs_0_), channel_id=1, source_target_pairs={{0,56},{4,60},{8,0},{12,4},{16,8},{20,12},{24,16},{28,20},{32,24},... | collective-permute-start | bytes 798728 | tf_op jit(solution)/shard_map/ppermute | solution.py:250
  21.6 13.9 %collective-permute-done.18.refs_7_ = bf16[1024,128]{1,0:T(8,128)(2,1)S(1)} collective-permute-done((bf16[1024,128]{1,0:T(8,128)(2,1)S(1)}, bf16[1024,128]{1,0:T(8,128)(2,1)S(1)}, u32[]{:S(2)}, u32[]{:S(2)}) %collective-permute-start.18) | collective-permute-done | bytes 262176 | tf_op jit(solution)/shard_map/ppermute | solution.py:250
  35.6 1.5 collective-permute-start.19
  37.1 5.3 %collective-permute-done.15.refs_1_ = bf16[1024,128]{1,0:T(8,128)(2,1)S(1)} collective-permute-done((bf16[1024,128]{1,0:T(8,128)(2,1)S(1)}, bf16[1024,128]{1,0:T(8,128)(2,1)S(1)}, u32[]{:S(2)}, u32[]{:S(2)}) %collective-permute-start.15) | collective-permute-done | bytes 262176 | tf_op jit(solution)/shard_map/ppermute | solution.py:250
  42.4 1.3 collective-permute-start.7
  43.7 1.5 collective-permute-start.8
  46.9 1.5 collective-permute-start.20
  48.4 2.2 %collective-permute-done.16.refs_2_ = bf16[1024,128]{1,0:T(8,128)(2,1)S(1)} collective-permute-done((bf16[1024,128]{1,0:T(8,128)(2,1)S(1)}, bf16[1024,128]{1,0:T(8,128)(2,1)S(1)}, u32[]{:S(2)}, u32[]{:S(2)}) %collective-permute-start.16) | collective-permute-done | bytes 262176 | tf_op jit(solution)/shard_map/ppermute | solution.py:250
  50.6 5.7 %collective-permute-done.1.refs_2_ = bf16[1040,128]{1,0:T(8,128)(2,1)S(1)} collective-permute-done((bf16[1040,128]{1,0:T(8,128)(2,1)S(1)}, bf16[1040,128]{1,0:T(8,128)(2,1)S(1)}, u32[]{:S(2)}, u32[]{:S(2)}) %collective-permute-start.1) | collective-permute-done | bytes 266272 | tf_op jit(solution)/shard_map/ppermute | solution.py:250
  56.3 2.7 %collective-permute-start.21 = (bf16[1024,128]{1,0:T(8,128)(2,1)S(1)}, bf16[1024,128]{1,0:T(8,128)(2,1)S(1)}, u32[]{:S(2)}, u32[]{:S(2)}) collective-permute-start(bf16[1024,128]{1,0:T(8,128)(2,1)S(1)} %collective-permute-done.20.refs_5_), channel_id=1, source_target_pairs={{0,56},{4,60},{8,0},{12,4},{16,8},{20,12},{24,16},{28,20},{32,24},... | collective-permute-start | bytes 786440 | tf_op jit(solution)/shard_map/ppermute | solution.py:250
  59.1 1.4 collective-permute-start.9
  60.5 1.7 %collective-permute-start.10 = (bf16[8,64,256]{2,1,0:T(8,128)(2,1)S(1)}, bf16[8,64,256]{2,1,0:T(8,128)(2,1)S(1)}, u32[]{:S(2)}, u32[]{:S(2)}) collective-permute-start(bf16[8,64,256]{2,1,0:T(8,128)(2,1)S(1)} %slice.9), channel_id=1, source_target_pairs={{0,192},{64,0},{128,64},{192,128},{1,193},{65,1},{129,65},{193,129... | collective-permute-start | bytes 786440 | tf_op jit(solution)/shard_map/ppermute | solution.py:254
  62.2 7.0 %collective-permute-done.17.refs_3_ = bf16[1024,128]{1,0:T(8,128)(2,1)S(1)} collective-permute-done((bf16[1024,128]{1,0:T(8,128)(2,1)S(1)}, bf16[1024,128]{1,0:T(8,128)(2,1)S(1)}, u32[]{:S(2)}, u32[]{:S(2)}) %collective-permute-start.17) | collective-permute-done | bytes 262176 | tf_op jit(solution)/shard_map/ppermute | solution.py:250
  69.2 1.5 collective-permute-start.3
  70.7 2.2 %shard_map.59 = bf16[1024,512]{1,0:T(8,128)(2,1)S(1)} custom-call(bf16[1024,128]{1,0:T(8,128)(2,1)S(1)} %get-tuple-element.30.refs_0_, bf16[1024,128]{1,0:T(8,128)(2,1)S(1)} %collective-permute-done.15.refs_1_, bf16[1024,128]{1,0:T(8,128)(2,1)S(1)} %collective-permute-done.16.refs_2_, bf16[1024,128]{1,0:T(8,128)(2,1)S(1)} %collective-permute-done.17.refs_3_, ...), custom_call_target="tpu_custom_call" | custom-call | flops 1073741824 | bytes 3145728 | tf_op jit(solution)/shard_map/pallas_call | solution.py:151
  73.0 3.3 %collective-permute-start.22 = (bf16[1024,512]{1,0:T(8,128)(2,1)S(1)}, bf16[1024,512]{1,0:T(8,128)(2,1)S(1)}, u32[]{:S(2)}, u32[]{:S(2)}) collective-permute-start(bf16[1024,512]{1,0:T(8,128)(2,1)S(1)} %shard_map.59), channel_id=1, source_target_pairs={{0,4},{4,0},{8,12},{12,8},{16,20},{20,16},{24,28},{28,24},{32,36},... | collective-permute-start | bytes 3145736 | tf_op jit(solution)/shard_map/ppermute | solution.py:281
  76.3 2.3 %shard_map.57 = bf16[1040,512]{1,0:T(8,128)(2,1)S(1)} custom-call(bf16[1040,128]{1,0:T(8,128)(2,1)S(1)} %get-tuple-element.23.refs_0_, bf16[1040,128]{1,0:T(8,128)(2,1)S(1)} %collective-permute-done.refs_1_, bf16[1040,128]{1,0:T(8,128)(2,1)S(1)} %collective-permute-done.1.refs_2_, bf16[1040,128]{1,0:T(8,128)(2,1)S(1)} %collective-permute-done.2.refs_3_, ...), custom_call_target="tpu_custom_call" | custom-call | flops 1073741824 | bytes 3145728 | tf_op jit(solution)/shard_map/pallas_call | solution.py:151
  78.6 3.3 %collective-permute-start.11 = (bf16[1040,512]{1,0:T(8,128)(2,1)S(1)}, bf16[1040,512]{1,0:T(8,128)(2,1)S(1)}, u32[]{:S(2)}, u32[]{:S(2)}) collective-permute-start(bf16[1040,512]{1,0:T(8,128)(2,1)S(1)} %shard_map.57), channel_id=1, source_target_pairs={{0,4},{4,0},{8,12},{12,8},{16,20},{20,16},{24,28},{28,24},{32,36},... | collective-permute-start | bytes 3194888 | tf_op jit(solution)/shard_map/ppermute | solution.py:281
  82.9 3.6 %shard_map.60 = (f32[256,512]{1,0:T(8,128)S(1)}, bf16[256,512]{1,0:T(8,128)(2,1)S(1)}, bf16[256,512]{1,0:T(8,128)(2,1)S(1)}, bf16[256,512]{1,0:T(8,128)(2,1)S(1)}) custom-call(bf16[1024,128]{1,0:T(8,128)(2,1)S(1)} %get-tuple-element.30.refs_0_, bf16[1024,128]{1,0:T(8,128)(2,1)S(1)} %collective-permute-done.15.refs_1_, ...), custom_call_target="tpu_custom_call" | custom-call | flops 1073741824 | bytes 4194304 | tf_op jit(solution)/shard_map/pallas_call | solution.py:184
  86.5 1.3 collective-permute-start.23
  87.8 2.4 %collective-permute-start.24 = (bf16[256,512]{1,0:T(8,128)(2,1)S(1)}, bf16[256,512]{1,0:T(8,128)(2,1)S(1)}, u32[]{:S(2)}, u32[]{:S(2)}) collective-permute-start(bf16[256,512]{1,0:T(8,128)(2,1)S(1)} %get-tuple-element.33), channel_id=1, source_target_pairs={{0,2},{1,3},{2,0},{3,1},{4,6},{5,7},{6,4},{7,5},{8,10},{9,11},{10,... | collective-permute-start | bytes 786440 | tf_op jit(solution)/shard_map/ppermute | solution.py:254
  92.4 3.7 %shard_map.58 = (f32[256,512]{1,0:T(8,128)S(1)}, bf16[256,512]{1,0:T(8,128)(2,1)S(1)}, bf16[256,512]{1,0:T(8,128)(2,1)S(1)}, bf16[256,512]{1,0:T(8,128)(2,1)S(1)}, f32[16,512]{1,0:T(8,128)S(1)}) custom-call(bf16[1040,128]{1,0:T(8,128)(2,1)S(1)} %get-tuple-element.23.refs_0_, bf16[1040,128]{1,0:T(8,128)(2,1)S(1)} %collective-permute-done.refs_1_, ...), custom_call_target="tpu_custom_call" | custom-call | flops 1073741824 | bytes 4194304 | tf_op jit(solution)/shard_map/pallas_call | solution.py:184
  97.3 1.6 %collective-permute-start.14 = (bf16[256,512]{1,0:T(8,128)(2,1)S(1)}, bf16[256,512]{1,0:T(8,128)(2,1)S(1)}, u32[]{:S(2)}, u32[]{:S(2)}) collective-permute-start(bf16[256,512]{1,0:T(8,128)(2,1)S(1)} %get-tuple-element.29), channel_id=1, source_target_pairs={{0,3},{1,0},{2,1},{3,2},{4,7},{5,4},{6,5},{7,6},{8,11},{9,8},{10,9... | collective-permute-start | bytes 786440 | tf_op jit(solution)/shard_map/ppermute | solution.py:254
  98.9 3.4 %collective-permute-done.24.refs_7_ = bf16[256,512]{1,0:T(8,128)(2,1)S(1)} collective-permute-done((bf16[256,512]{1,0:T(8,128)(2,1)S(1)}, bf16[256,512]{1,0:T(8,128)(2,1)S(1)}, u32[]{:S(2)}, u32[]{:S(2)}) %collective-permute-start.24) | collective-permute-done | bytes 262176 | tf_op jit(solution)/shard_map/ppermute | solution.py:254
  102.3 6.1 %collective-permute-done.12.refs_2_ = bf16[256,512]{1,0:T(8,128)(2,1)S(1)} collective-permute-done((bf16[256,512]{1,0:T(8,128)(2,1)S(1)}, bf16[256,512]{1,0:T(8,128)(2,1)S(1)}, u32[]{:S(2)}, u32[]{:S(2)}) %collective-permute-start.12) | collective-permute-done | bytes 262176 | tf_op jit(solution)/shard_map/ppermute | solution.py:254
  108.5 5.1 %collective-permute-done.13.refs_3_ = bf16[256,512]{1,0:T(8,128)(2,1)S(1)} collective-permute-done((bf16[256,512]{1,0:T(8,128)(2,1)S(1)}, bf16[256,512]{1,0:T(8,128)(2,1)S(1)}, u32[]{:S(2)}, u32[]{:S(2)}) %collective-permute-start.13) | collective-permute-done | bytes 262176 | tf_op jit(solution)/shard_map/ppermute | solution.py:254
  114.0 16.4 %all_to_all.15.mirrored = bf16[16,32,512]{2,1,0:T(8,128)(2,1)S(1)} all-to-all(bf16[16,32,512]{2,1,0:T(8,128)(2,1)S(1)} %bitcast.36), channel_id=1, replica_groups=mesh['row'=4,'col'=16,'layer'=4] {'row','layer'}, dimensions={0} | all-to-all | bytes 1048576 | tf_op jit(solution)/shard_map/all_to_all | solution.py:289
  130.4 24.6 %all_to_all.16.own = bf16[16,32,512]{2,1,0:T(8,128)(2,1)S(1)} all-to-all(bf16[16,32,512]{2,1,0:T(8,128)(2,1)S(1)} %bitcast.35), channel_id=1, replica_groups=mesh['row'=4,'col'=16,'layer'=4] {'col'}, dimensions={0} | all-to-all | bytes 1048576 | tf_op jit(solution)/shard_map/all_to_all | solution.py:288
  155.0 1.3 shard_map.62
  (48 shorter events, 11.5 us)
Async XLA Ops:
  0.0 1.0 copy-start
  1.0 0.7 copy-start.2
  3.0 1.0 copy-start.1
  6.3 36.1 %all-to-all-start = ((bf16[16,64,256]{2,1,0:T(8,128)(2,1)}), bf16[16,64,256]{2,1,0:T(8,128)(2,1)S(1)}, u32[]{:S(2)}, u32[]{:S(2)}) async-start(bf16[16,64,256]{2,1,0:T(8,128)(2,1)} %shard_map.56), calls=%async_computation | async-start | bytes 1048576 | tf_op jit(solution)/shard_map/all_to_all | solution.py:262
  16.3 19.3 %collective-permute-start.18 = (bf16[1024,128]{1,0:T(8,128)(2,1)S(1)}, bf16[1024,128]{1,0:T(8,128)(2,1)S(1)}, u32[]{:S(2)}, u32[]{:S(2)}) collective-permute-start(bf16[1024,128]{1,0:T(8,128)(2,1)S(1)} %get-tuple-element.30.refs_0_), channel_id=1, source_target_pairs={{0,56},{4,60},{8,0},{12,4},{16,8},{20,12},{24,16},{28,20},{32,24},... | collective-permute-start | bytes 786440 | tf_op jit(solution)/shard_map/ppermute | solution.py:250
  18.9 24.8 %collective-permute-start = (bf16[1040,128]{1,0:T(8,128)(2,1)S(1)}, bf16[1040,128]{1,0:T(8,128)(2,1)S(1)}, u32[]{:S(2)}, u32[]{:S(2)}) collective-permute-start(bf16[1040,128]{1,0:T(8,128)(2,1)S(1)} %get-tuple-element.23.refs_0_), channel_id=1, source_target_pairs={{0,8},{4,12},{8,16},{12,20},{16,24},{20,28},{24,32},{28,36},{32,40... | collective-permute-start | bytes 798728 | tf_op jit(solution)/shard_map/ppermute | solution.py:250
  18.9 23.5 %collective-permute-start.15 = (bf16[1024,128]{1,0:T(8,128)(2,1)S(1)}, bf16[1024,128]{1,0:T(8,128)(2,1)S(1)}, u32[]{:S(2)}, u32[]{:S(2)}) collective-permute-start(bf16[1024,128]{1,0:T(8,128)(2,1)S(1)} %get-tuple-element.30.refs_0_), channel_id=1, source_target_pairs={{0,8},{4,12},{8,16},{12,20},{16,24},{20,28},{24,32},{28,36},{32,40... | collective-permute-start | bytes 786440 | tf_op jit(solution)/shard_map/ppermute | solution.py:250
  19.2 26.1 %collective-permute-start.4 = (bf16[1040,128]{1,0:T(8,128)(2,1)S(1)}, bf16[1040,128]{1,0:T(8,128)(2,1)S(1)}, u32[]{:S(2)}, u32[]{:S(2)}) collective-permute-start(bf16[1040,128]{1,0:T(8,128)(2,1)S(1)} %get-tuple-element.23.refs_0_), channel_id=1, source_target_pairs={{0,56},{4,60},{8,0},{12,4},{16,8},{20,12},{24,16},{28,20},{32,24},... | collective-permute-start | bytes 798728 | tf_op jit(solution)/shard_map/ppermute | solution.py:250
  35.6 11.3 %collective-permute-start.19 = (bf16[1024,128]{1,0:T(8,128)(2,1)S(1)}, bf16[1024,128]{1,0:T(8,128)(2,1)S(1)}, u32[]{:S(2)}, u32[]{:S(2)}) collective-permute-start(bf16[1024,128]{1,0:T(8,128)(2,1)S(1)} %collective-permute-done.18.refs_7_), channel_id=1, source_target_pairs={{0,56},{4,60},{8,0},{12,4},{16,8},{20,12},{24,16},{28,20},{32,24},... | collective-permute-start | bytes 786440 | tf_op jit(solution)/shard_map/ppermute | solution.py:250
  42.4 8.2 %collective-permute-start.16 = (bf16[1024,128]{1,0:T(8,128)(2,1)S(1)}, bf16[1024,128]{1,0:T(8,128)(2,1)S(1)}, u32[]{:S(2)}, u32[]{:S(2)}) collective-permute-start(bf16[1024,128]{1,0:T(8,128)(2,1)S(1)} %collective-permute-done.15.refs_1_), channel_id=1, source_target_pairs={{0,8},{4,12},{8,16},{12,20},{16,24},{20,28},{24,32},{28,36},{32,40... | collective-permute-start | bytes 786440 | tf_op jit(solution)/shard_map/ppermute | solution.py:250
  42.4 13.9 %collective-permute-start.7 = (bf16[16,64,256]{2,1,0:T(8,128)(2,1)S(1)}, bf16[16,64,256]{2,1,0:T(8,128)(2,1)S(1)}, u32[]{:S(2)}, u32[]{:S(2)}) collective-permute-start(bf16[16,64,256]{2,1,0:T(8,128)(2,1)S(1)} %all-to-all-done), channel_id=1, source_target_pairs={{0,64},{64,128},{128,192},{192,0},{1,65},{65,129},{129,193},{193,1... | collective-permute-start | bytes 1572872 | tf_op jit(solution)/shard_map/ppermute | solution.py:254
  43.7 15.3 %collective-permute-start.8 = (bf16[16,64,256]{2,1,0:T(8,128)(2,1)S(1)}, bf16[16,64,256]{2,1,0:T(8,128)(2,1)S(1)}, u32[]{:S(2)}, u32[]{:S(2)}) collective-permute-start(bf16[16,64,256]{2,1,0:T(8,128)(2,1)S(1)} %all-to-all-done), channel_id=1, source_target_pairs={{0,192},{64,0},{128,64},{192,128},{1,193},{65,1},{129,65},{193,129... | collective-permute-start | bytes 1572872 | tf_op jit(solution)/shard_map/ppermute | solution.py:254
  45.3 11.0 %collective-permute-start.1 = (bf16[1040,128]{1,0:T(8,128)(2,1)S(1)}, bf16[1040,128]{1,0:T(8,128)(2,1)S(1)}, u32[]{:S(2)}, u32[]{:S(2)}) collective-permute-start(bf16[1040,128]{1,0:T(8,128)(2,1)S(1)} %collective-permute-done.refs_1_), channel_id=1, source_target_pairs={{0,8},{4,12},{8,16},{12,20},{16,24},{20,28},{24,32},{28,36},{32,40... | collective-permute-start | bytes 798728 | tf_op jit(solution)/shard_map/ppermute | solution.py:250
  46.9 9.4 %collective-permute-start.20 = (bf16[1024,128]{1,0:T(8,128)(2,1)S(1)}, bf16[1024,128]{1,0:T(8,128)(2,1)S(1)}, u32[]{:S(2)}, u32[]{:S(2)}) collective-permute-start(bf16[1024,128]{1,0:T(8,128)(2,1)S(1)} %collective-permute-done.19.refs_6_), channel_id=1, source_target_pairs={{0,56},{4,60},{8,0},{12,4},{16,8},{20,12},{24,16},{28,20},{32,24},... | collective-permute-start | bytes 786440 | tf_op jit(solution)/shard_map/ppermute | solution.py:250
  50.6 9.9 %collective-permute-start.5 = (bf16[1040,128]{1,0:T(8,128)(2,1)S(1)}, bf16[1040,128]{1,0:T(8,128)(2,1)S(1)}, u32[]{:S(2)}, u32[]{:S(2)}) collective-permute-start(bf16[1040,128]{1,0:T(8,128)(2,1)S(1)} %collective-permute-done.4.refs_7_), channel_id=1, source_target_pairs={{0,56},{4,60},{8,0},{12,4},{16,8},{20,12},{24,16},{28,20},{32,24},... | collective-permute-start | bytes 798728 | tf_op jit(solution)/shard_map/ppermute | solution.py:250
  56.3 12.9 %collective-permute-start.2 = (bf16[1040,128]{1,0:T(8,128)(2,1)S(1)}, bf16[1040,128]{1,0:T(8,128)(2,1)S(1)}, u32[]{:S(2)}, u32[]{:S(2)}) collective-permute-start(bf16[1040,128]{1,0:T(8,128)(2,1)S(1)} %collective-permute-done.1.refs_2_), channel_id=1, source_target_pairs={{0,8},{4,12},{8,16},{12,20},{16,24},{20,28},{24,32},{28,36},{32,40... | collective-permute-start | bytes 798728 | tf_op jit(solution)/shard_map/ppermute | solution.py:250
  56.3 12.9 %collective-permute-start.17 = (bf16[1024,128]{1,0:T(8,128)(2,1)S(1)}, bf16[1024,128]{1,0:T(8,128)(2,1)S(1)}, u32[]{:S(2)}, u32[]{:S(2)}) collective-permute-start(bf16[1024,128]{1,0:T(8,128)(2,1)S(1)} %collective-permute-done.16.refs_2_), channel_id=1, source_target_pairs={{0,8},{4,12},{8,16},{12,20},{16,24},{20,28},{24,32},{28,36},{32,40... | collective-permute-start | bytes 786440 | tf_op jit(solution)/shard_map/ppermute | solution.py:250
  56.3 14.4 %collective-permute-start.21 = (bf16[1024,128]{1,0:T(8,128)(2,1)S(1)}, bf16[1024,128]{1,0:T(8,128)(2,1)S(1)}, u32[]{:S(2)}, u32[]{:S(2)}) collective-permute-start(bf16[1024,128]{1,0:T(8,128)(2,1)S(1)} %collective-permute-done.20.refs_5_), channel_id=1, source_target_pairs={{0,56},{4,60},{8,0},{12,4},{16,8},{20,12},{24,16},{28,20},{32,24},... | collective-permute-start | bytes 786440 | tf_op jit(solution)/shard_map/ppermute | solution.py:250
  59.1 11.6 %collective-permute-start.9 = (bf16[8,64,256]{2,1,0:T(8,128)(2,1)S(1)}, bf16[8,64,256]{2,1,0:T(8,128)(2,1)S(1)}, u32[]{:S(2)}, u32[]{:S(2)}) collective-permute-start(bf16[8,64,256]{2,1,0:T(8,128)(2,1)S(1)} %slice.8), channel_id=1, source_target_pairs={{0,64},{64,128},{128,192},{192,0},{1,65},{65,129},{129,193},{193,1... | collective-permute-start | bytes 786440 | tf_op jit(solution)/shard_map/ppermute | solution.py:254
  60.5 10.2 %collective-permute-start.10 = (bf16[8,64,256]{2,1,0:T(8,128)(2,1)S(1)}, bf16[8,64,256]{2,1,0:T(8,128)(2,1)S(1)}, u32[]{:S(2)}, u32[]{:S(2)}) collective-permute-start(bf16[8,64,256]{2,1,0:T(8,128)(2,1)S(1)} %slice.9), channel_id=1, source_target_pairs={{0,192},{64,0},{128,64},{192,128},{1,193},{65,1},{129,65},{193,129... | collective-permute-start | bytes 786440 | tf_op jit(solution)/shard_map/ppermute | solution.py:254
  69.2 7.1 %collective-permute-start.6 = (bf16[1040,128]{1,0:T(8,128)(2,1)S(1)}, bf16[1040,128]{1,0:T(8,128)(2,1)S(1)}, u32[]{:S(2)}, u32[]{:S(2)}) collective-permute-start(bf16[1040,128]{1,0:T(8,128)(2,1)S(1)} %collective-permute-done.5.refs_6_), channel_id=1, source_target_pairs={{0,56},{4,60},{8,0},{12,4},{16,8},{20,12},{24,16},{28,20},{32,24},... | collective-permute-start | bytes 798728 | tf_op jit(solution)/shard_map/ppermute | solution.py:250
  69.2 7.1 %collective-permute-start.3 = (bf16[1040,128]{1,0:T(8,128)(2,1)S(1)}, bf16[1040,128]{1,0:T(8,128)(2,1)S(1)}, u32[]{:S(2)}, u32[]{:S(2)}) collective-permute-start(bf16[1040,128]{1,0:T(8,128)(2,1)S(1)} %collective-permute-done.2.refs_3_), channel_id=1, source_target_pairs={{0,8},{4,12},{8,16},{12,20},{16,24},{20,28},{24,32},{28,36},{32,40... | collective-permute-start | bytes 798728 | tf_op jit(solution)/shard_map/ppermute | solution.py:250
  73.0 9.0 %collective-permute-start.22 = (bf16[1024,512]{1,0:T(8,128)(2,1)S(1)}, bf16[1024,512]{1,0:T(8,128)(2,1)S(1)}, u32[]{:S(2)}, u32[]{:S(2)}) collective-permute-start(bf16[1024,512]{1,0:T(8,128)(2,1)S(1)} %shard_map.59), channel_id=1, source_target_pairs={{0,4},{4,0},{8,12},{12,8},{16,20},{20,16},{24,28},{28,24},{32,36},... | collective-permute-start | bytes 3145736 | tf_op jit(solution)/shard_map/ppermute | solution.py:281
  78.6 12.8 %collective-permute-start.11 = (bf16[1040,512]{1,0:T(8,128)(2,1)S(1)}, bf16[1040,512]{1,0:T(8,128)(2,1)S(1)}, u32[]{:S(2)}, u32[]{:S(2)}) collective-permute-start(bf16[1040,512]{1,0:T(8,128)(2,1)S(1)} %shard_map.57), channel_id=1, source_target_pairs={{0,4},{4,0},{8,12},{12,8},{16,20},{20,16},{24,28},{28,24},{32,36},... | collective-permute-start | bytes 3194888 | tf_op jit(solution)/shard_map/ppermute | solution.py:281
  81.9 1.0 copy-start.6
  86.5 10.8 %collective-permute-start.23 = (bf16[256,512]{1,0:T(8,128)(2,1)S(1)}, bf16[256,512]{1,0:T(8,128)(2,1)S(1)}, u32[]{:S(2)}, u32[]{:S(2)}) collective-permute-start(bf16[256,512]{1,0:T(8,128)(2,1)S(1)} %get-tuple-element.32), channel_id=1, source_target_pairs={{0,1},{1,2},{2,3},{3,0},{4,5},{5,6},{6,7},{7,4},{8,9},{9,10},{10,1... | collective-permute-start | bytes 786440 | tf_op jit(solution)/shard_map/ppermute | solution.py:254
  87.8 14.6 %collective-permute-start.24 = (bf16[256,512]{1,0:T(8,128)(2,1)S(1)}, bf16[256,512]{1,0:T(8,128)(2,1)S(1)}, u32[]{:S(2)}, u32[]{:S(2)}) collective-permute-start(bf16[256,512]{1,0:T(8,128)(2,1)S(1)} %get-tuple-element.33), channel_id=1, source_target_pairs={{0,2},{1,3},{2,0},{3,1},{4,6},{5,7},{6,4},{7,5},{8,10},{9,11},{10,... | collective-permute-start | bytes 786440 | tf_op jit(solution)/shard_map/ppermute | solution.py:254
  90.2 12.1 %collective-permute-start.25 = (bf16[256,512]{1,0:T(8,128)(2,1)S(1)}, bf16[256,512]{1,0:T(8,128)(2,1)S(1)}, u32[]{:S(2)}, u32[]{:S(2)}) collective-permute-start(bf16[256,512]{1,0:T(8,128)(2,1)S(1)} %get-tuple-element.34), channel_id=1, source_target_pairs={{0,3},{1,0},{2,1},{3,2},{4,7},{5,4},{6,5},{7,6},{8,11},{9,8},{10,9... | collective-permute-start | bytes 786440 | tf_op jit(solution)/shard_map/ppermute | solution.py:254
  91.4 1.0 copy-start.5
  96.0 12.4 %collective-permute-start.12 = (bf16[256,512]{1,0:T(8,128)(2,1)S(1)}, bf16[256,512]{1,0:T(8,128)(2,1)S(1)}, u32[]{:S(2)}, u32[]{:S(2)}) collective-permute-start(bf16[256,512]{1,0:T(8,128)(2,1)S(1)} %get-tuple-element.27), channel_id=1, source_target_pairs={{0,1},{1,2},{2,3},{3,0},{4,5},{5,6},{6,7},{7,4},{8,9},{9,10},{10,1... | collective-permute-start | bytes 786440 | tf_op jit(solution)/shard_map/ppermute | solution.py:254
  96.4 17.1 %collective-permute-start.13 = (bf16[256,512]{1,0:T(8,128)(2,1)S(1)}, bf16[256,512]{1,0:T(8,128)(2,1)S(1)}, u32[]{:S(2)}, u32[]{:S(2)}) collective-permute-start(bf16[256,512]{1,0:T(8,128)(2,1)S(1)} %get-tuple-element.28), channel_id=1, source_target_pairs={{0,2},{1,3},{2,0},{3,1},{4,6},{5,7},{6,4},{7,5},{8,10},{9,11},{10,... | collective-permute-start | bytes 786440 | tf_op jit(solution)/shard_map/ppermute | solution.py:254
  97.3 16.3 %collective-permute-start.14 = (bf16[256,512]{1,0:T(8,128)(2,1)S(1)}, bf16[256,512]{1,0:T(8,128)(2,1)S(1)}, u32[]{:S(2)}, u32[]{:S(2)}) collective-permute-start(bf16[256,512]{1,0:T(8,128)(2,1)S(1)} %get-tuple-element.29), channel_id=1, source_target_pairs={{0,3},{1,0},{2,1},{3,2},{4,7},{5,4},{6,5},{7,6},{8,11},{9,8},{10,9... | collective-permute-start | bytes 786440 | tf_op jit(solution)/shard_map/ppermute | solution.py:254
  (2 other events, 1.3 us)
where the time goes:
time: 157 us; the launch traced here: 156 us
  waiting for transfers between devices  50.1 us (32%)
  starting transfers between devices  43.4 us (28%)
  blocking collectives  41.1 us (26%)
  Pallas kernels  15.6 us (10%)
  local copies, waits for them, and re-layouts  6.08 us (4%)
    ppermute x14, waiting for transfers between devices, turn_z(): return lax.ppermute(value, 'col', pairs)  35.4 us
    all_to_all x1, blocking collectives, per_device(): own = lax.all_to_all(product.reshape(16, 32, 512), 'col', 0, 0)  24.6 us
    all_to_all x1, blocking collectives, per_device(): lax.all_to_all(flipped.reshape(16, 32, 512), ('row', 'layer'), 0, 0)  16.4 us
    ppermute x10, waiting for transfers between devices, turn(): return lax.ppermute(value, axis, [(i, (i + shift) % 4) for i in range(4)])  14.7 us
    ppermute x10, starting transfers between devices, turn(): return lax.ppermute(value, axis, [(i, (i + shift) % 4) for i in range(4)])  13.7 us
    ppermute x14, starting transfers between devices, turn_z(): return lax.ppermute(value, 'col', pairs)  13 us
    all_to_all x1, starting transfers between devices, per_device(): b_own = lax.all_to_all(b_send, 'col', 0, 0)  9.98 us
    pallas_call x2, Pallas kernels, keep_half(): pl.pallas_call(lambda *refs: keep_kernel(q, *refs), out_shape=shapes, in_...  7.23 us
  transfers between devices with their start and end apart: 27, of which 9 were waited for; matrix products, arithmetic and copies ran while one was open for 0% of the time, Pallas kernels for 8%

commit v1 on v0

--- a/solution.py
+++ b/solution.py
@@ -16,7 +16,7 @@
 ANYWHERE = pl.BlockSpec(memory_space=pl.ANY)
 
 
-def params(mib=48):
+def params(mib=16):
     return pltpu.CompilerParams(vmem_limit_bytes=mib * 1024 * 1024)
 
 
@@ -83,16 +83,18 @@
     )(mask, b)
 
 
-def load_and_multiply(q, half, pieces, bs, a_full, b_full, sems, tails):
-    y, z, core, _ = position()
-    copies = []
-    bands = (slice(0, 16), slice(0, 16), slice(0, 16), slice(0, 8), slice(8, 16))
+def load(q, half, pieces, bs, a_full, b_full, sems, b_sems, tails, more=()):
+    y, z, _, x = position()
+    copies = list(more)
+    bands = (slice(0, 4), slice(0, 4), slice(0, 4), slice(0, 2), slice(2, 4))
     for s, back in enumerate((0, 1, 3, 2, 2)):
-        y0 = lax.rem(y - back + 4, 4)
-        copies.append(pltpu.make_async_copy(bs[s].at[:, half], b_full.at[y0, bands[s]], sems.at[8 + s]))
+        lanes = pl.ds(pl.multiple_of(lax.rem(y - back + 4, 4) * 256, 256), 256)
+        for ahead in range(4):
+            layer = lax.rem(x + ahead, 4)
+            to = b_full.at[ahead, bands[s], :, lanes]
+            copies.append(pltpu.make_async_copy(bs[s].at[:, layer, half], to, b_sems.at[4 * s + ahead]))
     for s in range(8):
-        z0 = lax.rem(z - s + 8, 8)
-        lanes = pl.ds(pl.multiple_of(z0 * 128, 128), 128)
+        lanes = pl.ds(pl.multiple_of(lax.rem(z - s + 8, 8) * 128, 128), 128)
         copies.append(pltpu.make_async_copy(pieces[s].at[0:MQ], a_full.at[:, lanes], sems.at[s]))
     if q == 0:
         for s in range(8):
@@ -101,49 +103,51 @@
         copy.start()
     for copy in copies:
         copy.wait()
-    total = None
-    for y0 in range(4):
-        term = lax.dot_general(
-            a_full[:, y0 * 256 : (y0 + 1) * 256],
-            b_full[y0].reshape(512, 256),
-            (((1,), (1,)), ((), ())),
-            preferred_element_type=F32,
-        )
-        total = term if total is None else total + term
-    return total
+
+
+def multiply(a_full, b_full, rows):
+    return lax.dot_general(
+        a_full[rows, :],
+        b_full[...].reshape(512, 1024),
+        (((1,), (1,)), ((), ())),
+        preferred_element_type=F32,
+    )
 
 
 def mask_rows(tails):
-    _, z, core, _ = position()
+    _, z, core, x = position()
     row = lax.broadcasted_iota(jnp.int32, (TAIL, 128), 0)
     lane = lax.broadcasted_iota(jnp.int32, (TAIL, 128), 1)
-    wide = lax.broadcasted_iota(jnp.int32, (TAIL, 512), 1) // 32
-    mask = jnp.zeros((TAIL, 512), F32)
+    mask = jnp.zeros((TAIL, 128), F32)
     for s in range(8):
-        z0 = lax.rem(z - s + 8, 8)
+        band = 2 * lax.rem(z - s + 8, 8) + core
         values = tails[s].astype(F32)
         chosen = jnp.sum(jnp.where(row == z // 2, values, 0.0), axis=0, keepdims=True)
         column = jnp.sum(jnp.where(row == lane, chosen, 0.0), axis=1, keepdims=True)
-        mask = jnp.where(wide == 2 * z0 + core, column, mask)
+        mask = jnp.where(lane // 32 * 4 + x == band, column, mask)
     return mask
 
 
 def send_kernel(q, *refs):
     pieces, bs, out = refs[:8], refs[8:13], refs[13]
-    a_full, b_full, tails, sems = refs[14:]
+    a_full, b_full, tails, sems, b_sems = refs[14:]
     core = position()[2]
-    total = load_and_multiply(q, 1 - core, pieces, bs, a_full, b_full, sems, tails)
-    out[0:MQ, :] = total.astype(BF)
-    if q == 0:
-        out[MQ : MQ + TAIL, :] = mask_rows(tails).astype(BF)
+    load(q, 1 - core, pieces, bs, a_full, b_full, sems, b_sems, tails)
+    for part in range(4):
+        rows = slice(part * (MQ // 4), (part + 1) * (MQ // 4))
+        out[rows, :] = multiply(a_full, b_full, rows).astype(BF)
+    if q == 0:
+        out[MQ : MQ + TAIL, :] = jnp.zeros((TAIL, 512), BF)
+        out[MQ : MQ + TAIL, 0:128] = mask_rows(tails).astype(BF)
 
 
 def scratches():
     return [
         VMEM((MQ, 1024), BF),
-        VMEM((4, 16, 32, 256), BF),
+        VMEM((4, 4, 32, 1024), BF),
         VMEM((8, TAIL, 128), BF),
-        pltpu.SemaphoreType.DMA((21,)),
+        pltpu.SemaphoreType.DMA((22,)),
+        pltpu.SemaphoreType.DMA((20,)),
     ]
 
 
@@ -165,84 +169,99 @@
     rest = refs[18:]
     if q == 0:
         mask, rest = rest[0], rest[1:]
-    a_full, b_full, tails, sems, total = rest
-    _, _, core, x = position()
-    part = load_and_multiply(q, core, pieces, bs, a_full, b_full, sems, tails)
-    total[...] = (part + received[0:MQ, :].astype(F32)).reshape(4, MQ // 4, 512)
-    own[...] = total[x]
-    for s in range(1, 4):
-        outs[s - 1][...] = total[lax.rem(x + s, 4)].astype(BF)
-    if q == 0:
-        mask[...] = mask_rows(tails) + received[MQ : MQ + TAIL, :].astype(F32)
+    a_full, b_full, tails, sems, b_sems, other = rest
+    core = position()[2]
+    arrival = pltpu.make_async_copy(received, other, sems.at[21])
+    load(q, core, pieces, bs, a_full, b_full, sems, b_sems, tails, [arrival])
+    for part in range(4):
+        rows = slice(part * (MQ // 4), (part + 1) * (MQ // 4))
+        value = multiply(a_full, b_full, rows) + other[rows, :].astype(F32)
+        own[rows, :] = value[:, 0:128]
+        for s in range(1, 4):
+            outs[s - 1][rows, :] = value[:, s * 128 : (s + 1) * 128].astype(BF)
+    if q == 0:
+        mask[...] = mask_rows(tails) + other[MQ : MQ + TAIL, 0:128].astype(F32)
 
 
 def keep_half(q, pieces, bs, received):
-    part = (MQ // 4, 512)
+    part = (MQ, 128)
     shapes = [jax.ShapeDtypeStruct(part, F32)] + [jax.ShapeDtypeStruct(part, BF)] * 3
     if q == 0:
-        shapes.append(jax.ShapeDtypeStruct((TAIL, 512), F32))
+        shapes.append(jax.ShapeDtypeStruct((TAIL, 128), F32))
     return pl.pallas_call(
         lambda *refs: keep_kernel(q, *refs),
         out_shape=shapes,
-        in_specs=[ANYWHERE] * 13 + [WHOLE],
+        in_specs=[ANYWHERE] * 14,
         out_specs=[WHOLE] * len(shapes),
-        scratch_shapes=scratches() + [VMEM((4, MQ // 4, 512), F32)],
+        scratch_shapes=scratches() + [VMEM((rows_of(q), 512), BF)],
         compiler_params=params(),
         cost_estimate=cost(2 * MQ * 1024 * 512, MQ * 1024 * 2 + 2 * 1024 * 1024),
     )(*pieces, *bs, received)
 
 
 def sum_kernel(*refs):
-    mask, parts, out, flipped = refs[0], refs[1:-2], refs[-2], refs[-1]
-    x = position()[3]
-    for q in range(NQ):
-        own, first, second, third = parts[4 * q : 4 * q + 4]
-        for j in range(4 // NQ):
-            block = q * (4 // NQ) + j
-            rows = slice(j * 128, (j + 1) * 128)
-            value = own[rows, :] + first[rows, :].astype(F32) + second[rows, :].astype(F32) + third[rows, :].astype(F32)
-            value = value * mask[pl.ds(x * 4 + block, 1), :]
-            out[block * 128 : (block + 1) * 128, :] = value.astype(BF)
-            flipped[:, block * 128 : (block + 1) * 128] = value.T.astype(BF)
+    mask, parts, out, flips, turned = refs[0], refs[1:-6], refs[-6], refs[-5:-1], refs[-1]
+    y = position()[0]
+    size = MQ // 4
+    for xb in range(4):
+        for q in range(NQ):
+            own, first, second, third = parts[4 * q : 4 * q + 4]
+            for j in range(4 // NQ):
+                at = xb * size + j * 128
+                rows = slice(at, at + 128)
+                value = own[rows, :] + first[rows, :].astype(F32)
+                value = value + second[rows, :].astype(F32) + third[rows, :].astype(F32)
+                block = q * (4 // NQ) + j
+                value = value * mask[xb * 4 + block : xb * 4 + block + 1, :]
+                out[4 * block : 4 * block + 4, xb] = value.astype(BF).reshape(4, 32, 128)
+                lanes = slice((xb * 4 + block) * 128, (xb * 4 + block + 1) * 128)
+                turned[:, :, lanes] = value.T.astype(BF).reshape(4, 32, 128)
+    for s in range(4):
+        flips[s][...] = turned[lax.rem(y + s, 4)]
 
 
 def sum_parts(mask, parts):
     return pl.pallas_call(
         sum_kernel,
-        out_shape=[jax.ShapeDtypeStruct((512, 512), BF)] * 2,
+        out_shape=[jax.ShapeDtypeStruct((16, 4, 32, 128), BF)] + [jax.ShapeDtypeStruct((32, 2048), BF)] * 4,
         in_specs=[WHOLE] * (1 + len(parts)),
-        out_specs=[WHOLE] * 2,
+        out_specs=[WHOLE] * 5,
+        scratch_shapes=[VMEM((4, 32, 2048), BF)],
         compiler_params=params(),
         cost_estimate=cost(512 * 512 * 5, 512 * 512 * 14),
     )(mask, *parts)
 
 
-def final_kernel(own, mirrored, out):
+def final_kernel(own, *refs):
+    mirrored, out, ordered = refs[:4], refs[4], refs[5]
+    y = position()[0]
+    for s in range(4):
+        ordered[lax.rem(y - s + 4, 4)] = mirrored[s][...]
     group = lax.broadcasted_iota(jnp.int32, (32, 128), 1) // 32
     for k_high in range(4):
-        for b_high in range(4):
-            sources = [own[4 * k_high + k, :, b_high * 128 : (b_high + 1) * 128].astype(F32) for k in range(4)]
-            for b in range(4):
+        for layer in range(4):
+            sources = [own[(4 * k_high + k) * 4 + layer].astype(F32) for k in range(4)]
+            at = layer * 512 + k_high * 128
+            for row in range(4):
                 value = None
                 for k in range(4):
-                    shift = ((k - b) % 4) * 32
+                    shift = ((k - row) % 4) * 32
                     turned = pltpu.roll(sources[k], shift, 1) if shift else sources[k]
                     value = turned if value is None else jnp.where(group == k, turned, value)
-                band = b_high * 4 + b
-                value = value + mirrored[band, :, k_high * 128 : (k_high + 1) * 128].astype(F32)
-                at = band * 512 + k_high * 128
-                out[:, at : at + 128] = value.astype(BF)
+                value = value + ordered[row, :, at : at + 128].astype(F32)
+                out[:, row * 2048 + at : row * 2048 + at + 128] = value.astype(BF)
 
 
 def finish(own, mirrored):
     return pl.pallas_call(
         final_kernel,
         out_shape=jax.ShapeDtypeStruct((32, 8192), BF),
-        in_specs=[WHOLE] * 2,
+        in_specs=[WHOLE] * 5,
         out_specs=WHOLE,
+        scratch_shapes=[VMEM((4, 32, 2048), BF)],
         compiler_params=params(),
         cost_estimate=cost(32 * 8192 * 8, 3 * 32 * 8192 * 2),
-    )(own, mirrored)
+    )(own, *mirrored)
 
 
 def turn_z(value, shift):
@@ -260,18 +279,21 @@
     b_send = prep_b(response.reshape(512, 512), response_mask.reshape(4, 4))
 
     b_own = lax.all_to_all(b_send, "col", 0, 0)
-    behind, ahead = turn(b_own, "row", 1), turn(b_own, "row", -1)
-    bs = [b_own, behind, ahead, turn(behind[:8], "row", 1), turn(ahead[8:], "row", -1)]
-    bs = [value.reshape(-1, 2, 32, 256) for value in bs]
 
     gathered = [{0: chunk} for chunk in chunks]
     for step in range(1, 5):
+        if step == 2:
+            gathered[1][1], gathered[1][7], b_own = lax.optimization_barrier((gathered[1][1], gathered[1][7], b_own))
         for q in range(NQ):
             got = gathered[q]
             if step < 4 or q % 2 == 0:
                 got[step] = turn_z(got[step - 1], 1)
             if step < 4 or q % 2 == 1:
                 got[8 - step] = turn_z(got[(9 - step) % 8], -1)
+
+    behind, ahead = turn(b_own, "row", 1), turn(b_own, "row", -1)
+    bs = [b_own, behind, ahead, turn(behind[:8], "row", 1), turn(ahead[8:], "row", -1)]
+    bs = [value.reshape(-1, 4, 2, 32, 256) for value in bs]
 
     parts = []
     mask = None
@@ -284,9 +306,9 @@
             mask = kept[4]
         parts += [kept[0]] + [turn(kept[s], "layer", s) for s in (1, 2, 3)]
 
-    product, flipped = sum_parts(mask, parts)
-    own = lax.all_to_all(product.reshape(16, 32, 512), "col", 0, 0)
-    mirrored = lax.all_to_all(flipped.reshape(16, 32, 512), ("row", "layer"), 0, 0)
+    product, *flips = sum_parts(mask, parts)
+    own = lax.all_to_all(product.reshape(64, 32, 128), ("col", "layer"), 0, 0)
+    mirrored = [flips[0]] + [turn(flips[s], "row", s) for s in (1, 2, 3)]
     return finish(own, mirrored).reshape(1, 1, 32, 8192)
 
 

time: 157 us -> 141 us (0.90)
  blocking collectives: 41.1 us -> 0 us
  starting transfers between devices: 43.4 us -> 62.4 us
  waiting for transfers between devices: 50.1 us -> 59.2 us
  local copies, waits for them, and re-layouts: 6.08 us -> 4.13 us
    all_to_all x2 -> x0, blocking collectives: 41.1 us -> none  [the longest x1 24.6 us: per_device(): own = lax.all_to_all(product.reshape(16, 32, 512), 'col', 0, 0)]
    all_to_all x0 -> x1, starting transfers between devices: none -> 9.62 us  [per_device(): own = lax.all_to_all(product.reshape(64, 32, 128), ('col', 'layer'), 0, 0)]
    all_to_all x0 -> x1, waiting for transfers between devices: none -> 7.58 us  [per_device(): own = lax.all_to_all(product.reshape(64, 32, 128), ('col', 'layer'), 0, 0)]
    ppermute x10 -> x13, waiting for transfers between devices: 14.7 us -> 21.8 us  [turn(): return lax.ppermute(value, axis, [(i, (i + shift) % 4) for i in range(4)])]
    ppermute x10 -> x13, starting transfers between devices: 13.7 us -> 19.5 us  [turn(): return lax.ppermute(value, axis, [(i, (i + shift) % 4) for i in range(4)])]
    ppermute x14, waiting for transfers between devices: 35.4 us -> 29.8 us  [turn_z(): return lax.ppermute(value, 'col', pairs)]
    ppermute x14, starting transfers between devices: 13 us -> 16.7 us  [turn_z(): return lax.ppermute(value, 'col', pairs)]
    pallas_call x2, Pallas kernels: 7.23 us -> 5.19 us  [keep_half(): pl.pallas_call(lambda *refs: keep_kernel(q, *refs), out_shape=shapes, in_...]
  transfers between devices with their start and end apart: 27 -> 31, of which waited for: 9 -> 14; matrix products, arithmetic and copies ran while one was open for 0% -> 0% of each run, Pallas kernels for 8% -> 7%
where the time goes in v1:
time: 141 us
  starting transfers between devices  62.4 us (44%)
  waiting for transfers between devices  59.2 us (42%)
  Pallas kernels  14.8 us (10%)
  local copies, waits for them, and re-layouts  4.13 us (3%)
    ppermute x14, waiting for transfers between devices, turn_z(): return lax.ppermute(value, 'col', pairs)  29.8 us
    ppermute x13, waiting for transfers between devices, turn(): return lax.ppermute(value, axis, [(i, (i + shift) % 4) for i in range(4)])  21.8 us
    ppermute x13, starting transfers between devices, turn(): return lax.ppermute(value, axis, [(i, (i + shift) % 4) for i in range(4)])  19.5 us
    ppermute x14, starting transfers between devices, turn_z(): return lax.ppermute(value, 'col', pairs)  16.7 us
    all_to_all x1, starting transfers between devices, per_device(): b_own = lax.all_to_all(b_send, 'col', 0, 0)  9.98 us
    all_to_all x1, starting transfers between devices, per_device(): own = lax.all_to_all(product.reshape(64, 32, 128), ('col', 'layer'), 0, 0)  9.62 us
    all_to_all x1, waiting for transfers between devices, per_device(): own = lax.all_to_all(product.reshape(64, 32, 128), ('col', 'layer'), 0, 0)  7.58 us
    ppermute x2, starting transfers between devices, per_device(): received = lax.ppermute(other, 'col', [(i, i ^ 1) for i in range(16)])  6.68 us
  transfers between devices with their start and end apart: 31, of which 14 were waited for; matrix products, arithmetic and copies ran while one was open for 0% of the time, Pallas kernels for 7%

profile of v1, /device:TPU:1, one launch (start us, length us, event | category | flops | bytes accessed | tf_op | source)
XLA Modules:
  0.0 140.7 jit_solution(12233212088123806730)
XLA Ops:
  4.7 1.6 %shard_map.56 = bf16[16,64,256]{2,1,0:T(8,128)(2,1)} custom-call(s32[4,4]{1,0:T(4,128)S(1)} %bitcast.35, bf16[512,512]{1,0:T(8,128)(2,1)S(1)} %bitcast.33), custom_call_target="tpu_custom_call" | custom-call | flops 262144 | bytes 1048576 | tf_op jit(solution)/shard_map/pallas_call | solution.py:76
  6.3 10.0 %all-to-all-start = ((bf16[16,64,256]{2,1,0:T(8,128)(2,1)}), bf16[16,64,256]{2,1,0:T(8,128)(2,1)S(1)}, u32[]{:S(2)}, u32[]{:S(2)}) async-start(bf16[16,64,256]{2,1,0:T(8,128)(2,1)} %shard_map.56), calls=%async_computation | async-start | bytes 1048576 | tf_op jit(solution)/shard_map/all_to_all | solution.py:281
  16.3 1.4 collective-permute-start.7
  17.7 1.3 collective-permute-start.8
  19.2 2.5 %collective-permute-start.4 = (bf16[1040,128]{1,0:T(8,128)(2,1)S(1)}, bf16[1040,128]{1,0:T(8,128)(2,1)S(1)}, u32[]{:S(2)}, u32[]{:S(2)}) collective-permute-start(bf16[1040,128]{1,0:T(8,128)(2,1)S(1)} %get-tuple-element.29.refs_0_), channel_id=1, source_target_pairs={{0,56},{4,60},{8,0},{12,4},{16,8},{20,12},{24,16},{28,20},{32,24},... | collective-permute-start | bytes 798728 | tf_op jit(solution)/shard_map/ppermute | solution.py:269
  21.7 15.1 %collective-permute-done.7.refs_1_ = bf16[1024,128]{1,0:T(8,128)(2,1)S(1)} collective-permute-done((bf16[1024,128]{1,0:T(8,128)(2,1)S(1)}, bf16[1024,128]{1,0:T(8,128)(2,1)S(1)}, u32[]{:S(2)}, u32[]{:S(2)}) %collective-permute-start.7) | collective-permute-done | bytes 262176 | tf_op jit(solution)/shard_map/ppermute | solution.py:269
  38.0 4.4 %collective-permute-done.refs_1_ = bf16[1040,128]{1,0:T(8,128)(2,1)S(1)} collective-permute-done((bf16[1040,128]{1,0:T(8,128)(2,1)S(1)}, bf16[1040,128]{1,0:T(8,128)(2,1)S(1)}, u32[]{:S(2)}, u32[]{:S(2)}) %collective-permute-start) | collective-permute-done | bytes 266272 | tf_op jit(solution)/shard_map/ppermute | solution.py:269
  42.4 2.7 %collective-permute-start.10 = (bf16[16,64,256]{2,1,0:T(8,128)(2,1)S(1)}, bf16[16,64,256]{2,1,0:T(8,128)(2,1)S(1)}, u32[]{:S(2)}, u32[]{:S(2)}) collective-permute-start(bf16[16,64,256]{2,1,0:T(8,128)(2,1)S(1)} %all-to-all-done), channel_id=1, source_target_pairs={{0,192},{64,0},{128,64},{192,128},{1,193},{65,1},{129,65},{193,129... | collective-permute-start | bytes 1572872 | tf_op jit(solution)/shard_map/ppermute | solution.py:273
  45.2 2.7 %collective-permute-start.19 = (bf16[1024,128]{1,0:T(8,128)(2,1)S(1)}, bf16[1024,128]{1,0:T(8,128)(2,1)S(1)}, u32[]{:S(2)}, u32[]{:S(2)}) collective-permute-start(bf16[1024,128]{1,0:T(8,128)(2,1)S(1)} %collective-permute-done.8.refs_7_), channel_id=1, source_target_pairs={{0,56},{4,60},{8,0},{12,4},{16,8},{20,12},{24,16},{28,20},{32,24},... | collective-permute-start | bytes 786440 | tf_op jit(solution)/shard_map/ppermute | solution.py:269
  47.8 2.8 %collective-permute-done.1.refs_2_ = bf16[1040,128]{1,0:T(8,128)(2,1)S(1)} collective-permute-done((bf16[1040,128]{1,0:T(8,128)(2,1)S(1)}, bf16[1040,128]{1,0:T(8,128)(2,1)S(1)}, u32[]{:S(2)}, u32[]{:S(2)}) %collective-permute-start.1) | collective-permute-done | bytes 266272 | tf_op jit(solution)/shard_map/ppermute | solution.py:269
  50.7 1.3 collective-permute-done.19.refs_6_
  52.0 3.4 %collective-permute-start.20 = (bf16[1024,128]{1,0:T(8,128)(2,1)S(1)}, bf16[1024,128]{1,0:T(8,128)(2,1)S(1)}, u32[]{:S(2)}, u32[]{:S(2)}) collective-permute-start(bf16[1024,128]{1,0:T(8,128)(2,1)S(1)} %collective-permute-done.19.refs_6_), channel_id=1, source_target_pairs={{0,56},{4,60},{8,0},{12,4},{16,8},{20,12},{24,16},{28,20},{32,24},... | collective-permute-start | bytes 786440 | tf_op jit(solution)/shard_map/ppermute | solution.py:269
  56.1 1.6 %collective-permute-start.11 = (bf16[8,64,256]{2,1,0:T(8,128)(2,1)S(1)}, bf16[8,64,256]{2,1,0:T(8,128)(2,1)S(1)}, u32[]{:S(2)}, u32[]{:S(2)}) collective-permute-start(bf16[8,64,256]{2,1,0:T(8,128)(2,1)S(1)} %slice.8), channel_id=1, source_target_pairs={{0,64},{64,128},{128,192},{192,0},{1,65},{65,129},{129,193},{193,1... | collective-permute-start | bytes 786440 | tf_op jit(solution)/shard_map/ppermute | solution.py:273
  57.8 1.5 %collective-permute-start.12 = (bf16[8,64,256]{2,1,0:T(8,128)(2,1)S(1)}, bf16[8,64,256]{2,1,0:T(8,128)(2,1)S(1)}, u32[]{:S(2)}, u32[]{:S(2)}) collective-permute-start(bf16[8,64,256]{2,1,0:T(8,128)(2,1)S(1)} %slice.9), channel_id=1, source_target_pairs={{0,192},{64,0},{128,64},{192,128},{1,193},{65,1},{129,65},{193,129... | collective-permute-start | bytes 786440 | tf_op jit(solution)/shard_map/ppermute | solution.py:273
  59.3 4.0 %collective-permute-done.20.refs_5_ = bf16[1024,128]{1,0:T(8,128)(2,1)S(1)} collective-permute-done((bf16[1024,128]{1,0:T(8,128)(2,1)S(1)}, bf16[1024,128]{1,0:T(8,128)(2,1)S(1)}, u32[]{:S(2)}, u32[]{:S(2)}) %collective-permute-start.20) | collective-permute-done | bytes 262176 | tf_op jit(solution)/shard_map/ppermute | solution.py:269
  63.3 3.4 %collective-permute-start.21 = (bf16[1024,128]{1,0:T(8,128)(2,1)S(1)}, bf16[1024,128]{1,0:T(8,128)(2,1)S(1)}, u32[]{:S(2)}, u32[]{:S(2)}) collective-permute-start(bf16[1024,128]{1,0:T(8,128)(2,1)S(1)} %collective-permute-done.20.refs_5_), channel_id=1, source_target_pairs={{0,56},{4,60},{8,0},{12,4},{16,8},{20,12},{24,16},{28,20},{32,24},... | collective-permute-start | bytes 786440 | tf_op jit(solution)/shard_map/ppermute | solution.py:269
  66.8 1.4 %collective-permute-start.3 = (bf16[1040,128]{1,0:T(8,128)(2,1)S(1)}, bf16[1040,128]{1,0:T(8,128)(2,1)S(1)}, u32[]{:S(2)}, u32[]{:S(2)}) collective-permute-start(bf16[1040,128]{1,0:T(8,128)(2,1)S(1)} %collective-permute-done.2.refs_3_), channel_id=1, source_target_pairs={{0,8},{4,12},{8,16},{12,20},{16,24},{20,28},{24,32},{28,36},{32,40... | collective-permute-start | bytes 798728 | tf_op jit(solution)/shard_map/ppermute | solution.py:269
  68.2 1.8 %collective-permute-done.21.refs_4_ = bf16[1024,128]{1,0:T(8,128)(2,1)S(1)} collective-permute-done((bf16[1024,128]{1,0:T(8,128)(2,1)S(1)}, bf16[1024,128]{1,0:T(8,128)(2,1)S(1)}, u32[]{:S(2)}, u32[]{:S(2)}) %collective-permute-start.21) | collective-permute-done | bytes 262176 | tf_op jit(solution)/shard_map/ppermute | solution.py:269
  70.1 2.5 %shard_map.59 = bf16[1024,512]{1,0:T(8,128)(2,1)S(1)} custom-call(bf16[1024,128]{1,0:T(8,128)(2,1)S(1)} %get-tuple-element.30.refs_0_, bf16[1024,128]{1,0:T(8,128)(2,1)S(1)} %collective-permute-done.7.refs_1_, bf16[1024,128]{1,0:T(8,128)(2,1)S(1)} %collective-permute-done.17.refs_2_, bf16[1024,128]{1,0:T(8,128)(2,1)S(1)} %collective-permute-done.18.refs_3_, ...), custom_call_target="tpu_custom_call" | custom-call | flops 1073741824 | bytes 3145728 | tf_op jit(solution)/shard_map/pallas_call | solution.py:155
  72.5 6.2 %collective-permute-start.22 = (bf16[1024,512]{1,0:T(8,128)(2,1)S(1)}, bf16[1024,512]{1,0:T(8,128)(2,1)S(1)}, u32[]{:S(2)}, u32[]{:S(2)}) collective-permute-start(bf16[1024,512]{1,0:T(8,128)(2,1)S(1)} %shard_map.59), channel_id=1, source_target_pairs={{0,4},{4,0},{8,12},{12,8},{16,20},{20,16},{24,28},{28,24},{32,36},... | collective-permute-start | bytes 3145736 | tf_op jit(solution)/shard_map/ppermute | solution.py:303
  78.7 2.5 %shard_map.57 = bf16[1040,512]{1,0:T(8,128)(2,1)S(1)} custom-call(bf16[1040,128]{1,0:T(8,128)(2,1)S(1)} %get-tuple-element.29.refs_0_, bf16[1040,128]{1,0:T(8,128)(2,1)S(1)} %collective-permute-done.refs_1_, bf16[1040,128]{1,0:T(8,128)(2,1)S(1)} %collective-permute-done.1.refs_2_, bf16[1040,128]{1,0:T(8,128)(2,1)S(1)} %collective-permute-done.2.refs_3_, ...), custom_call_target="tpu_custom_call" | custom-call | flops 1073741824 | bytes 3145728 | tf_op jit(solution)/shard_map/pallas_call | solution.py:155
  81.8 2.5 %shard_map.60 = (f32[1024,128]{1,0:T(8,128)S(1)}, bf16[1024,128]{1,0:T(8,128)(2,1)S(1)}, bf16[1024,128]{1,0:T(8,128)(2,1)S(1)}, bf16[1024,128]{1,0:T(8,128)(2,1)S(1)}) custom-call(bf16[1024,128]{1,0:T(8,128)(2,1)S(1)} %get-tuple-element.30.refs_0_, bf16[1024,128]{1,0:T(8,128)(2,1)S(1)} %collective-permute-done.7.refs_1_, ...), custom_call_target="tpu_custom_call" | custom-call | flops 1073741824 | bytes 4194304 | tf_op jit(solution)/shard_map/pallas_call | solution.py:191
  84.3 1.3 collective-permute-start.23
  85.6 2.5 %collective-permute-start.24 = (bf16[1024,128]{1,0:T(8,128)(2,1)S(1)}, bf16[1024,128]{1,0:T(8,128)(2,1)S(1)}, u32[]{:S(2)}, u32[]{:S(2)}) collective-permute-start(bf16[1024,128]{1,0:T(8,128)(2,1)S(1)} %get-tuple-element.42), channel_id=1, source_target_pairs={{0,2},{1,3},{2,0},{3,1},{4,6},{5,7},{6,4},{7,5},{8,10},{9,11},{10,... | collective-permute-start | bytes 786440 | tf_op jit(solution)/shard_map/ppermute | solution.py:273
  89.2 2.6 %shard_map.58 = (f32[1024,128]{1,0:T(8,128)S(1)}, bf16[1024,128]{1,0:T(8,128)(2,1)S(1)}, bf16[1024,128]{1,0:T(8,128)(2,1)S(1)}, bf16[1024,128]{1,0:T(8,128)(2,1)S(1)}, f32[16,128]{1,0:T(8,128)S(1)}) custom-call(bf16[1040,128]{1,0:T(8,128)(2,1)S(1)} %get-tuple-element.29.refs_0_, bf16[1040,128]{1,0:T(8,128)(2,1)S(1)} %collective-permute-done.refs_1_, ...), custom_call_target="tpu_custom_call" | custom-call | flops 1073741824 | bytes 4194304 | tf_op jit(solution)/shard_map/pallas_call | solution.py:191
  94.8 5.4 %collective-permute-done.24.refs_7_ = bf16[1024,128]{1,0:T(8,128)(2,1)S(1)} collective-permute-done((bf16[1024,128]{1,0:T(8,128)(2,1)S(1)}, bf16[1024,128]{1,0:T(8,128)(2,1)S(1)}, u32[]{:S(2)}, u32[]{:S(2)}) %collective-permute-start.24) | collective-permute-done | bytes 262176 | tf_op jit(solution)/shard_map/ppermute | solution.py:273
  100.1 6.3 %collective-permute-done.14.refs_2_ = bf16[1024,128]{1,0:T(8,128)(2,1)S(1)} collective-permute-done((bf16[1024,128]{1,0:T(8,128)(2,1)S(1)}, bf16[1024,128]{1,0:T(8,128)(2,1)S(1)}, u32[]{:S(2)}, u32[]{:S(2)}) %collective-permute-start.14) | collective-permute-done | bytes 262176 | tf_op jit(solution)/shard_map/ppermute | solution.py:273
  106.4 5.0 %collective-permute-done.15.refs_3_ = bf16[1024,128]{1,0:T(8,128)(2,1)S(1)} collective-permute-done((bf16[1024,128]{1,0:T(8,128)(2,1)S(1)}, bf16[1024,128]{1,0:T(8,128)(2,1)S(1)}, u32[]{:S(2)}, u32[]{:S(2)}) %collective-permute-start.15) | collective-permute-done | bytes 262176 | tf_op jit(solution)/shard_map/ppermute | solution.py:273
  112.5 9.6 %all-to-all-start.1 = ((bf16[64,32,128]{2,1,0:T(8,128)(2,1)}), bf16[64,32,128]{2,1,0:T(8,128)(2,1)S(1)}, u32[]{:S(2)}, u32[]{:S(2)}) async-start(bf16[64,32,128]{2,1,0:T(8,128)(2,1)} %bitcast.10), calls=%async_computation.1 | async-start | bytes 1048576 | tf_op jit(solution)/shard_map/all_to_all | solution.py:310
  123.3 2.6 %collective-permute-start.27 = (bf16[32,2048]{1,0:T(8,128)(2,1)S(1)}, bf16[32,2048]{1,0:T(8,128)(2,1)S(1)}, u32[]{:S(2)}, u32[]{:S(2)}) collective-permute-start(bf16[32,2048]{1,0:T(8,128)(2,1)S(1)} %get-tuple-element.47), channel_id=1, source_target_pairs={{0,128},{64,192},{128,0},{192,64},{1,129},{65,193},{129,1},{193,65... | collective-permute-start | bytes 393224 | tf_op jit(solution)/shard_map/ppermute | solution.py:273
  128.1 3.8 %collective-permute-done.27.refs_2_ = bf16[32,2048]{1,0:T(8,128)(2,1)S(1)} collective-permute-done((bf16[32,2048]{1,0:T(8,128)(2,1)S(1)}, bf16[32,2048]{1,0:T(8,128)(2,1)S(1)}, u32[]{:S(2)}, u32[]{:S(2)}) %collective-permute-start.27) | collective-permute-done | bytes 131104 | tf_op jit(solution)/shard_map/ppermute | solution.py:273
  131.8 7.6 %all-to-all-done.1.own = bf16[64,32,128]{2,1,0:T(8,128)(2,1)S(1)} async-done(((bf16[64,32,128]{2,1,0:T(8,128)(2,1)}), bf16[64,32,128]{2,1,0:T(8,128)(2,1)S(1)}, u32[]{:S(2)}, u32[]{:S(2)}) %all-to-all-start.1) | async-done | bytes 524320 | tf_op jit(solution)/shard_map/all_to_all | solution.py:310
  (50 shorter events, 17.2 us)
Async XLA Ops:
  3.0 1.0 copy-start.1
  6.3 30.4 %all-to-all-start = ((bf16[16,64,256]{2,1,0:T(8,128)(2,1)}), bf16[16,64,256]{2,1,0:T(8,128)(2,1)S(1)}, u32[]{:S(2)}, u32[]{:S(2)}) async-start(bf16[16,64,256]{2,1,0:T(8,128)(2,1)} %shard_map.56), calls=%async_computation | async-start | bytes 1048576 | tf_op jit(solution)/shard_map/all_to_all | solution.py:281
  16.3 20.4 %collective-permute-start.7 = (bf16[1024,128]{1,0:T(8,128)(2,1)S(1)}, bf16[1024,128]{1,0:T(8,128)(2,1)S(1)}, u32[]{:S(2)}, u32[]{:S(2)}) collective-permute-start(bf16[1024,128]{1,0:T(8,128)(2,1)S(1)} %get-tuple-element.30.refs_0_), channel_id=1, source_target_pairs={{0,8},{4,12},{8,16},{12,20},{16,24},{20,28},{24,32},{28,36},{32,40... | collective-permute-start | bytes 786440 | tf_op jit(solution)/shard_map/ppermute | solution.py:269
  17.7 19.0 %collective-permute-start.8 = (bf16[1024,128]{1,0:T(8,128)(2,1)S(1)}, bf16[1024,128]{1,0:T(8,128)(2,1)S(1)}, u32[]{:S(2)}, u32[]{:S(2)}) collective-permute-start(bf16[1024,128]{1,0:T(8,128)(2,1)S(1)} %get-tuple-element.30.refs_0_), channel_id=1, source_target_pairs={{0,56},{4,60},{8,0},{12,4},{16,8},{20,12},{24,16},{28,20},{32,24},... | collective-permute-start | bytes 786440 | tf_op jit(solution)/shard_map/ppermute | solution.py:269
  19.0 23.4 %collective-permute-start = (bf16[1040,128]{1,0:T(8,128)(2,1)S(1)}, bf16[1040,128]{1,0:T(8,128)(2,1)S(1)}, u32[]{:S(2)}, u32[]{:S(2)}) collective-permute-start(bf16[1040,128]{1,0:T(8,128)(2,1)S(1)} %get-tuple-element.29.refs_0_), channel_id=1, source_target_pairs={{0,8},{4,12},{8,16},{12,20},{16,24},{20,28},{24,32},{28,36},{32,40... | collective-permute-start | bytes 798728 | tf_op jit(solution)/shard_map/ppermute | solution.py:269
  19.2 28.7 %collective-permute-start.4 = (bf16[1040,128]{1,0:T(8,128)(2,1)S(1)}, bf16[1040,128]{1,0:T(8,128)(2,1)S(1)}, u32[]{:S(2)}, u32[]{:S(2)}) collective-permute-start(bf16[1040,128]{1,0:T(8,128)(2,1)S(1)} %get-tuple-element.29.refs_0_), channel_id=1, source_target_pairs={{0,56},{4,60},{8,0},{12,4},{16,8},{20,12},{24,16},{28,20},{32,24},... | collective-permute-start | bytes 798728 | tf_op jit(solution)/shard_map/ppermute | solution.py:269
  36.7 19.0 %collective-permute-start.9 = (bf16[16,64,256]{2,1,0:T(8,128)(2,1)S(1)}, bf16[16,64,256]{2,1,0:T(8,128)(2,1)S(1)}, u32[]{:S(2)}, u32[]{:S(2)}) collective-permute-start(bf16[16,64,256]{2,1,0:T(8,128)(2,1)S(1)} %all-to-all-done), channel_id=1, source_target_pairs={{0,64},{64,128},{128,192},{192,0},{1,65},{65,129},{129,193},{193,1... | collective-permute-start | bytes 1572872 | tf_op jit(solution)/shard_map/ppermute | solution.py:273
  42.4 8.2 %collective-permute-start.1 = (bf16[1040,128]{1,0:T(8,128)(2,1)S(1)}, bf16[1040,128]{1,0:T(8,128)(2,1)S(1)}, u32[]{:S(2)}, u32[]{:S(2)}) collective-permute-start(bf16[1040,128]{1,0:T(8,128)(2,1)S(1)} %collective-permute-done.refs_1_), channel_id=1, source_target_pairs={{0,8},{4,12},{8,16},{12,20},{16,24},{20,28},{24,32},{28,36},{32,40... | collective-permute-start | bytes 798728 | tf_op jit(solution)/shard_map/ppermute | solution.py:269
  42.4 13.6 %collective-permute-start.10 = (bf16[16,64,256]{2,1,0:T(8,128)(2,1)S(1)}, bf16[16,64,256]{2,1,0:T(8,128)(2,1)S(1)}, u32[]{:S(2)}, u32[]{:S(2)}) collective-permute-start(bf16[16,64,256]{2,1,0:T(8,128)(2,1)S(1)} %all-to-all-done), channel_id=1, source_target_pairs={{0,192},{64,0},{128,64},{192,128},{1,193},{65,1},{129,65},{193,129... | collective-permute-start | bytes 1572872 | tf_op jit(solution)/shard_map/ppermute | solution.py:273
  45.2 6.8 %collective-permute-start.19 = (bf16[1024,128]{1,0:T(8,128)(2,1)S(1)}, bf16[1024,128]{1,0:T(8,128)(2,1)S(1)}, u32[]{:S(2)}, u32[]{:S(2)}) collective-permute-start(bf16[1024,128]{1,0:T(8,128)(2,1)S(1)} %collective-permute-done.8.refs_7_), channel_id=1, source_target_pairs={{0,56},{4,60},{8,0},{12,4},{16,8},{20,12},{24,16},{28,20},{32,24},... | collective-permute-start | bytes 786440 | tf_op jit(solution)/shard_map/ppermute | solution.py:269
  47.8 7.9 %collective-permute-start.17 = (bf16[1024,128]{1,0:T(8,128)(2,1)S(1)}, bf16[1024,128]{1,0:T(8,128)(2,1)S(1)}, u32[]{:S(2)}, u32[]{:S(2)}) collective-permute-start(bf16[1024,128]{1,0:T(8,128)(2,1)S(1)} %collective-permute-done.7.refs_1_), channel_id=1, source_target_pairs={{0,8},{4,12},{8,16},{12,20},{16,24},{20,28},{24,32},{28,36},{32,40... | collective-permute-start | bytes 786440 | tf_op jit(solution)/shard_map/ppermute | solution.py:269
  50.7 7.1 %collective-permute-start.5 = (bf16[1040,128]{1,0:T(8,128)(2,1)S(1)}, bf16[1040,128]{1,0:T(8,128)(2,1)S(1)}, u32[]{:S(2)}, u32[]{:S(2)}) collective-permute-start(bf16[1040,128]{1,0:T(8,128)(2,1)S(1)} %collective-permute-done.4.refs_7_), channel_id=1, source_target_pairs={{0,56},{4,60},{8,0},{12,4},{16,8},{20,12},{24,16},{28,20},{32,24},... | collective-permute-start | bytes 798728 | tf_op jit(solution)/shard_map/ppermute | solution.py:269
  52.0 11.3 %collective-permute-start.20 = (bf16[1024,128]{1,0:T(8,128)(2,1)S(1)}, bf16[1024,128]{1,0:T(8,128)(2,1)S(1)}, u32[]{:S(2)}, u32[]{:S(2)}) collective-permute-start(bf16[1024,128]{1,0:T(8,128)(2,1)S(1)} %collective-permute-done.19.refs_6_), channel_id=1, source_target_pairs={{0,56},{4,60},{8,0},{12,4},{16,8},{20,12},{24,16},{28,20},{32,24},... | collective-permute-start | bytes 786440 | tf_op jit(solution)/shard_map/ppermute | solution.py:269
  55.7 11.0 %collective-permute-start.2 = (bf16[1040,128]{1,0:T(8,128)(2,1)S(1)}, bf16[1040,128]{1,0:T(8,128)(2,1)S(1)}, u32[]{:S(2)}, u32[]{:S(2)}) collective-permute-start(bf16[1040,128]{1,0:T(8,128)(2,1)S(1)} %collective-permute-done.1.refs_2_), channel_id=1, source_target_pairs={{0,8},{4,12},{8,16},{12,20},{16,24},{20,28},{24,32},{28,36},{32,40... | collective-permute-start | bytes 798728 | tf_op jit(solution)/shard_map/ppermute | solution.py:269
  55.7 11.1 %collective-permute-start.18 = (bf16[1024,128]{1,0:T(8,128)(2,1)S(1)}, bf16[1024,128]{1,0:T(8,128)(2,1)S(1)}, u32[]{:S(2)}, u32[]{:S(2)}) collective-permute-start(bf16[1024,128]{1,0:T(8,128)(2,1)S(1)} %collective-permute-done.17.refs_2_), channel_id=1, source_target_pairs={{0,8},{4,12},{8,16},{12,20},{16,24},{20,28},{24,32},{28,36},{32,40... | collective-permute-start | bytes 786440 | tf_op jit(solution)/shard_map/ppermute | solution.py:269
  56.1 12.1 %collective-permute-start.11 = (bf16[8,64,256]{2,1,0:T(8,128)(2,1)S(1)}, bf16[8,64,256]{2,1,0:T(8,128)(2,1)S(1)}, u32[]{:S(2)}, u32[]{:S(2)}) collective-permute-start(bf16[8,64,256]{2,1,0:T(8,128)(2,1)S(1)} %slice.8), channel_id=1, source_target_pairs={{0,64},{64,128},{128,192},{192,0},{1,65},{65,129},{129,193},{193,1... | collective-permute-start | bytes 786440 | tf_op jit(solution)/shard_map/ppermute | solution.py:273
  57.8 10.5 %collective-permute-start.12 = (bf16[8,64,256]{2,1,0:T(8,128)(2,1)S(1)}, bf16[8,64,256]{2,1,0:T(8,128)(2,1)S(1)}, u32[]{:S(2)}, u32[]{:S(2)}) collective-permute-start(bf16[8,64,256]{2,1,0:T(8,128)(2,1)S(1)} %slice.9), channel_id=1, source_target_pairs={{0,192},{64,0},{128,64},{192,128},{1,193},{65,1},{129,65},{193,129... | collective-permute-start | bytes 786440 | tf_op jit(solution)/shard_map/ppermute | solution.py:273
  63.3 6.7 %collective-permute-start.21 = (bf16[1024,128]{1,0:T(8,128)(2,1)S(1)}, bf16[1024,128]{1,0:T(8,128)(2,1)S(1)}, u32[]{:S(2)}, u32[]{:S(2)}) collective-permute-start(bf16[1024,128]{1,0:T(8,128)(2,1)S(1)} %collective-permute-done.20.refs_5_), channel_id=1, source_target_pairs={{0,56},{4,60},{8,0},{12,4},{16,8},{20,12},{24,16},{28,20},{32,24},... | collective-permute-start | bytes 786440 | tf_op jit(solution)/shard_map/ppermute | solution.py:269
  66.7 12.0 %collective-permute-start.6 = (bf16[1040,128]{1,0:T(8,128)(2,1)S(1)}, bf16[1040,128]{1,0:T(8,128)(2,1)S(1)}, u32[]{:S(2)}, u32[]{:S(2)}) collective-permute-start(bf16[1040,128]{1,0:T(8,128)(2,1)S(1)} %collective-permute-done.5.refs_6_), channel_id=1, source_target_pairs={{0,56},{4,60},{8,0},{12,4},{16,8},{20,12},{24,16},{28,20},{32,24},... | collective-permute-start | bytes 798728 | tf_op jit(solution)/shard_map/ppermute | solution.py:269
  66.8 11.9 %collective-permute-start.3 = (bf16[1040,128]{1,0:T(8,128)(2,1)S(1)}, bf16[1040,128]{1,0:T(8,128)(2,1)S(1)}, u32[]{:S(2)}, u32[]{:S(2)}) collective-permute-start(bf16[1040,128]{1,0:T(8,128)(2,1)S(1)} %collective-permute-done.2.refs_3_), channel_id=1, source_target_pairs={{0,8},{4,12},{8,16},{12,20},{16,24},{20,28},{24,32},{28,36},{32,40... | collective-permute-start | bytes 798728 | tf_op jit(solution)/shard_map/ppermute | solution.py:269
  72.5 9.2 %collective-permute-start.22 = (bf16[1024,512]{1,0:T(8,128)(2,1)S(1)}, bf16[1024,512]{1,0:T(8,128)(2,1)S(1)}, u32[]{:S(2)}, u32[]{:S(2)}) collective-permute-start(bf16[1024,512]{1,0:T(8,128)(2,1)S(1)} %shard_map.59), channel_id=1, source_target_pairs={{0,4},{4,0},{8,12},{12,8},{16,20},{20,16},{24,28},{28,24},{32,36},... | collective-permute-start | bytes 3145736 | tf_op jit(solution)/shard_map/ppermute | solution.py:303
  81.3 8.0 %collective-permute-start.13 = (bf16[1040,512]{1,0:T(8,128)(2,1)S(1)}, bf16[1040,512]{1,0:T(8,128)(2,1)S(1)}, u32[]{:S(2)}, u32[]{:S(2)}) collective-permute-start(bf16[1040,512]{1,0:T(8,128)(2,1)S(1)} %shard_map.57), channel_id=1, source_target_pairs={{0,4},{4,0},{8,12},{12,8},{16,20},{20,16},{24,28},{28,24},{32,36},... | collective-permute-start | bytes 3194888 | tf_op jit(solution)/shard_map/ppermute | solution.py:303
  84.3 9.2 %collective-permute-start.23 = (bf16[1024,128]{1,0:T(8,128)(2,1)S(1)}, bf16[1024,128]{1,0:T(8,128)(2,1)S(1)}, u32[]{:S(2)}, u32[]{:S(2)}) collective-permute-start(bf16[1024,128]{1,0:T(8,128)(2,1)S(1)} %get-tuple-element.41), channel_id=1, source_target_pairs={{0,1},{1,2},{2,3},{3,0},{4,5},{5,6},{6,7},{7,4},{8,9},{9,10},{10,1... | collective-permute-start | bytes 786440 | tf_op jit(solution)/shard_map/ppermute | solution.py:273
  85.6 14.5 %collective-permute-start.24 = (bf16[1024,128]{1,0:T(8,128)(2,1)S(1)}, bf16[1024,128]{1,0:T(8,128)(2,1)S(1)}, u32[]{:S(2)}, u32[]{:S(2)}) collective-permute-start(bf16[1024,128]{1,0:T(8,128)(2,1)S(1)} %get-tuple-element.42), channel_id=1, source_target_pairs={{0,2},{1,3},{2,0},{3,1},{4,6},{5,7},{6,4},{7,5},{8,10},{9,11},{10,... | collective-permute-start | bytes 786440 | tf_op jit(solution)/shard_map/ppermute | solution.py:273
  88.1 12.1 %collective-permute-start.25 = (bf16[1024,128]{1,0:T(8,128)(2,1)S(1)}, bf16[1024,128]{1,0:T(8,128)(2,1)S(1)}, u32[]{:S(2)}, u32[]{:S(2)}) collective-permute-start(bf16[1024,128]{1,0:T(8,128)(2,1)S(1)} %get-tuple-element.43), channel_id=1, source_target_pairs={{0,3},{1,0},{2,1},{3,2},{4,7},{5,4},{6,5},{7,6},{8,11},{9,8},{10,9... | collective-permute-start | bytes 786440 | tf_op jit(solution)/shard_map/ppermute | solution.py:273
  91.9 14.5 %collective-permute-start.14 = (bf16[1024,128]{1,0:T(8,128)(2,1)S(1)}, bf16[1024,128]{1,0:T(8,128)(2,1)S(1)}, u32[]{:S(2)}, u32[]{:S(2)}) collective-permute-start(bf16[1024,128]{1,0:T(8,128)(2,1)S(1)} %get-tuple-element.35), channel_id=1, source_target_pairs={{0,1},{1,2},{2,3},{3,0},{4,5},{5,6},{6,7},{7,4},{8,9},{9,10},{10,1... | collective-permute-start | bytes 786440 | tf_op jit(solution)/shard_map/ppermute | solution.py:273
  92.3 19.1 %collective-permute-start.15 = (bf16[1024,128]{1,0:T(8,128)(2,1)S(1)}, bf16[1024,128]{1,0:T(8,128)(2,1)S(1)}, u32[]{:S(2)}, u32[]{:S(2)}) collective-permute-start(bf16[1024,128]{1,0:T(8,128)(2,1)S(1)} %get-tuple-element.36), channel_id=1, source_target_pairs={{0,2},{1,3},{2,0},{3,1},{4,6},{5,7},{6,4},{7,5},{8,10},{9,11},{10,... | collective-permute-start | bytes 786440 | tf_op jit(solution)/shard_map/ppermute | solution.py:273
  93.5 17.9 %collective-permute-start.16 = (bf16[1024,128]{1,0:T(8,128)(2,1)S(1)}, bf16[1024,128]{1,0:T(8,128)(2,1)S(1)}, u32[]{:S(2)}, u32[]{:S(2)}) collective-permute-start(bf16[1024,128]{1,0:T(8,128)(2,1)S(1)} %get-tuple-element.37), channel_id=1, source_target_pairs={{0,3},{1,0},{2,1},{3,2},{4,7},{5,4},{6,5},{7,6},{8,11},{9,8},{10,9... | collective-permute-start | bytes 786440 | tf_op jit(solution)/shard_map/ppermute | solution.py:273
  112.5 26.9 %all-to-all-start.1 = ((bf16[64,32,128]{2,1,0:T(8,128)(2,1)}), bf16[64,32,128]{2,1,0:T(8,128)(2,1)S(1)}, u32[]{:S(2)}, u32[]{:S(2)}) async-start(bf16[64,32,128]{2,1,0:T(8,128)(2,1)} %bitcast.10), calls=%async_computation.1 | async-start | bytes 1048576 | tf_op jit(solution)/shard_map/all_to_all | solution.py:310
  122.2 5.9 %collective-permute-start.26 = (bf16[32,2048]{1,0:T(8,128)(2,1)S(1)}, bf16[32,2048]{1,0:T(8,128)(2,1)S(1)}, u32[]{:S(2)}, u32[]{:S(2)}) collective-permute-start(bf16[32,2048]{1,0:T(8,128)(2,1)S(1)} %get-tuple-element.46), channel_id=1, source_target_pairs={{0,64},{64,128},{128,192},{192,0},{1,65},{65,129},{129,193},{193,1... | collective-permute-start | bytes 393224 | tf_op jit(solution)/shard_map/ppermute | solution.py:273
  123.3 8.6 %collective-permute-start.27 = (bf16[32,2048]{1,0:T(8,128)(2,1)S(1)}, bf16[32,2048]{1,0:T(8,128)(2,1)S(1)}, u32[]{:S(2)}, u32[]{:S(2)}) collective-permute-start(bf16[32,2048]{1,0:T(8,128)(2,1)S(1)} %get-tuple-element.47), channel_id=1, source_target_pairs={{0,128},{64,192},{128,0},{192,64},{1,129},{65,193},{129,1},{193,65... | collective-permute-start | bytes 393224 | tf_op jit(solution)/shard_map/ppermute | solution.py:273
  125.9 6.0 %collective-permute-start.28 = (bf16[32,2048]{1,0:T(8,128)(2,1)S(1)}, bf16[32,2048]{1,0:T(8,128)(2,1)S(1)}, u32[]{:S(2)}, u32[]{:S(2)}) collective-permute-start(bf16[32,2048]{1,0:T(8,128)(2,1)S(1)} %get-tuple-element.48), channel_id=1, source_target_pairs={{0,192},{64,0},{128,64},{192,128},{1,193},{65,1},{129,65},{193,129... | collective-permute-start | bytes 393224 | tf_op jit(solution)/shard_map/ppermute | solution.py:273
  (4 other events, 3.1 us)

commit v2 on v1

--- a/solution.py
+++ b/solution.py
@@ -12,7 +12,8 @@
 F32 = jnp.float32
 VMEM = pltpu.VMEM
 WHOLE = pl.BlockSpec(memory_space=pltpu.VMEM)
-SCALARS = pl.BlockSpec(memory_space=pltpu.SMEM)
+FAR = pl.BlockSpec(memory_space=pltpu.HBM)
+PREP = 60
 ANYWHERE = pl.BlockSpec(memory_space=pl.ANY)
 
 
@@ -33,14 +34,23 @@
     return MQ + TAIL if q == 0 else MQ
 
 
-def prep_a_kernel(dm, a, rm, *rest):
-    outs, spare = rest[:NQ], rest[NQ]
+def fetch(pairs, sems):
+    copies = [pltpu.make_async_copy(source, to, sems.at[n]) for n, (source, to) in enumerate(pairs)]
+    for copy in copies:
+        copy.start()
+    for copy in copies:
+        copy.wait()
+
+
+def prep_a_kernel(dm_in, a_in, rm_in, *rest):
+    outs, (spare, dm, a, rm, sems) = rest[:NQ], rest[NQ:]
+    fetch(((dm_in, dm), (a_in, a), (rm_in, rm)), sems)
     per = 4 // NQ
     for q in range(NQ):
         for xb in range(4):
             for j in range(per):
                 block = xb * 4 + q * per + j
-                keep = dm[block].astype(F32)
+                keep = dm[0, block].astype(F32)
                 value = a[block * 128 : (block + 1) * 128, :].astype(F32) * keep
                 at = (xb * per + j) * 128
                 outs[q][at : at + 128, :] = value.astype(BF)
@@ -53,15 +63,22 @@
     return pl.pallas_call(
         prep_a_kernel,
         out_shape=[jax.ShapeDtypeStruct((rows_of(q), 128), BF) for q in range(NQ)],
-        in_specs=[SCALARS, WHOLE, WHOLE],
+        in_specs=[FAR] * 3,
         out_specs=[WHOLE] * NQ,
-        scratch_shapes=[VMEM((TAIL, 128), F32)],
-        compiler_params=params(),
+        scratch_shapes=[
+            VMEM((TAIL, 128), F32),
+            pltpu.SMEM((1, 16), jnp.int32),
+            VMEM((2048, 128), BF),
+            VMEM((4, 16), jnp.int32),
+            pltpu.SemaphoreType.DMA((3,)),
+        ],
+        compiler_params=params(PREP),
         cost_estimate=cost(2048 * 128, 2 * 2048 * 128 * 2),
     )(dm, a, rm)
 
 
-def prep_b_kernel(mask, b, out):
+def prep_b_kernel(mask_in, b_in, out, mask, b, sems):
+    fetch(((mask_in, mask), (b_in, b)), sems)
     for tb in range(4):
         for cb in range(4):
             keep = mask[tb, cb].astype(F32)
@@ -76,39 +93,57 @@
     return pl.pallas_call(
         prep_b_kernel,
         out_shape=jax.ShapeDtypeStruct((16, 64, 256), BF),
-        in_specs=[SCALARS, WHOLE],
+        in_specs=[FAR] * 2,
         out_specs=WHOLE,
-        compiler_params=params(),
+        scratch_shapes=[pltpu.SMEM((4, 4), jnp.int32), VMEM((512, 512), BF), pltpu.SemaphoreType.DMA((2,))],
+        compiler_params=params(PREP),
         cost_estimate=cost(512 * 512, 2 * 512 * 512 * 2),
     )(mask, b)
 
 
-def load(q, half, pieces, bs, a_full, b_full, sems, b_sems, tails, more=()):
-    y, z, _, x = position()
-    copies = list(more)
+def arrange_kernel(*refs):
+    bs, outs, sems = refs[:5], refs[5:7], refs[7]
+    y, _, core, x = position()
     bands = (slice(0, 4), slice(0, 4), slice(0, 4), slice(0, 2), slice(2, 4))
+    pairs = []
     for s, back in enumerate((0, 1, 3, 2, 2)):
         lanes = pl.ds(pl.multiple_of(lax.rem(y - back + 4, 4) * 256, 256), 256)
         for ahead in range(4):
             layer = lax.rem(x + ahead, 4)
-            to = b_full.at[ahead, bands[s], :, lanes]
-            copies.append(pltpu.make_async_copy(bs[s].at[:, layer, half], to, b_sems.at[4 * s + ahead]))
+            for half in range(2):
+                side = core if half == 0 else 1 - core
+                pairs.append((bs[s].at[:, layer, side], outs[half].at[ahead, bands[s], :, lanes]))
+    fetch(pairs, sems)
+
+
+def arrange(bs):
+    return pl.pallas_call(
+        arrange_kernel,
+        out_shape=[jax.ShapeDtypeStruct((4, 4, 32, 1024), BF)] * 2,
+        in_specs=[ANYWHERE] * 5,
+        out_specs=[WHOLE] * 2,
+        scratch_shapes=[pltpu.SemaphoreType.DMA((40,))],
+        compiler_params=params(),
+        cost_estimate=cost(0, 4 * 1024 * 1024),
+    )(*bs)
+
+
+def load(q, pieces, a_full, sems, tails, more=()):
+    z = position()[1]
+    pairs = list(more)
     for s in range(8):
         lanes = pl.ds(pl.multiple_of(lax.rem(z - s + 8, 8) * 128, 128), 128)
-        copies.append(pltpu.make_async_copy(pieces[s].at[0:MQ], a_full.at[:, lanes], sems.at[s]))
+        pairs.append((pieces[s].at[0:MQ], a_full.at[:, lanes]))
     if q == 0:
         for s in range(8):
-            copies.append(pltpu.make_async_copy(pieces[s].at[MQ : MQ + TAIL], tails.at[s], sems.at[13 + s]))
-    for copy in copies:
-        copy.start()
-    for copy in copies:
-        copy.wait()
-
-
-def multiply(a_full, b_full, rows):
+            pairs.append((pieces[s].at[MQ : MQ + TAIL], tails.at[s]))
+    fetch(pairs, sems)
+
+
+def multiply(a_full, b, rows):
     return lax.dot_general(
         a_full[rows, :],
-        b_full[...].reshape(512, 1024),
+        b[...].reshape(512, 1024),
         (((1,), (1,)), ((), ())),
         preferred_element_type=F32,
     )
@@ -129,53 +164,44 @@
 
 
 def send_kernel(q, *refs):
-    pieces, bs, out = refs[:8], refs[8:13], refs[13]
-    a_full, b_full, tails, sems, b_sems = refs[14:]
-    core = position()[2]
-    load(q, 1 - core, pieces, bs, a_full, b_full, sems, b_sems, tails)
+    pieces, b, out = refs[:8], refs[8], refs[9]
+    a_full, tails, sems = refs[10:]
+    load(q, pieces, a_full, sems, tails)
     for part in range(4):
         rows = slice(part * (MQ // 4), (part + 1) * (MQ // 4))
-        out[rows, :] = multiply(a_full, b_full, rows).astype(BF)
+        out[rows, :] = multiply(a_full, b, rows).astype(BF)
     if q == 0:
         out[MQ : MQ + TAIL, :] = jnp.zeros((TAIL, 512), BF)
         out[MQ : MQ + TAIL, 0:128] = mask_rows(tails).astype(BF)
 
 
 def scratches():
-    return [
-        VMEM((MQ, 1024), BF),
-        VMEM((4, 4, 32, 1024), BF),
-        VMEM((8, TAIL, 128), BF),
-        pltpu.SemaphoreType.DMA((22,)),
-        pltpu.SemaphoreType.DMA((20,)),
-    ]
-
-
-def send_half(q, pieces, bs):
+    return [VMEM((MQ, 1024), BF), VMEM((8, TAIL, 128), BF), pltpu.SemaphoreType.DMA((17,))]
+
+
+def send_half(q, pieces, b):
     return pl.pallas_call(
         lambda *refs: send_kernel(q, *refs),
         out_shape=jax.ShapeDtypeStruct((rows_of(q), 512), BF),
-        in_specs=[ANYWHERE] * 13,
+        in_specs=[ANYWHERE] * 8 + [WHOLE],
         out_specs=WHOLE,
         scratch_shapes=scratches(),
         compiler_params=params(),
         cost_estimate=cost(2 * MQ * 1024 * 512, MQ * 1024 * 2 + 1024 * 1024),
-    )(*pieces, *bs)
+    )(*pieces, b)
 
 
 def keep_kernel(q, *refs):
-    pieces, bs, received = refs[:8], refs[8:13], refs[13]
-    own, outs = refs[14], refs[15:18]
-    rest = refs[18:]
+    pieces, b, received = refs[:8], refs[8], refs[9]
+    own, outs = refs[10], refs[11:14]
+    rest = refs[14:]
     if q == 0:
         mask, rest = rest[0], rest[1:]
-    a_full, b_full, tails, sems, b_sems, other = rest
-    core = position()[2]
-    arrival = pltpu.make_async_copy(received, other, sems.at[21])
-    load(q, core, pieces, bs, a_full, b_full, sems, b_sems, tails, [arrival])
+    a_full, tails, sems, other = rest
+    load(q, pieces, a_full, sems, tails, [(received, other)])
     for part in range(4):
         rows = slice(part * (MQ // 4), (part + 1) * (MQ // 4))
-        value = multiply(a_full, b_full, rows) + other[rows, :].astype(F32)
+        value = multiply(a_full, b, rows) + other[rows, :].astype(F32)
         own[rows, :] = value[:, 0:128]
         for s in range(1, 4):
             outs[s - 1][rows, :] = value[:, s * 128 : (s + 1) * 128].astype(BF)
@@ -183,7 +209,7 @@
         mask[...] = mask_rows(tails) + other[MQ : MQ + TAIL, 0:128].astype(F32)
 
 
-def keep_half(q, pieces, bs, received):
+def keep_half(q, pieces, b, received):
     part = (MQ, 128)
     shapes = [jax.ShapeDtypeStruct(part, F32)] + [jax.ShapeDtypeStruct(part, BF)] * 3
     if q == 0:
@@ -191,12 +217,12 @@
     return pl.pallas_call(
         lambda *refs: keep_kernel(q, *refs),
         out_shape=shapes,
-        in_specs=[ANYWHERE] * 14,
+        in_specs=[ANYWHERE] * 8 + [WHOLE, ANYWHERE],
         out_specs=[WHOLE] * len(shapes),
         scratch_shapes=scratches() + [VMEM((rows_of(q), 512), BF)],
         compiler_params=params(),
         cost_estimate=cost(2 * MQ * 1024 * 512, MQ * 1024 * 2 + 2 * 1024 * 1024),
-    )(*pieces, *bs, received)
+    )(*pieces, b, received)
 
 
 def sum_kernel(*refs):
@@ -274,7 +300,7 @@
 
 
 def per_device(density, response, density_mask, response_mask, result_mask):
-    chunks = prep_a(density.reshape(2048, 128), density_mask.reshape(16), result_mask.T)
+    chunks = prep_a(density.reshape(2048, 128), density_mask.reshape(1, 16), result_mask.T)
     chunks, response = lax.optimization_barrier((chunks, response))
     b_send = prep_b(response.reshape(512, 512), response_mask.reshape(4, 4))
 
@@ -295,13 +321,15 @@
     bs = [b_own, behind, ahead, turn(behind[:8], "row", 1), turn(ahead[8:], "row", -1)]
     bs = [value.reshape(-1, 4, 2, 32, 256) for value in bs]
 
+    kept_b, sent_b = arrange(bs)
+
     parts = []
     mask = None
     for q in range(NQ):
         pieces = [gathered[q][s] for s in range(8)]
-        other = send_half(q, pieces, bs)
+        other = send_half(q, pieces, sent_b)
         received = lax.ppermute(other, "col", [(i, i ^ 1) for i in range(16)])
-        kept = keep_half(q, pieces, bs, received)
+        kept = keep_half(q, pieces, kept_b, received)
         if q == 0:
             mask = kept[4]
         parts += [kept[0]] + [turn(kept[s], "layer", s) for s in (1, 2, 3)]

time: 141 us -> 138 us (0.979)
  local copies, waits for them, and re-layouts: 4.13 us -> 0.05 us
    unnamed x10 -> x4, local copies, waits for them, and re-layouts: 4.09 us -> 0.01 us
    ppermute x13, starting transfers between devices: 19.5 us -> 17 us  [turn(): return lax.ppermute(value, axis, [(i, (i + shift) % 4) for i in range(4)])]
  transfers between devices with their start and end apart: 31 -> 31, of which waited for: 14 -> 16; matrix products, arithmetic and copies ran while one was open for 0% -> 0% of each run, Pallas kernels for 7% -> 7%
where the time goes in v2:
time: 138 us
  starting transfers between devices  61.5 us (45%)
  waiting for transfers between devices  60 us (43%)
  Pallas kernels  15.9 us (12%)
    ppermute x14, waiting for transfers between devices, turn_z(): return lax.ppermute(value, 'col', pairs)  29.7 us
    ppermute x13, waiting for transfers between devices, turn(): return lax.ppermute(value, axis, [(i, (i + shift) % 4) for i in range(4)])  22.1 us
    ppermute x14, starting transfers between devices, turn_z(): return lax.ppermute(value, 'col', pairs)  17.9 us
    ppermute x13, starting transfers between devices, turn(): return lax.ppermute(value, axis, [(i, (i + shift) % 4) for i in range(4)])  17 us
    all_to_all x1, starting transfers between devices, per_device(): own = lax.all_to_all(product.reshape(64, 32, 128), ('col', 'layer'), 0, 0)  10.3 us
    all_to_all x1, starting transfers between devices, per_device(): b_own = lax.all_to_all(b_send, 'col', 0, 0)  9.99 us
    all_to_all x1, waiting for transfers between devices, per_device(): own = lax.all_to_all(product.reshape(64, 32, 128), ('col', 'layer'), 0, 0)  8.19 us
    ppermute x2, starting transfers between devices, per_device(): received = lax.ppermute(other, 'col', [(i, i ^ 1) for i in range(16)])  6.27 us
  transfers between devices with their start and end apart: 31, of which 16 were waited for; matrix products, arithmetic and copies ran while one was open for 0% of the time, Pallas kernels for 7%

profile of v2, /device:TPU:1, one launch (start us, length us, event | category | flops | bytes accessed | tf_op | source)
XLA Modules:
  0.0 137.5 jit_solution(1168105864878398542)
XLA Ops:
  0.0 2.0 %shard_map.55 = (bf16[1040,128]{1,0:T(8,128)(2,1)}, bf16[1024,128]{1,0:T(8,128)(2,1)}) custom-call(s32[1,16]{1,0:T(1,128)} %bitcast.21, bf16[2048,128]{1,0:T(8,128)(2,1)} %bitcast.17, s32[4,16]{1,0:T(4,128)} %bitcast.19), custom_call_target="tpu_custom_call" | custom-call | flops 262144 | bytes 1048576 | tf_op jit(solution)/shard_map/pallas_call | solution.py:63
  2.0 2.1 %shard_map.56 = bf16[16,64,256]{2,1,0:T(8,128)(2,1)} custom-call(s32[4,4]{1,0:T(4,128)} %bitcast.20, bf16[512,512]{1,0:T(8,128)(2,1)} %bitcast.18), custom_call_target="tpu_custom_call" | custom-call | flops 262144 | bytes 1048576 | tf_op jit(solution)/shard_map/pallas_call | solution.py:93
  4.1 10.0 %all-to-all-start = ((bf16[16,64,256]{2,1,0:T(8,128)(2,1)}), bf16[16,64,256]{2,1,0:T(8,128)(2,1)S(1)}, u32[]{:S(2)}, u32[]{:S(2)}) async-start(bf16[16,64,256]{2,1,0:T(8,128)(2,1)} %shard_map.56), calls=%async_computation | async-start | bytes 1048576 | tf_op jit(solution)/shard_map/all_to_all | solution.py:307
  14.1 1.5 %collective-permute-start.7 = (bf16[1024,128]{1,0:T(8,128)(2,1)S(1)}, bf16[1024,128]{1,0:T(8,128)(2,1)S(1)}, u32[]{:S(2)}, u32[]{:S(2)}) collective-permute-start(bf16[1024,128]{1,0:T(8,128)(2,1)S(1)} %copy-done.1), channel_id=1, source_target_pairs={{0,8},{4,12},{8,16},{12,20},{16,24},{20,28},{24,32},{28,36},{32,40... | collective-permute-start | bytes 786440 | tf_op jit(solution)/shard_map/ppermute | solution.py:295
  15.6 1.3 collective-permute-start.8
  17.1 17.5 %collective-permute-done.7.refs_1_ = bf16[1024,128]{1,0:T(8,128)(2,1)S(1)} collective-permute-done((bf16[1024,128]{1,0:T(8,128)(2,1)S(1)}, bf16[1024,128]{1,0:T(8,128)(2,1)S(1)}, u32[]{:S(2)}, u32[]{:S(2)}) %collective-permute-start.7) | collective-permute-done | bytes 262176 | tf_op jit(solution)/shard_map/ppermute | solution.py:295
  35.8 1.5 %collective-permute-start.10 = (bf16[16,64,256]{2,1,0:T(8,128)(2,1)S(1)}, bf16[16,64,256]{2,1,0:T(8,128)(2,1)S(1)}, u32[]{:S(2)}, u32[]{:S(2)}) collective-permute-start(bf16[16,64,256]{2,1,0:T(8,128)(2,1)S(1)} %all-to-all-done), channel_id=1, source_target_pairs={{0,192},{64,0},{128,64},{192,128},{1,193},{65,1},{129,65},{193,129... | collective-permute-start | bytes 1572872 | tf_op jit(solution)/shard_map/ppermute | solution.py:299
  38.6 1.7 %collective-permute-done.refs_1_ = bf16[1040,128]{1,0:T(8,128)(2,1)S(1)} collective-permute-done((bf16[1040,128]{1,0:T(8,128)(2,1)S(1)}, bf16[1040,128]{1,0:T(8,128)(2,1)S(1)}, u32[]{:S(2)}, u32[]{:S(2)}) %collective-permute-start) | collective-permute-done | bytes 266272 | tf_op jit(solution)/shard_map/ppermute | solution.py:295
  40.3 2.7 %collective-permute-start.19 = (bf16[1024,128]{1,0:T(8,128)(2,1)S(1)}, bf16[1024,128]{1,0:T(8,128)(2,1)S(1)}, u32[]{:S(2)}, u32[]{:S(2)}) collective-permute-start(bf16[1024,128]{1,0:T(8,128)(2,1)S(1)} %collective-permute-done.8.refs_7_), channel_id=1, source_target_pairs={{0,56},{4,60},{8,0},{12,4},{16,8},{20,12},{24,16},{28,20},{32,24},... | collective-permute-start | bytes 786440 | tf_op jit(solution)/shard_map/ppermute | solution.py:295
  43.5 2.4 %collective-permute-start.5 = (bf16[1040,128]{1,0:T(8,128)(2,1)S(1)}, bf16[1040,128]{1,0:T(8,128)(2,1)S(1)}, u32[]{:S(2)}, u32[]{:S(2)}) collective-permute-start(bf16[1040,128]{1,0:T(8,128)(2,1)S(1)} %collective-permute-done.4.refs_7_), channel_id=1, source_target_pairs={{0,56},{4,60},{8,0},{12,4},{16,8},{20,12},{24,16},{28,20},{32,24},... | collective-permute-start | bytes 798728 | tf_op jit(solution)/shard_map/ppermute | solution.py:295
  45.9 2.6 %collective-permute-done.1.refs_2_ = bf16[1040,128]{1,0:T(8,128)(2,1)S(1)} collective-permute-done((bf16[1040,128]{1,0:T(8,128)(2,1)S(1)}, bf16[1040,128]{1,0:T(8,128)(2,1)S(1)}, u32[]{:S(2)}, u32[]{:S(2)}) %collective-permute-start.1) | collective-permute-done | bytes 266272 | tf_op jit(solution)/shard_map/ppermute | solution.py:295
  49.1 3.4 %collective-permute-start.20 = (bf16[1024,128]{1,0:T(8,128)(2,1)S(1)}, bf16[1024,128]{1,0:T(8,128)(2,1)S(1)}, u32[]{:S(2)}, u32[]{:S(2)}) collective-permute-start(bf16[1024,128]{1,0:T(8,128)(2,1)S(1)} %collective-permute-done.19.refs_6_), channel_id=1, source_target_pairs={{0,56},{4,60},{8,0},{12,4},{16,8},{20,12},{24,16},{28,20},{32,24},... | collective-permute-start | bytes 786440 | tf_op jit(solution)/shard_map/ppermute | solution.py:295
  52.7 2.1 %collective-permute-done.5.refs_6_ = bf16[1040,128]{1,0:T(8,128)(2,1)S(1)} collective-permute-done((bf16[1040,128]{1,0:T(8,128)(2,1)S(1)}, bf16[1040,128]{1,0:T(8,128)(2,1)S(1)}, u32[]{:S(2)}, u32[]{:S(2)}) %collective-permute-start.5) | collective-permute-done | bytes 266272 | tf_op jit(solution)/shard_map/ppermute | solution.py:295
  54.8 2.3 %collective-permute-start.12 = (bf16[8,64,256]{2,1,0:T(8,128)(2,1)S(1)}, bf16[8,64,256]{2,1,0:T(8,128)(2,1)S(1)}, u32[]{:S(2)}, u32[]{:S(2)}) collective-permute-start(bf16[8,64,256]{2,1,0:T(8,128)(2,1)S(1)} %slice.9), channel_id=1, source_target_pairs={{0,192},{64,0},{128,64},{192,128},{1,193},{65,1},{129,65},{193,129... | collective-permute-start | bytes 786440 | tf_op jit(solution)/shard_map/ppermute | solution.py:299
  57.6 2.9 %collective-permute-done.20.refs_5_ = bf16[1024,128]{1,0:T(8,128)(2,1)S(1)} collective-permute-done((bf16[1024,128]{1,0:T(8,128)(2,1)S(1)}, bf16[1024,128]{1,0:T(8,128)(2,1)S(1)}, u32[]{:S(2)}, u32[]{:S(2)}) %collective-permute-start.20) | collective-permute-done | bytes 262176 | tf_op jit(solution)/shard_map/ppermute | solution.py:295
  60.4 3.4 %collective-permute-start.21 = (bf16[1024,128]{1,0:T(8,128)(2,1)S(1)}, bf16[1024,128]{1,0:T(8,128)(2,1)S(1)}, u32[]{:S(2)}, u32[]{:S(2)}) collective-permute-start(bf16[1024,128]{1,0:T(8,128)(2,1)S(1)} %collective-permute-done.20.refs_5_), channel_id=1, source_target_pairs={{0,56},{4,60},{8,0},{12,4},{16,8},{20,12},{24,16},{28,20},{32,24},... | collective-permute-start | bytes 786440 | tf_op jit(solution)/shard_map/ppermute | solution.py:295
  63.9 1.4 %collective-permute-start.3 = (bf16[1040,128]{1,0:T(8,128)(2,1)S(1)}, bf16[1040,128]{1,0:T(8,128)(2,1)S(1)}, u32[]{:S(2)}, u32[]{:S(2)}) collective-permute-start(bf16[1040,128]{1,0:T(8,128)(2,1)S(1)} %collective-permute-done.2.refs_3_), channel_id=1, source_target_pairs={{0,8},{4,12},{8,16},{12,20},{16,24},{20,28},{24,32},{28,36},{32,40... | collective-permute-start | bytes 798728 | tf_op jit(solution)/shard_map/ppermute | solution.py:295
  67.8 2.1 %shard_map.60 = bf16[1024,512]{1,0:T(8,128)(2,1)S(1)} custom-call(bf16[1024,128]{1,0:T(8,128)(2,1)S(1)} %copy-done.1, bf16[1024,128]{1,0:T(8,128)(2,1)S(1)} %collective-permute-done.7.refs_1_, bf16[1024,128]{1,0:T(8,128)(2,1)S(1)} %collective-permute-done.17.refs_2_, bf16[1024,128]{1,0:T(8,128)(2,1)S(1)} %collective-permute-done.18.refs_3_, ...), custom_call_target="tpu_custom_call" | custom-call | flops 1073741824 | bytes 3145728 | tf_op jit(solution)/shard_map/pallas_call | solution.py:183
  69.9 4.9 %collective-permute-start.22 = (bf16[1024,512]{1,0:T(8,128)(2,1)S(1)}, bf16[1024,512]{1,0:T(8,128)(2,1)S(1)}, u32[]{:S(2)}, u32[]{:S(2)}) collective-permute-start(bf16[1024,512]{1,0:T(8,128)(2,1)S(1)} %shard_map.60), channel_id=1, source_target_pairs={{0,4},{4,0},{8,12},{12,8},{16,20},{20,16},{24,28},{28,24},{32,36},... | collective-permute-start | bytes 3145736 | tf_op jit(solution)/shard_map/ppermute | solution.py:331
  74.7 2.1 %shard_map.58 = bf16[1040,512]{1,0:T(8,128)(2,1)S(1)} custom-call(bf16[1040,128]{1,0:T(8,128)(2,1)S(1)} %copy-done, bf16[1040,128]{1,0:T(8,128)(2,1)S(1)} %collective-permute-done.refs_1_, bf16[1040,128]{1,0:T(8,128)(2,1)S(1)} %collective-permute-done.1.refs_2_, bf16[1040,128]{1,0:T(8,128)(2,1)S(1)} %collective-permute-done.2.refs_3_, ...), custom_call_target="tpu_custom_call" | custom-call | flops 1073741824 | bytes 3145728 | tf_op jit(solution)/shard_map/pallas_call | solution.py:183
  76.9 1.4 %collective-permute-start.13 = (bf16[1040,512]{1,0:T(8,128)(2,1)S(1)}, bf16[1040,512]{1,0:T(8,128)(2,1)S(1)}, u32[]{:S(2)}, u32[]{:S(2)}) collective-permute-start(bf16[1040,512]{1,0:T(8,128)(2,1)S(1)} %shard_map.58), channel_id=1, source_target_pairs={{0,4},{4,0},{8,12},{12,8},{16,20},{20,16},{24,28},{28,24},{32,36},... | collective-permute-start | bytes 3194888 | tf_op jit(solution)/shard_map/ppermute | solution.py:331
  78.3 2.1 %shard_map.61 = (f32[1024,128]{1,0:T(8,128)S(1)}, bf16[1024,128]{1,0:T(8,128)(2,1)S(1)}, bf16[1024,128]{1,0:T(8,128)(2,1)S(1)}, bf16[1024,128]{1,0:T(8,128)(2,1)S(1)}) custom-call(bf16[1024,128]{1,0:T(8,128)(2,1)S(1)} %copy-done.1, bf16[1024,128]{1,0:T(8,128)(2,1)S(1)} %collective-permute-done.7.refs_1_, ...), custom_call_target="tpu_custom_call" | custom-call | flops 1073741824 | bytes 4194304 | tf_op jit(solution)/shard_map/pallas_call | solution.py:217
  81.8 2.4 %collective-permute-start.24 = (bf16[1024,128]{1,0:T(8,128)(2,1)S(1)}, bf16[1024,128]{1,0:T(8,128)(2,1)S(1)}, u32[]{:S(2)}, u32[]{:S(2)}) collective-permute-start(bf16[1024,128]{1,0:T(8,128)(2,1)S(1)} %get-tuple-element.46), channel_id=1, source_target_pairs={{0,2},{1,3},{2,0},{3,1},{4,6},{5,7},{6,4},{7,5},{8,10},{9,11},{10,... | collective-permute-start | bytes 786440 | tf_op jit(solution)/shard_map/ppermute | solution.py:299
  85.4 2.2 %shard_map.59 = (f32[1024,128]{1,0:T(8,128)S(1)}, bf16[1024,128]{1,0:T(8,128)(2,1)S(1)}, bf16[1024,128]{1,0:T(8,128)(2,1)S(1)}, bf16[1024,128]{1,0:T(8,128)(2,1)S(1)}, f32[16,128]{1,0:T(8,128)S(1)}) custom-call(bf16[1040,128]{1,0:T(8,128)(2,1)S(1)} %copy-done, bf16[1040,128]{1,0:T(8,128)(2,1)S(1)} %collective-permute-done.refs_1_, ...), custom_call_target="tpu_custom_call" | custom-call | flops 1073741824 | bytes 4194304 | tf_op jit(solution)/shard_map/pallas_call | solution.py:217
  90.9 5.4 %collective-permute-done.24.refs_7_ = bf16[1024,128]{1,0:T(8,128)(2,1)S(1)} collective-permute-done((bf16[1024,128]{1,0:T(8,128)(2,1)S(1)}, bf16[1024,128]{1,0:T(8,128)(2,1)S(1)}, u32[]{:S(2)}, u32[]{:S(2)}) %collective-permute-start.24) | collective-permute-done | bytes 262176 | tf_op jit(solution)/shard_map/ppermute | solution.py:299
  96.3 6.2 %collective-permute-done.14.refs_2_ = bf16[1024,128]{1,0:T(8,128)(2,1)S(1)} collective-permute-done((bf16[1024,128]{1,0:T(8,128)(2,1)S(1)}, bf16[1024,128]{1,0:T(8,128)(2,1)S(1)}, u32[]{:S(2)}, u32[]{:S(2)}) %collective-permute-start.14) | collective-permute-done | bytes 262176 | tf_op jit(solution)/shard_map/ppermute | solution.py:299
  102.5 5.0 %collective-permute-done.15.refs_3_ = bf16[1024,128]{1,0:T(8,128)(2,1)S(1)} collective-permute-done((bf16[1024,128]{1,0:T(8,128)(2,1)S(1)}, bf16[1024,128]{1,0:T(8,128)(2,1)S(1)}, u32[]{:S(2)}, u32[]{:S(2)}) %collective-permute-start.15) | collective-permute-done | bytes 262176 | tf_op jit(solution)/shard_map/ppermute | solution.py:299
  108.7 10.3 %all-to-all-start.1 = ((bf16[64,32,128]{2,1,0:T(8,128)(2,1)}), bf16[64,32,128]{2,1,0:T(8,128)(2,1)S(1)}, u32[]{:S(2)}, u32[]{:S(2)}) async-start(bf16[64,32,128]{2,1,0:T(8,128)(2,1)} %bitcast.10), calls=%async_computation.1 | async-start | bytes 1048576 | tf_op jit(solution)/shard_map/all_to_all | solution.py:338
  119.5 2.6 %collective-permute-start.27 = (bf16[32,2048]{1,0:T(8,128)(2,1)S(1)}, bf16[32,2048]{1,0:T(8,128)(2,1)S(1)}, u32[]{:S(2)}, u32[]{:S(2)}) collective-permute-start(bf16[32,2048]{1,0:T(8,128)(2,1)S(1)} %get-tuple-element.51), channel_id=1, source_target_pairs={{0,128},{64,192},{128,0},{192,64},{1,129},{65,193},{129,1},{193,65... | collective-permute-start | bytes 393224 | tf_op jit(solution)/shard_map/ppermute | solution.py:299
  123.2 1.7 %collective-permute-done.26.refs_1_ = bf16[32,2048]{1,0:T(8,128)(2,1)S(1)} collective-permute-done((bf16[32,2048]{1,0:T(8,128)(2,1)S(1)}, bf16[32,2048]{1,0:T(8,128)(2,1)S(1)}, u32[]{:S(2)}, u32[]{:S(2)}) %collective-permute-start.26) | collective-permute-done | bytes 131104 | tf_op jit(solution)/shard_map/ppermute | solution.py:299
  124.9 3.2 %collective-permute-done.27.refs_2_ = bf16[32,2048]{1,0:T(8,128)(2,1)S(1)} collective-permute-done((bf16[32,2048]{1,0:T(8,128)(2,1)S(1)}, bf16[32,2048]{1,0:T(8,128)(2,1)S(1)}, u32[]{:S(2)}, u32[]{:S(2)}) %collective-permute-start.27) | collective-permute-done | bytes 131104 | tf_op jit(solution)/shard_map/ppermute | solution.py:299
  128.1 8.2 %all-to-all-done.1.own = bf16[64,32,128]{2,1,0:T(8,128)(2,1)S(1)} async-done(((bf16[64,32,128]{2,1,0:T(8,128)(2,1)}), bf16[64,32,128]{2,1,0:T(8,128)(2,1)S(1)}, u32[]{:S(2)}, u32[]{:S(2)}) %all-to-all-start.1) | async-done | bytes 524320 | tf_op jit(solution)/shard_map/all_to_all | solution.py:338
  (45 shorter events, 16.7 us)
Async XLA Ops:
  2.0 14.9 %copy-start = (bf16[1040,128]{1,0:T(8,128)(2,1)S(1)}, bf16[1040,128]{1,0:T(8,128)(2,1)}, u32[]{:S(2)}) copy-start(bf16[1040,128]{1,0:T(8,128)(2,1)} %get-tuple-element.31.refs_0_) | copy-start | bytes 798724
  4.1 30.4 %all-to-all-start = ((bf16[16,64,256]{2,1,0:T(8,128)(2,1)}), bf16[16,64,256]{2,1,0:T(8,128)(2,1)S(1)}, u32[]{:S(2)}, u32[]{:S(2)}) async-start(bf16[16,64,256]{2,1,0:T(8,128)(2,1)} %shard_map.56), calls=%async_computation | async-start | bytes 1048576 | tf_op jit(solution)/shard_map/all_to_all | solution.py:307
  14.1 20.4 %collective-permute-start.7 = (bf16[1024,128]{1,0:T(8,128)(2,1)S(1)}, bf16[1024,128]{1,0:T(8,128)(2,1)S(1)}, u32[]{:S(2)}, u32[]{:S(2)}) collective-permute-start(bf16[1024,128]{1,0:T(8,128)(2,1)S(1)} %copy-done.1), channel_id=1, source_target_pairs={{0,8},{4,12},{8,16},{12,20},{16,24},{20,28},{24,32},{28,36},{32,40... | collective-permute-start | bytes 786440 | tf_op jit(solution)/shard_map/ppermute | solution.py:295
  15.6 19.0 %collective-permute-start.8 = (bf16[1024,128]{1,0:T(8,128)(2,1)S(1)}, bf16[1024,128]{1,0:T(8,128)(2,1)S(1)}, u32[]{:S(2)}, u32[]{:S(2)}) collective-permute-start(bf16[1024,128]{1,0:T(8,128)(2,1)S(1)} %copy-done.1), channel_id=1, source_target_pairs={{0,56},{4,60},{8,0},{12,4},{16,8},{20,12},{24,16},{28,20},{32,24},... | collective-permute-start | bytes 786440 | tf_op jit(solution)/shard_map/ppermute | solution.py:295
  16.9 23.3 %collective-permute-start = (bf16[1040,128]{1,0:T(8,128)(2,1)S(1)}, bf16[1040,128]{1,0:T(8,128)(2,1)S(1)}, u32[]{:S(2)}, u32[]{:S(2)}) collective-permute-start(bf16[1040,128]{1,0:T(8,128)(2,1)S(1)} %copy-done), channel_id=1, source_target_pairs={{0,8},{4,12},{8,16},{12,20},{16,24},{20,28},{24,32},{28,36},{32,40... | collective-permute-start | bytes 798728 | tf_op jit(solution)/shard_map/ppermute | solution.py:295
  34.5 18.0 %collective-permute-start.9 = (bf16[16,64,256]{2,1,0:T(8,128)(2,1)S(1)}, bf16[16,64,256]{2,1,0:T(8,128)(2,1)S(1)}, u32[]{:S(2)}, u32[]{:S(2)}) collective-permute-start(bf16[16,64,256]{2,1,0:T(8,128)(2,1)S(1)} %all-to-all-done), channel_id=1, source_target_pairs={{0,64},{64,128},{128,192},{192,0},{1,65},{65,129},{129,193},{193,1... | collective-permute-start | bytes 1572872 | tf_op jit(solution)/shard_map/ppermute | solution.py:299
  35.8 16.7 %collective-permute-start.10 = (bf16[16,64,256]{2,1,0:T(8,128)(2,1)S(1)}, bf16[16,64,256]{2,1,0:T(8,128)(2,1)S(1)}, u32[]{:S(2)}, u32[]{:S(2)}) collective-permute-start(bf16[16,64,256]{2,1,0:T(8,128)(2,1)S(1)} %all-to-all-done), channel_id=1, source_target_pairs={{0,192},{64,0},{128,64},{192,128},{1,193},{65,1},{129,65},{193,129... | collective-permute-start | bytes 1572872 | tf_op jit(solution)/shard_map/ppermute | solution.py:299
  37.4 6.1 %collective-permute-start.4 = (bf16[1040,128]{1,0:T(8,128)(2,1)S(1)}, bf16[1040,128]{1,0:T(8,128)(2,1)S(1)}, u32[]{:S(2)}, u32[]{:S(2)}) collective-permute-start(bf16[1040,128]{1,0:T(8,128)(2,1)S(1)} %copy-done), channel_id=1, source_target_pairs={{0,56},{4,60},{8,0},{12,4},{16,8},{20,12},{24,16},{28,20},{32,24},... | collective-permute-start | bytes 798728 | tf_op jit(solution)/shard_map/ppermute | solution.py:295
  40.2 8.2 %collective-permute-start.1 = (bf16[1040,128]{1,0:T(8,128)(2,1)S(1)}, bf16[1040,128]{1,0:T(8,128)(2,1)S(1)}, u32[]{:S(2)}, u32[]{:S(2)}) collective-permute-start(bf16[1040,128]{1,0:T(8,128)(2,1)S(1)} %collective-permute-done.refs_1_), channel_id=1, source_target_pairs={{0,8},{4,12},{8,16},{12,20},{16,24},{20,28},{24,32},{28,36},{32,40... | collective-permute-start | bytes 798728 | tf_op jit(solution)/shard_map/ppermute | solution.py:295
  40.3 8.9 %collective-permute-start.19 = (bf16[1024,128]{1,0:T(8,128)(2,1)S(1)}, bf16[1024,128]{1,0:T(8,128)(2,1)S(1)}, u32[]{:S(2)}, u32[]{:S(2)}) collective-permute-start(bf16[1024,128]{1,0:T(8,128)(2,1)S(1)} %collective-permute-done.8.refs_7_), channel_id=1, source_target_pairs={{0,56},{4,60},{8,0},{12,4},{16,8},{20,12},{24,16},{28,20},{32,24},... | collective-permute-start | bytes 786440 | tf_op jit(solution)/shard_map/ppermute | solution.py:295
  43.5 11.3 %collective-permute-start.5 = (bf16[1040,128]{1,0:T(8,128)(2,1)S(1)}, bf16[1040,128]{1,0:T(8,128)(2,1)S(1)}, u32[]{:S(2)}, u32[]{:S(2)}) collective-permute-start(bf16[1040,128]{1,0:T(8,128)(2,1)S(1)} %collective-permute-done.4.refs_7_), channel_id=1, source_target_pairs={{0,56},{4,60},{8,0},{12,4},{16,8},{20,12},{24,16},{28,20},{32,24},... | collective-permute-start | bytes 798728 | tf_op jit(solution)/shard_map/ppermute | solution.py:295
  48.5 8.6 %collective-permute-start.17 = (bf16[1024,128]{1,0:T(8,128)(2,1)S(1)}, bf16[1024,128]{1,0:T(8,128)(2,1)S(1)}, u32[]{:S(2)}, u32[]{:S(2)}) collective-permute-start(bf16[1024,128]{1,0:T(8,128)(2,1)S(1)} %collective-permute-done.7.refs_1_), channel_id=1, source_target_pairs={{0,8},{4,12},{8,16},{12,20},{16,24},{20,28},{24,32},{28,36},{32,40... | collective-permute-start | bytes 786440 | tf_op jit(solution)/shard_map/ppermute | solution.py:295
  49.1 11.3 %collective-permute-start.20 = (bf16[1024,128]{1,0:T(8,128)(2,1)S(1)}, bf16[1024,128]{1,0:T(8,128)(2,1)S(1)}, u32[]{:S(2)}, u32[]{:S(2)}) collective-permute-start(bf16[1024,128]{1,0:T(8,128)(2,1)S(1)} %collective-permute-done.19.refs_6_), channel_id=1, source_target_pairs={{0,56},{4,60},{8,0},{12,4},{16,8},{20,12},{24,16},{28,20},{32,24},... | collective-permute-start | bytes 786440 | tf_op jit(solution)/shard_map/ppermute | solution.py:295
  52.5 11.3 %collective-permute-start.2 = (bf16[1040,128]{1,0:T(8,128)(2,1)S(1)}, bf16[1040,128]{1,0:T(8,128)(2,1)S(1)}, u32[]{:S(2)}, u32[]{:S(2)}) collective-permute-start(bf16[1040,128]{1,0:T(8,128)(2,1)S(1)} %collective-permute-done.1.refs_2_), channel_id=1, source_target_pairs={{0,8},{4,12},{8,16},{12,20},{16,24},{20,28},{24,32},{28,36},{32,40... | collective-permute-start | bytes 798728 | tf_op jit(solution)/shard_map/ppermute | solution.py:295
  52.6 11.3 %collective-permute-start.11 = (bf16[8,64,256]{2,1,0:T(8,128)(2,1)S(1)}, bf16[8,64,256]{2,1,0:T(8,128)(2,1)S(1)}, u32[]{:S(2)}, u32[]{:S(2)}) collective-permute-start(bf16[8,64,256]{2,1,0:T(8,128)(2,1)S(1)} %slice.8), channel_id=1, source_target_pairs={{0,64},{64,128},{128,192},{192,0},{1,65},{65,129},{129,193},{193,1... | collective-permute-start | bytes 786440 | tf_op jit(solution)/shard_map/ppermute | solution.py:299
  54.8 10.5 %collective-permute-start.12 = (bf16[8,64,256]{2,1,0:T(8,128)(2,1)S(1)}, bf16[8,64,256]{2,1,0:T(8,128)(2,1)S(1)}, u32[]{:S(2)}, u32[]{:S(2)}) collective-permute-start(bf16[8,64,256]{2,1,0:T(8,128)(2,1)S(1)} %slice.9), channel_id=1, source_target_pairs={{0,192},{64,0},{128,64},{192,128},{1,193},{65,1},{129,65},{193,129... | collective-permute-start | bytes 786440 | tf_op jit(solution)/shard_map/ppermute | solution.py:299
  57.1 10.1 %collective-permute-start.18 = (bf16[1024,128]{1,0:T(8,128)(2,1)S(1)}, bf16[1024,128]{1,0:T(8,128)(2,1)S(1)}, u32[]{:S(2)}, u32[]{:S(2)}) collective-permute-start(bf16[1024,128]{1,0:T(8,128)(2,1)S(1)} %collective-permute-done.17.refs_2_), channel_id=1, source_target_pairs={{0,8},{4,12},{8,16},{12,20},{16,24},{20,28},{24,32},{28,36},{32,40... | collective-permute-start | bytes 786440 | tf_op jit(solution)/shard_map/ppermute | solution.py:295
  60.4 7.3 %collective-permute-start.21 = (bf16[1024,128]{1,0:T(8,128)(2,1)S(1)}, bf16[1024,128]{1,0:T(8,128)(2,1)S(1)}, u32[]{:S(2)}, u32[]{:S(2)}) collective-permute-start(bf16[1024,128]{1,0:T(8,128)(2,1)S(1)} %collective-permute-done.20.refs_5_), channel_id=1, source_target_pairs={{0,56},{4,60},{8,0},{12,4},{16,8},{20,12},{24,16},{28,20},{32,24},... | collective-permute-start | bytes 786440 | tf_op jit(solution)/shard_map/ppermute | solution.py:295
  63.9 10.9 %collective-permute-start.6 = (bf16[1040,128]{1,0:T(8,128)(2,1)S(1)}, bf16[1040,128]{1,0:T(8,128)(2,1)S(1)}, u32[]{:S(2)}, u32[]{:S(2)}) collective-permute-start(bf16[1040,128]{1,0:T(8,128)(2,1)S(1)} %collective-permute-done.5.refs_6_), channel_id=1, source_target_pairs={{0,56},{4,60},{8,0},{12,4},{16,8},{20,12},{24,16},{28,20},{32,24},... | collective-permute-start | bytes 798728 | tf_op jit(solution)/shard_map/ppermute | solution.py:295
  63.9 10.9 %collective-permute-start.3 = (bf16[1040,128]{1,0:T(8,128)(2,1)S(1)}, bf16[1040,128]{1,0:T(8,128)(2,1)S(1)}, u32[]{:S(2)}, u32[]{:S(2)}) collective-permute-start(bf16[1040,128]{1,0:T(8,128)(2,1)S(1)} %collective-permute-done.2.refs_3_), channel_id=1, source_target_pairs={{0,8},{4,12},{8,16},{12,20},{16,24},{20,28},{24,32},{28,36},{32,40... | collective-permute-start | bytes 798728 | tf_op jit(solution)/shard_map/ppermute | solution.py:295
  69.9 8.4 %collective-permute-start.22 = (bf16[1024,512]{1,0:T(8,128)(2,1)S(1)}, bf16[1024,512]{1,0:T(8,128)(2,1)S(1)}, u32[]{:S(2)}, u32[]{:S(2)}) collective-permute-start(bf16[1024,512]{1,0:T(8,128)(2,1)S(1)} %shard_map.60), channel_id=1, source_target_pairs={{0,4},{4,0},{8,12},{12,8},{16,20},{20,16},{24,28},{28,24},{32,36},... | collective-permute-start | bytes 3145736 | tf_op jit(solution)/shard_map/ppermute | solution.py:331
  76.9 8.5 %collective-permute-start.13 = (bf16[1040,512]{1,0:T(8,128)(2,1)S(1)}, bf16[1040,512]{1,0:T(8,128)(2,1)S(1)}, u32[]{:S(2)}, u32[]{:S(2)}) collective-permute-start(bf16[1040,512]{1,0:T(8,128)(2,1)S(1)} %shard_map.58), channel_id=1, source_target_pairs={{0,4},{4,0},{8,12},{12,8},{16,20},{20,16},{24,28},{28,24},{32,36},... | collective-permute-start | bytes 3194888 | tf_op jit(solution)/shard_map/ppermute | solution.py:331
  80.5 9.2 %collective-permute-start.23 = (bf16[1024,128]{1,0:T(8,128)(2,1)S(1)}, bf16[1024,128]{1,0:T(8,128)(2,1)S(1)}, u32[]{:S(2)}, u32[]{:S(2)}) collective-permute-start(bf16[1024,128]{1,0:T(8,128)(2,1)S(1)} %get-tuple-element.45), channel_id=1, source_target_pairs={{0,1},{1,2},{2,3},{3,0},{4,5},{5,6},{6,7},{7,4},{8,9},{9,10},{10,1... | collective-permute-start | bytes 786440 | tf_op jit(solution)/shard_map/ppermute | solution.py:299
  81.8 14.5 %collective-permute-start.24 = (bf16[1024,128]{1,0:T(8,128)(2,1)S(1)}, bf16[1024,128]{1,0:T(8,128)(2,1)S(1)}, u32[]{:S(2)}, u32[]{:S(2)}) collective-permute-start(bf16[1024,128]{1,0:T(8,128)(2,1)S(1)} %get-tuple-element.46), channel_id=1, source_target_pairs={{0,2},{1,3},{2,0},{3,1},{4,6},{5,7},{6,4},{7,5},{8,10},{9,11},{10,... | collective-permute-start | bytes 786440 | tf_op jit(solution)/shard_map/ppermute | solution.py:299
  84.2 12.1 %collective-permute-start.25 = (bf16[1024,128]{1,0:T(8,128)(2,1)S(1)}, bf16[1024,128]{1,0:T(8,128)(2,1)S(1)}, u32[]{:S(2)}, u32[]{:S(2)}) collective-permute-start(bf16[1024,128]{1,0:T(8,128)(2,1)S(1)} %get-tuple-element.47), channel_id=1, source_target_pairs={{0,3},{1,0},{2,1},{3,2},{4,7},{5,4},{6,5},{7,6},{8,11},{9,8},{10,9... | collective-permute-start | bytes 786440 | tf_op jit(solution)/shard_map/ppermute | solution.py:299
  87.6 14.9 %collective-permute-start.14 = (bf16[1024,128]{1,0:T(8,128)(2,1)S(1)}, bf16[1024,128]{1,0:T(8,128)(2,1)S(1)}, u32[]{:S(2)}, u32[]{:S(2)}) collective-permute-start(bf16[1024,128]{1,0:T(8,128)(2,1)S(1)} %get-tuple-element.39), channel_id=1, source_target_pairs={{0,1},{1,2},{2,3},{3,0},{4,5},{5,6},{6,7},{7,4},{8,9},{9,10},{10,1... | collective-permute-start | bytes 786440 | tf_op jit(solution)/shard_map/ppermute | solution.py:299
  88.2 19.3 %collective-permute-start.15 = (bf16[1024,128]{1,0:T(8,128)(2,1)S(1)}, bf16[1024,128]{1,0:T(8,128)(2,1)S(1)}, u32[]{:S(2)}, u32[]{:S(2)}) collective-permute-start(bf16[1024,128]{1,0:T(8,128)(2,1)S(1)} %get-tuple-element.40), channel_id=1, source_target_pairs={{0,2},{1,3},{2,0},{3,1},{4,6},{5,7},{6,4},{7,5},{8,10},{9,11},{10,... | collective-permute-start | bytes 786440 | tf_op jit(solution)/shard_map/ppermute | solution.py:299
  89.6 17.9 %collective-permute-start.16 = (bf16[1024,128]{1,0:T(8,128)(2,1)S(1)}, bf16[1024,128]{1,0:T(8,128)(2,1)S(1)}, u32[]{:S(2)}, u32[]{:S(2)}) collective-permute-start(bf16[1024,128]{1,0:T(8,128)(2,1)S(1)} %get-tuple-element.41), channel_id=1, source_target_pairs={{0,3},{1,0},{2,1},{3,2},{4,7},{5,4},{6,5},{7,6},{8,11},{9,8},{10,9... | collective-permute-start | bytes 786440 | tf_op jit(solution)/shard_map/ppermute | solution.py:299
  108.7 27.6 %all-to-all-start.1 = ((bf16[64,32,128]{2,1,0:T(8,128)(2,1)}), bf16[64,32,128]{2,1,0:T(8,128)(2,1)S(1)}, u32[]{:S(2)}, u32[]{:S(2)}) async-start(bf16[64,32,128]{2,1,0:T(8,128)(2,1)} %bitcast.10), calls=%async_computation.1 | async-start | bytes 1048576 | tf_op jit(solution)/shard_map/all_to_all | solution.py:338
  119.0 5.9 %collective-permute-start.26 = (bf16[32,2048]{1,0:T(8,128)(2,1)S(1)}, bf16[32,2048]{1,0:T(8,128)(2,1)S(1)}, u32[]{:S(2)}, u32[]{:S(2)}) collective-permute-start(bf16[32,2048]{1,0:T(8,128)(2,1)S(1)} %get-tuple-element.50), channel_id=1, source_target_pairs={{0,64},{64,128},{128,192},{192,0},{1,65},{65,129},{129,193},{193,1... | collective-permute-start | bytes 393224 | tf_op jit(solution)/shard_map/ppermute | solution.py:299
  119.5 8.6 %collective-permute-start.27 = (bf16[32,2048]{1,0:T(8,128)(2,1)S(1)}, bf16[32,2048]{1,0:T(8,128)(2,1)S(1)}, u32[]{:S(2)}, u32[]{:S(2)}) collective-permute-start(bf16[32,2048]{1,0:T(8,128)(2,1)S(1)} %get-tuple-element.51), channel_id=1, source_target_pairs={{0,128},{64,192},{128,0},{192,64},{1,129},{65,193},{129,1},{193,65... | collective-permute-start | bytes 393224 | tf_op jit(solution)/shard_map/ppermute | solution.py:299
  122.1 6.0 %collective-permute-start.28 = (bf16[32,2048]{1,0:T(8,128)(2,1)S(1)}, bf16[32,2048]{1,0:T(8,128)(2,1)S(1)}, u32[]{:S(2)}, u32[]{:S(2)}) collective-permute-start(bf16[32,2048]{1,0:T(8,128)(2,1)S(1)} %get-tuple-element.52), channel_id=1, source_target_pairs={{0,192},{64,0},{128,64},{192,128},{1,193},{65,1},{129,65},{193,129... | collective-permute-start | bytes 393224 | tf_op jit(solution)/shard_map/ppermute | solution.py:299
  (1 other events, 12.1 us)

commit v3 on v2

--- a/solution.py
+++ b/solution.py
@@ -193,8 +193,8 @@
 
 def keep_kernel(q, *refs):
     pieces, b, received = refs[:8], refs[8], refs[9]
-    own, outs = refs[10], refs[11:14]
-    rest = refs[14:]
+    own, behind, ahead, upper, lower = refs[10:15]
+    rest = refs[15:]
     if q == 0:
         mask, rest = rest[0], rest[1:]
     a_full, tails, sems, other = rest
@@ -203,15 +203,17 @@
         rows = slice(part * (MQ // 4), (part + 1) * (MQ // 4))
         value = multiply(a_full, b, rows) + other[rows, :].astype(F32)
         own[rows, :] = value[:, 0:128]
-        for s in range(1, 4):
-            outs[s - 1][rows, :] = value[:, s * 128 : (s + 1) * 128].astype(BF)
+        ahead[rows, :] = value[:, 128:256]
+        behind[rows, :] = value[:, 384:512]
+        half = upper if part < 2 else lower
+        at = (part % 2) * (MQ // 4)
+        half[at : at + MQ // 4, :] = value[:, 256:384].astype(BF)
     if q == 0:
         mask[...] = mask_rows(tails) + other[MQ : MQ + TAIL, 0:128].astype(F32)
 
 
 def keep_half(q, pieces, b, received):
-    part = (MQ, 128)
-    shapes = [jax.ShapeDtypeStruct(part, F32)] + [jax.ShapeDtypeStruct(part, BF)] * 3
+    shapes = [jax.ShapeDtypeStruct((MQ, 128), F32)] * 3 + [jax.ShapeDtypeStruct((MQ // 2, 128), BF)] * 2
     if q == 0:
         shapes.append(jax.ShapeDtypeStruct((TAIL, 128), F32))
     return pl.pallas_call(
@@ -223,6 +225,25 @@
         compiler_params=params(),
         cost_estimate=cost(2 * MQ * 1024 * 512, MQ * 1024 * 2 + 2 * 1024 * 1024),
     )(*pieces, b, received)
+
+
+def relay_kernel(behind, ahead, upper, lower, behind_out, ahead_out):
+    half = MQ // 2
+    ahead_out[0:half, :] = (ahead[0:half, :] + upper[...].astype(F32)).astype(BF)
+    ahead_out[half:MQ, :] = ahead[half:MQ, :].astype(BF)
+    behind_out[0:half, :] = behind[0:half, :].astype(BF)
+    behind_out[half:MQ, :] = (behind[half:MQ, :] + lower[...].astype(F32)).astype(BF)
+
+
+def relay(behind, ahead, upper, lower):
+    return pl.pallas_call(
+        relay_kernel,
+        out_shape=[jax.ShapeDtypeStruct((MQ, 128), BF)] * 2,
+        in_specs=[WHOLE] * 4,
+        out_specs=[WHOLE] * 2,
+        compiler_params=params(),
+        cost_estimate=cost(MQ * 128 * 2, MQ * 128 * 14),
+    )(behind, ahead, upper, lower)
 
 
 def sum_kernel(*refs):
@@ -231,12 +252,11 @@
     size = MQ // 4
     for xb in range(4):
         for q in range(NQ):
-            own, first, second, third = parts[4 * q : 4 * q + 4]
+            own, first, second = parts[3 * q : 3 * q + 3]
             for j in range(4 // NQ):
                 at = xb * size + j * 128
                 rows = slice(at, at + 128)
-                value = own[rows, :] + first[rows, :].astype(F32)
-                value = value + second[rows, :].astype(F32) + third[rows, :].astype(F32)
+                value = own[rows, :] + first[rows, :].astype(F32) + second[rows, :].astype(F32)
                 block = q * (4 // NQ) + j
                 value = value * mask[xb * 4 + block : xb * 4 + block + 1, :]
                 out[4 * block : 4 * block + 4, xb] = value.astype(BF).reshape(4, 32, 128)
@@ -331,8 +351,10 @@
         received = lax.ppermute(other, "col", [(i, i ^ 1) for i in range(16)])
         kept = keep_half(q, pieces, kept_b, received)
         if q == 0:
-            mask = kept[4]
-        parts += [kept[0]] + [turn(kept[s], "layer", s) for s in (1, 2, 3)]
+            mask = kept[5]
+        own_part, back, front, upper, lower = kept[:5]
+        back, front = relay(back, front, turn(upper, "layer", 1), turn(lower, "layer", -1))
+        parts += [own_part, turn(front, "layer", 1), turn(back, "layer", -1)]
 
     product, *flips = sum_parts(mask, parts)
     own = lax.all_to_all(product.reshape(64, 32, 128), ("col", "layer"), 0, 0)

time: 138 us -> 134 us (0.971)
  waiting for transfers between devices: 60 us -> 50.7 us
  starting transfers between devices: 61.5 us -> 66.6 us
    ppermute x13 -> x15, waiting for transfers between devices: 22.1 us -> 12.8 us  [turn(): return lax.ppermute(value, axis, [(i, (i + shift) % 4) for i in range(4)])]
    ppermute x13 -> x15, starting transfers between devices: 17 us -> 20.5 us  [turn(): return lax.ppermute(value, axis, [(i, (i + shift) % 4) for i in range(4)])]
    all_to_all x1, starting transfers between devices: 10.3 us -> 11.9 us  [per_device(): own = lax.all_to_all(product.reshape(64, 32, 128), ('col', 'layer'), 0, 0)]
  transfers between devices with their start and end apart: 31 -> 33, of which waited for: 16 -> 15; matrix products, arithmetic and copies ran while one was open for 0% -> 0% of each run, Pallas kernels for 7% -> 7%
where the time goes in v3:
time: 134 us
  starting transfers between devices  66.6 us (50%)
  waiting for transfers between devices  50.7 us (38%)
  Pallas kernels  16.1 us (12%)
    ppermute x14, waiting for transfers between devices, turn_z(): return lax.ppermute(value, 'col', pairs)  29.7 us
    ppermute x15, starting transfers between devices, turn(): return lax.ppermute(value, axis, [(i, (i + shift) % 4) for i in range(4)])  20.5 us
    ppermute x14, starting transfers between devices, turn_z(): return lax.ppermute(value, 'col', pairs)  17.9 us
    ppermute x15, waiting for transfers between devices, turn(): return lax.ppermute(value, axis, [(i, (i + shift) % 4) for i in range(4)])  12.8 us
    all_to_all x1, starting transfers between devices, per_device(): own = lax.all_to_all(product.reshape(64, 32, 128), ('col', 'layer'), 0, 0)  11.9 us
    all_to_all x1, starting transfers between devices, per_device(): b_own = lax.all_to_all(b_send, 'col', 0, 0)  9.99 us
    all_to_all x1, waiting for transfers between devices, per_device(): own = lax.all_to_all(product.reshape(64, 32, 128), ('col', 'layer'), 0, 0)  8.2 us
    ppermute x2, starting transfers between devices, per_device(): received = lax.ppermute(other, 'col', [(i, i ^ 1) for i in range(16)])  6.26 us
  transfers between devices with their start and end apart: 33, of which 15 were waited for; matrix products, arithmetic and copies ran while one was open for 0% of the time, Pallas kernels for 7%

profile of v3, /device:TPU:1, one launch (start us, length us, event | category | flops | bytes accessed | tf_op | source)
XLA Modules:
  0.0 133.6 jit_solution(9245703125120886596)
XLA Ops:
  0.0 2.0 %shard_map.55 = (bf16[1040,128]{1,0:T(8,128)(2,1)}, bf16[1024,128]{1,0:T(8,128)(2,1)}) custom-call(s32[1,16]{1,0:T(1,128)} %bitcast.21, bf16[2048,128]{1,0:T(8,128)(2,1)} %bitcast.17, s32[4,16]{1,0:T(4,128)} %bitcast.19), custom_call_target="tpu_custom_call" | custom-call | flops 262144 | bytes 1048576 | tf_op jit(solution)/shard_map/pallas_call | solution.py:63
  2.0 2.1 %shard_map.56 = bf16[16,64,256]{2,1,0:T(8,128)(2,1)} custom-call(s32[4,4]{1,0:T(4,128)} %bitcast.20, bf16[512,512]{1,0:T(8,128)(2,1)} %bitcast.18), custom_call_target="tpu_custom_call" | custom-call | flops 262144 | bytes 1048576 | tf_op jit(solution)/shard_map/pallas_call | solution.py:93
  4.1 10.0 %all-to-all-start = ((bf16[16,64,256]{2,1,0:T(8,128)(2,1)}), bf16[16,64,256]{2,1,0:T(8,128)(2,1)S(1)}, u32[]{:S(2)}, u32[]{:S(2)}) async-start(bf16[16,64,256]{2,1,0:T(8,128)(2,1)} %shard_map.56), calls=%async_computation | async-start | bytes 1048576 | tf_op jit(solution)/shard_map/all_to_all | solution.py:327
  14.1 1.5 %collective-permute-start.7 = (bf16[1024,128]{1,0:T(8,128)(2,1)S(1)}, bf16[1024,128]{1,0:T(8,128)(2,1)S(1)}, u32[]{:S(2)}, u32[]{:S(2)}) collective-permute-start(bf16[1024,128]{1,0:T(8,128)(2,1)S(1)} %copy-done.1), channel_id=1, source_target_pairs={{0,8},{4,12},{8,16},{12,20},{16,24},{20,28},{24,32},{28,36},{32,40... | collective-permute-start | bytes 786440 | tf_op jit(solution)/shard_map/ppermute | solution.py:315
  17.1 17.5 %collective-permute-done.7.refs_1_ = bf16[1024,128]{1,0:T(8,128)(2,1)S(1)} collective-permute-done((bf16[1024,128]{1,0:T(8,128)(2,1)S(1)}, bf16[1024,128]{1,0:T(8,128)(2,1)S(1)}, u32[]{:S(2)}, u32[]{:S(2)}) %collective-permute-start.7) | collective-permute-done | bytes 262176 | tf_op jit(solution)/shard_map/ppermute | solution.py:315
  35.8 1.5 %collective-permute-start.10 = (bf16[16,64,256]{2,1,0:T(8,128)(2,1)S(1)}, bf16[16,64,256]{2,1,0:T(8,128)(2,1)S(1)}, u32[]{:S(2)}, u32[]{:S(2)}) collective-permute-start(bf16[16,64,256]{2,1,0:T(8,128)(2,1)S(1)} %all-to-all-done), channel_id=1, source_target_pairs={{0,192},{64,0},{128,64},{192,128},{1,193},{65,1},{129,65},{193,129... | collective-permute-start | bytes 1572872 | tf_op jit(solution)/shard_map/ppermute | solution.py:319
  38.6 1.7 %collective-permute-done.refs_1_ = bf16[1040,128]{1,0:T(8,128)(2,1)S(1)} collective-permute-done((bf16[1040,128]{1,0:T(8,128)(2,1)S(1)}, bf16[1040,128]{1,0:T(8,128)(2,1)S(1)}, u32[]{:S(2)}, u32[]{:S(2)}) %collective-permute-start) | collective-permute-done | bytes 266272 | tf_op jit(solution)/shard_map/ppermute | solution.py:315
  40.3 2.7 %collective-permute-start.20 = (bf16[1024,128]{1,0:T(8,128)(2,1)S(1)}, bf16[1024,128]{1,0:T(8,128)(2,1)S(1)}, u32[]{:S(2)}, u32[]{:S(2)}) collective-permute-start(bf16[1024,128]{1,0:T(8,128)(2,1)S(1)} %collective-permute-done.8.refs_7_), channel_id=1, source_target_pairs={{0,56},{4,60},{8,0},{12,4},{16,8},{20,12},{24,16},{28,20},{32,24},... | collective-permute-start | bytes 786440 | tf_op jit(solution)/shard_map/ppermute | solution.py:315
  43.5 2.4 %collective-permute-start.5 = (bf16[1040,128]{1,0:T(8,128)(2,1)S(1)}, bf16[1040,128]{1,0:T(8,128)(2,1)S(1)}, u32[]{:S(2)}, u32[]{:S(2)}) collective-permute-start(bf16[1040,128]{1,0:T(8,128)(2,1)S(1)} %collective-permute-done.4.refs_7_), channel_id=1, source_target_pairs={{0,56},{4,60},{8,0},{12,4},{16,8},{20,12},{24,16},{28,20},{32,24},... | collective-permute-start | bytes 798728 | tf_op jit(solution)/shard_map/ppermute | solution.py:315
  45.9 2.6 %collective-permute-done.1.refs_2_ = bf16[1040,128]{1,0:T(8,128)(2,1)S(1)} collective-permute-done((bf16[1040,128]{1,0:T(8,128)(2,1)S(1)}, bf16[1040,128]{1,0:T(8,128)(2,1)S(1)}, u32[]{:S(2)}, u32[]{:S(2)}) %collective-permute-start.1) | collective-permute-done | bytes 266272 | tf_op jit(solution)/shard_map/ppermute | solution.py:315
  49.1 3.4 %collective-permute-start.21 = (bf16[1024,128]{1,0:T(8,128)(2,1)S(1)}, bf16[1024,128]{1,0:T(8,128)(2,1)S(1)}, u32[]{:S(2)}, u32[]{:S(2)}) collective-permute-start(bf16[1024,128]{1,0:T(8,128)(2,1)S(1)} %collective-permute-done.20.refs_6_), channel_id=1, source_target_pairs={{0,56},{4,60},{8,0},{12,4},{16,8},{20,12},{24,16},{28,20},{32,24},... | collective-permute-start | bytes 786440 | tf_op jit(solution)/shard_map/ppermute | solution.py:315
  52.7 2.1 %collective-permute-done.5.refs_6_ = bf16[1040,128]{1,0:T(8,128)(2,1)S(1)} collective-permute-done((bf16[1040,128]{1,0:T(8,128)(2,1)S(1)}, bf16[1040,128]{1,0:T(8,128)(2,1)S(1)}, u32[]{:S(2)}, u32[]{:S(2)}) %collective-permute-start.5) | collective-permute-done | bytes 266272 | tf_op jit(solution)/shard_map/ppermute | solution.py:315
  54.8 2.3 %collective-permute-start.12 = (bf16[8,64,256]{2,1,0:T(8,128)(2,1)S(1)}, bf16[8,64,256]{2,1,0:T(8,128)(2,1)S(1)}, u32[]{:S(2)}, u32[]{:S(2)}) collective-permute-start(bf16[8,64,256]{2,1,0:T(8,128)(2,1)S(1)} %slice.9), channel_id=1, source_target_pairs={{0,192},{64,0},{128,64},{192,128},{1,193},{65,1},{129,65},{193,129... | collective-permute-start | bytes 786440 | tf_op jit(solution)/shard_map/ppermute | solution.py:319
  57.6 2.9 %collective-permute-done.21.refs_5_ = bf16[1024,128]{1,0:T(8,128)(2,1)S(1)} collective-permute-done((bf16[1024,128]{1,0:T(8,128)(2,1)S(1)}, bf16[1024,128]{1,0:T(8,128)(2,1)S(1)}, u32[]{:S(2)}, u32[]{:S(2)}) %collective-permute-start.21) | collective-permute-done | bytes 262176 | tf_op jit(solution)/shard_map/ppermute | solution.py:315
  60.4 3.4 %collective-permute-start.22 = (bf16[1024,128]{1,0:T(8,128)(2,1)S(1)}, bf16[1024,128]{1,0:T(8,128)(2,1)S(1)}, u32[]{:S(2)}, u32[]{:S(2)}) collective-permute-start(bf16[1024,128]{1,0:T(8,128)(2,1)S(1)} %collective-permute-done.21.refs_5_), channel_id=1, source_target_pairs={{0,56},{4,60},{8,0},{12,4},{16,8},{20,12},{24,16},{28,20},{32,24},... | collective-permute-start | bytes 786440 | tf_op jit(solution)/shard_map/ppermute | solution.py:315
  63.9 1.4 %collective-permute-start.3 = (bf16[1040,128]{1,0:T(8,128)(2,1)S(1)}, bf16[1040,128]{1,0:T(8,128)(2,1)S(1)}, u32[]{:S(2)}, u32[]{:S(2)}) collective-permute-start(bf16[1040,128]{1,0:T(8,128)(2,1)S(1)} %collective-permute-done.2.refs_3_), channel_id=1, source_target_pairs={{0,8},{4,12},{8,16},{12,20},{16,24},{20,28},{24,32},{28,36},{32,40... | collective-permute-start | bytes 798728 | tf_op jit(solution)/shard_map/ppermute | solution.py:315
  67.8 2.1 %shard_map.61 = bf16[1024,512]{1,0:T(8,128)(2,1)S(1)} custom-call(bf16[1024,128]{1,0:T(8,128)(2,1)S(1)} %copy-done.1, bf16[1024,128]{1,0:T(8,128)(2,1)S(1)} %collective-permute-done.7.refs_1_, bf16[1024,128]{1,0:T(8,128)(2,1)S(1)} %collective-permute-done.18.refs_2_, bf16[1024,128]{1,0:T(8,128)(2,1)S(1)} %collective-permute-done.19.refs_3_, ...), custom_call_target="tpu_custom_call" | custom-call | flops 1073741824 | bytes 3145728 | tf_op jit(solution)/shard_map/pallas_call | solution.py:183
  69.9 4.9 %collective-permute-start.23 = (bf16[1024,512]{1,0:T(8,128)(2,1)S(1)}, bf16[1024,512]{1,0:T(8,128)(2,1)S(1)}, u32[]{:S(2)}, u32[]{:S(2)}) collective-permute-start(bf16[1024,512]{1,0:T(8,128)(2,1)S(1)} %shard_map.61), channel_id=1, source_target_pairs={{0,4},{4,0},{8,12},{12,8},{16,20},{20,16},{24,28},{28,24},{32,36},... | collective-permute-start | bytes 3145736 | tf_op jit(solution)/shard_map/ppermute | solution.py:351
  74.8 2.2 %shard_map.58 = bf16[1040,512]{1,0:T(8,128)(2,1)S(1)} custom-call(bf16[1040,128]{1,0:T(8,128)(2,1)S(1)} %copy-done, bf16[1040,128]{1,0:T(8,128)(2,1)S(1)} %collective-permute-done.refs_1_, bf16[1040,128]{1,0:T(8,128)(2,1)S(1)} %collective-permute-done.1.refs_2_, bf16[1040,128]{1,0:T(8,128)(2,1)S(1)} %collective-permute-done.2.refs_3_, ...), custom_call_target="tpu_custom_call" | custom-call | flops 1073741824 | bytes 3145728 | tf_op jit(solution)/shard_map/pallas_call | solution.py:183
  78.3 2.2 %shard_map.62 = (f32[1024,128]{1,0:T(8,128)S(1)}, f32[1024,128]{1,0:T(8,128)S(1)}, f32[1024,128]{1,0:T(8,128)S(1)}, bf16[512,128]{1,0:T(8,128)(2,1)S(1)}, bf16[512,128]{1,0:T(8,128)(2,1)S(1)}) custom-call(bf16[1024,128]{1,0:T(8,128)(2,1)S(1)} %copy-done.1, bf16[1024,128]{1,0:T(8,128)(2,1)S(1)} %collective-permute-done.7.refs_1_, ...), custom_call_target="tpu_custom_call" | custom-call | flops 1073741824 | bytes 4194304 | tf_op jit(solution)/shard_map/pallas_call | solution.py:219
  81.8 1.5 %collective-permute-start.25 = (bf16[512,128]{1,0:T(8,128)(2,1)S(1)}, bf16[512,128]{1,0:T(8,128)(2,1)S(1)}, u32[]{:S(2)}, u32[]{:S(2)}) collective-permute-start(bf16[512,128]{1,0:T(8,128)(2,1)S(1)} %get-tuple-element.57), channel_id=1, source_target_pairs={{0,3},{1,0},{2,1},{3,2},{4,7},{5,4},{6,5},{7,6},{8,11},{9,8},{10,9... | collective-permute-start | bytes 393224 | tf_op jit(solution)/shard_map/ppermute | solution.py:319
  83.3 2.2 %shard_map.59 = (f32[1024,128]{1,0:T(8,128)S(1)}, f32[1024,128]{1,0:T(8,128)S(1)}, f32[1024,128]{1,0:T(8,128)S(1)}, bf16[512,128]{1,0:T(8,128)(2,1)S(1)}, bf16[5...) custom-call(bf16[1040,128]{1,0:T(8,128)(2,1)S(1)} %copy-done, bf16[1040,128]{1,0:T(8,128)(2,1)S(1)} %collective-permute-done.refs_1_, ...), custom_call_target="tpu_custom_call" | custom-call | flops 1073741824 | bytes 4194304 | tf_op jit(solution)/shard_map/pallas_call | solution.py:219
  85.8 2.7 %collective-permute-start.15 = (bf16[512,128]{1,0:T(8,128)(2,1)S(1)}, bf16[512,128]{1,0:T(8,128)(2,1)S(1)}, u32[]{:S(2)}, u32[]{:S(2)}) collective-permute-start(bf16[512,128]{1,0:T(8,128)(2,1)S(1)} %get-tuple-element.48), channel_id=1, source_target_pairs={{0,3},{1,0},{2,1},{3,2},{4,7},{5,4},{6,5},{7,6},{8,11},{9,8},{10,9... | collective-permute-start | bytes 393224 | tf_op jit(solution)/shard_map/ppermute | solution.py:319
  88.7 2.7 %collective-permute-start.27 = (bf16[1024,128]{1,0:T(8,128)(2,1)S(1)}, bf16[1024,128]{1,0:T(8,128)(2,1)S(1)}, u32[]{:S(2)}, u32[]{:S(2)}) collective-permute-start(bf16[1024,128]{1,0:T(8,128)(2,1)S(1)} %get-tuple-element.59), channel_id=1, source_target_pairs={{0,3},{1,0},{2,1},{3,2},{4,7},{5,4},{6,5},{7,6},{8,11},{9,8},{10,9... | collective-permute-start | bytes 786440 | tf_op jit(solution)/shard_map/ppermute | solution.py:319
  91.6 2.7 %collective-permute-start.17 = (bf16[1024,128]{1,0:T(8,128)(2,1)S(1)}, bf16[1024,128]{1,0:T(8,128)(2,1)S(1)}, u32[]{:S(2)}, u32[]{:S(2)}) collective-permute-start(bf16[1024,128]{1,0:T(8,128)(2,1)S(1)} %get-tuple-element.50), channel_id=1, source_target_pairs={{0,3},{1,0},{2,1},{3,2},{4,7},{5,4},{6,5},{7,6},{8,11},{9,8},{10,9... | collective-permute-start | bytes 786440 | tf_op jit(solution)/shard_map/ppermute | solution.py:319
  94.3 2.2 %collective-permute-done.26.refs_5_ = bf16[1024,128]{1,0:T(8,128)(2,1)S(1)} collective-permute-done((bf16[1024,128]{1,0:T(8,128)(2,1)S(1)}, bf16[1024,128]{1,0:T(8,128)(2,1)S(1)}, u32[]{:S(2)}, u32[]{:S(2)}) %collective-permute-start.26) | collective-permute-done | bytes 262176 | tf_op jit(solution)/shard_map/ppermute | solution.py:319
  96.5 5.6 %collective-permute-done.16.refs_2_ = bf16[1024,128]{1,0:T(8,128)(2,1)S(1)} collective-permute-done((bf16[1024,128]{1,0:T(8,128)(2,1)S(1)}, bf16[1024,128]{1,0:T(8,128)(2,1)S(1)}, u32[]{:S(2)}, u32[]{:S(2)}) %collective-permute-start.16) | collective-permute-done | bytes 262176 | tf_op jit(solution)/shard_map/ppermute | solution.py:319
  103.2 11.9 %all-to-all-start.1 = ((bf16[64,32,128]{2,1,0:T(8,128)(2,1)}), bf16[64,32,128]{2,1,0:T(8,128)(2,1)S(1)}, u32[]{:S(2)}, u32[]{:S(2)}) async-start(bf16[64,32,128]{2,1,0:T(8,128)(2,1)} %bitcast.10), calls=%async_computation.1 | async-start | bytes 1048576 | tf_op jit(solution)/shard_map/all_to_all | solution.py:360
  115.5 2.6 %collective-permute-start.29 = (bf16[32,2048]{1,0:T(8,128)(2,1)S(1)}, bf16[32,2048]{1,0:T(8,128)(2,1)S(1)}, u32[]{:S(2)}, u32[]{:S(2)}) collective-permute-start(bf16[32,2048]{1,0:T(8,128)(2,1)S(1)} %get-tuple-element.63), channel_id=1, source_target_pairs={{0,128},{64,192},{128,0},{192,64},{1,129},{65,193},{129,1},{193,65... | collective-permute-start | bytes 393224 | tf_op jit(solution)/shard_map/ppermute | solution.py:319
  119.2 1.7 %collective-permute-done.28.refs_1_ = bf16[32,2048]{1,0:T(8,128)(2,1)S(1)} collective-permute-done((bf16[32,2048]{1,0:T(8,128)(2,1)S(1)}, bf16[32,2048]{1,0:T(8,128)(2,1)S(1)}, u32[]{:S(2)}, u32[]{:S(2)}) %collective-permute-start.28) | collective-permute-done | bytes 131104 | tf_op jit(solution)/shard_map/ppermute | solution.py:319
  121.0 3.1 %collective-permute-done.29.refs_2_ = bf16[32,2048]{1,0:T(8,128)(2,1)S(1)} collective-permute-done((bf16[32,2048]{1,0:T(8,128)(2,1)S(1)}, bf16[32,2048]{1,0:T(8,128)(2,1)S(1)}, u32[]{:S(2)}, u32[]{:S(2)}) %collective-permute-start.29) | collective-permute-done | bytes 131104 | tf_op jit(solution)/shard_map/ppermute | solution.py:319
  124.1 8.2 %all-to-all-done.1.own = bf16[64,32,128]{2,1,0:T(8,128)(2,1)S(1)} async-done(((bf16[64,32,128]{2,1,0:T(8,128)(2,1)}), bf16[64,32,128]{2,1,0:T(8,128)(2,1)S(1)}, u32[]{:S(2)}, u32[]{:S(2)}) %all-to-all-start.1) | async-done | bytes 524320 | tf_op jit(solution)/shard_map/all_to_all | solution.py:360
  (51 shorter events, 15.7 us)
Async XLA Ops:
  4.1 30.4 %all-to-all-start = ((bf16[16,64,256]{2,1,0:T(8,128)(2,1)}), bf16[16,64,256]{2,1,0:T(8,128)(2,1)S(1)}, u32[]{:S(2)}, u32[]{:S(2)}) async-start(bf16[16,64,256]{2,1,0:T(8,128)(2,1)} %shard_map.56), calls=%async_computation | async-start | bytes 1048576 | tf_op jit(solution)/shard_map/all_to_all | solution.py:327
  14.1 20.4 %collective-permute-start.7 = (bf16[1024,128]{1,0:T(8,128)(2,1)S(1)}, bf16[1024,128]{1,0:T(8,128)(2,1)S(1)}, u32[]{:S(2)}, u32[]{:S(2)}) collective-permute-start(bf16[1024,128]{1,0:T(8,128)(2,1)S(1)} %copy-done.1), channel_id=1, source_target_pairs={{0,8},{4,12},{8,16},{12,20},{16,24},{20,28},{24,32},{28,36},{32,40... | collective-permute-start | bytes 786440 | tf_op jit(solution)/shard_map/ppermute | solution.py:315
  15.6 19.0 %collective-permute-start.8 = (bf16[1024,128]{1,0:T(8,128)(2,1)S(1)}, bf16[1024,128]{1,0:T(8,128)(2,1)S(1)}, u32[]{:S(2)}, u32[]{:S(2)}) collective-permute-start(bf16[1024,128]{1,0:T(8,128)(2,1)S(1)} %copy-done.1), channel_id=1, source_target_pairs={{0,56},{4,60},{8,0},{12,4},{16,8},{20,12},{24,16},{28,20},{32,24},... | collective-permute-start | bytes 786440 | tf_op jit(solution)/shard_map/ppermute | solution.py:315
  16.9 23.3 %collective-permute-start = (bf16[1040,128]{1,0:T(8,128)(2,1)S(1)}, bf16[1040,128]{1,0:T(8,128)(2,1)S(1)}, u32[]{:S(2)}, u32[]{:S(2)}) collective-permute-start(bf16[1040,128]{1,0:T(8,128)(2,1)S(1)} %copy-done), channel_id=1, source_target_pairs={{0,8},{4,12},{8,16},{12,20},{16,24},{20,28},{24,32},{28,36},{32,40... | collective-permute-start | bytes 798728 | tf_op jit(solution)/shard_map/ppermute | solution.py:315
  34.5 18.0 %collective-permute-start.9 = (bf16[16,64,256]{2,1,0:T(8,128)(2,1)S(1)}, bf16[16,64,256]{2,1,0:T(8,128)(2,1)S(1)}, u32[]{:S(2)}, u32[]{:S(2)}) collective-permute-start(bf16[16,64,256]{2,1,0:T(8,128)(2,1)S(1)} %all-to-all-done), channel_id=1, source_target_pairs={{0,64},{64,128},{128,192},{192,0},{1,65},{65,129},{129,193},{193,1... | collective-permute-start | bytes 1572872 | tf_op jit(solution)/shard_map/ppermute | solution.py:319
  35.8 16.7 %collective-permute-start.10 = (bf16[16,64,256]{2,1,0:T(8,128)(2,1)S(1)}, bf16[16,64,256]{2,1,0:T(8,128)(2,1)S(1)}, u32[]{:S(2)}, u32[]{:S(2)}) collective-permute-start(bf16[16,64,256]{2,1,0:T(8,128)(2,1)S(1)} %all-to-all-done), channel_id=1, source_target_pairs={{0,192},{64,0},{128,64},{192,128},{1,193},{65,1},{129,65},{193,129... | collective-permute-start | bytes 1572872 | tf_op jit(solution)/shard_map/ppermute | solution.py:319
  37.4 6.1 %collective-permute-start.4 = (bf16[1040,128]{1,0:T(8,128)(2,1)S(1)}, bf16[1040,128]{1,0:T(8,128)(2,1)S(1)}, u32[]{:S(2)}, u32[]{:S(2)}) collective-permute-start(bf16[1040,128]{1,0:T(8,128)(2,1)S(1)} %copy-done), channel_id=1, source_target_pairs={{0,56},{4,60},{8,0},{12,4},{16,8},{20,12},{24,16},{28,20},{32,24},... | collective-permute-start | bytes 798728 | tf_op jit(solution)/shard_map/ppermute | solution.py:315
  40.2 8.2 %collective-permute-start.1 = (bf16[1040,128]{1,0:T(8,128)(2,1)S(1)}, bf16[1040,128]{1,0:T(8,128)(2,1)S(1)}, u32[]{:S(2)}, u32[]{:S(2)}) collective-permute-start(bf16[1040,128]{1,0:T(8,128)(2,1)S(1)} %collective-permute-done.refs_1_), channel_id=1, source_target_pairs={{0,8},{4,12},{8,16},{12,20},{16,24},{20,28},{24,32},{28,36},{32,40... | collective-permute-start | bytes 798728 | tf_op jit(solution)/shard_map/ppermute | solution.py:315
  40.3 8.9 %collective-permute-start.20 = (bf16[1024,128]{1,0:T(8,128)(2,1)S(1)}, bf16[1024,128]{1,0:T(8,128)(2,1)S(1)}, u32[]{:S(2)}, u32[]{:S(2)}) collective-permute-start(bf16[1024,128]{1,0:T(8,128)(2,1)S(1)} %collective-permute-done.8.refs_7_), channel_id=1, source_target_pairs={{0,56},{4,60},{8,0},{12,4},{16,8},{20,12},{24,16},{28,20},{32,24},... | collective-permute-start | bytes 786440 | tf_op jit(solution)/shard_map/ppermute | solution.py:315
  43.5 11.3 %collective-permute-start.5 = (bf16[1040,128]{1,0:T(8,128)(2,1)S(1)}, bf16[1040,128]{1,0:T(8,128)(2,1)S(1)}, u32[]{:S(2)}, u32[]{:S(2)}) collective-permute-start(bf16[1040,128]{1,0:T(8,128)(2,1)S(1)} %collective-permute-done.4.refs_7_), channel_id=1, source_target_pairs={{0,56},{4,60},{8,0},{12,4},{16,8},{20,12},{24,16},{28,20},{32,24},... | collective-permute-start | bytes 798728 | tf_op jit(solution)/shard_map/ppermute | solution.py:315
  48.5 8.6 %collective-permute-start.18 = (bf16[1024,128]{1,0:T(8,128)(2,1)S(1)}, bf16[1024,128]{1,0:T(8,128)(2,1)S(1)}, u32[]{:S(2)}, u32[]{:S(2)}) collective-permute-start(bf16[1024,128]{1,0:T(8,128)(2,1)S(1)} %collective-permute-done.7.refs_1_), channel_id=1, source_target_pairs={{0,8},{4,12},{8,16},{12,20},{16,24},{20,28},{24,32},{28,36},{32,40... | collective-permute-start | bytes 786440 | tf_op jit(solution)/shard_map/ppermute | solution.py:315
  49.1 11.3 %collective-permute-start.21 = (bf16[1024,128]{1,0:T(8,128)(2,1)S(1)}, bf16[1024,128]{1,0:T(8,128)(2,1)S(1)}, u32[]{:S(2)}, u32[]{:S(2)}) collective-permute-start(bf16[1024,128]{1,0:T(8,128)(2,1)S(1)} %collective-permute-done.20.refs_6_), channel_id=1, source_target_pairs={{0,56},{4,60},{8,0},{12,4},{16,8},{20,12},{24,16},{28,20},{32,24},... | collective-permute-start | bytes 786440 | tf_op jit(solution)/shard_map/ppermute | solution.py:315
  52.5 11.3 %collective-permute-start.2 = (bf16[1040,128]{1,0:T(8,128)(2,1)S(1)}, bf16[1040,128]{1,0:T(8,128)(2,1)S(1)}, u32[]{:S(2)}, u32[]{:S(2)}) collective-permute-start(bf16[1040,128]{1,0:T(8,128)(2,1)S(1)} %collective-permute-done.1.refs_2_), channel_id=1, source_target_pairs={{0,8},{4,12},{8,16},{12,20},{16,24},{20,28},{24,32},{28,36},{32,40... | collective-permute-start | bytes 798728 | tf_op jit(solution)/shard_map/ppermute | solution.py:315
  52.6 11.3 %collective-permute-start.11 = (bf16[8,64,256]{2,1,0:T(8,128)(2,1)S(1)}, bf16[8,64,256]{2,1,0:T(8,128)(2,1)S(1)}, u32[]{:S(2)}, u32[]{:S(2)}) collective-permute-start(bf16[8,64,256]{2,1,0:T(8,128)(2,1)S(1)} %slice.8), channel_id=1, source_target_pairs={{0,64},{64,128},{128,192},{192,0},{1,65},{65,129},{129,193},{193,1... | collective-permute-start | bytes 786440 | tf_op jit(solution)/shard_map/ppermute | solution.py:319
  54.8 10.5 %collective-permute-start.12 = (bf16[8,64,256]{2,1,0:T(8,128)(2,1)S(1)}, bf16[8,64,256]{2,1,0:T(8,128)(2,1)S(1)}, u32[]{:S(2)}, u32[]{:S(2)}) collective-permute-start(bf16[8,64,256]{2,1,0:T(8,128)(2,1)S(1)} %slice.9), channel_id=1, source_target_pairs={{0,192},{64,0},{128,64},{192,128},{1,193},{65,1},{129,65},{193,129... | collective-permute-start | bytes 786440 | tf_op jit(solution)/shard_map/ppermute | solution.py:319
  57.1 10.1 %collective-permute-start.19 = (bf16[1024,128]{1,0:T(8,128)(2,1)S(1)}, bf16[1024,128]{1,0:T(8,128)(2,1)S(1)}, u32[]{:S(2)}, u32[]{:S(2)}) collective-permute-start(bf16[1024,128]{1,0:T(8,128)(2,1)S(1)} %collective-permute-done.18.refs_2_), channel_id=1, source_target_pairs={{0,8},{4,12},{8,16},{12,20},{16,24},{20,28},{24,32},{28,36},{32,40... | collective-permute-start | bytes 786440 | tf_op jit(solution)/shard_map/ppermute | solution.py:315
  60.4 7.3 %collective-permute-start.22 = (bf16[1024,128]{1,0:T(8,128)(2,1)S(1)}, bf16[1024,128]{1,0:T(8,128)(2,1)S(1)}, u32[]{:S(2)}, u32[]{:S(2)}) collective-permute-start(bf16[1024,128]{1,0:T(8,128)(2,1)S(1)} %collective-permute-done.21.refs_5_), channel_id=1, source_target_pairs={{0,56},{4,60},{8,0},{12,4},{16,8},{20,12},{24,16},{28,20},{32,24},... | collective-permute-start | bytes 786440 | tf_op jit(solution)/shard_map/ppermute | solution.py:315
  63.9 10.9 %collective-permute-start.6 = (bf16[1040,128]{1,0:T(8,128)(2,1)S(1)}, bf16[1040,128]{1,0:T(8,128)(2,1)S(1)}, u32[]{:S(2)}, u32[]{:S(2)}) collective-permute-start(bf16[1040,128]{1,0:T(8,128)(2,1)S(1)} %collective-permute-done.5.refs_6_), channel_id=1, source_target_pairs={{0,56},{4,60},{8,0},{12,4},{16,8},{20,12},{24,16},{28,20},{32,24},... | collective-permute-start | bytes 798728 | tf_op jit(solution)/shard_map/ppermute | solution.py:315
  63.9 10.9 %collective-permute-start.3 = (bf16[1040,128]{1,0:T(8,128)(2,1)S(1)}, bf16[1040,128]{1,0:T(8,128)(2,1)S(1)}, u32[]{:S(2)}, u32[]{:S(2)}) collective-permute-start(bf16[1040,128]{1,0:T(8,128)(2,1)S(1)} %collective-permute-done.2.refs_3_), channel_id=1, source_target_pairs={{0,8},{4,12},{8,16},{12,20},{16,24},{20,28},{24,32},{28,36},{32,40... | collective-permute-start | bytes 798728 | tf_op jit(solution)/shard_map/ppermute | solution.py:315
  69.9 8.4 %collective-permute-start.23 = (bf16[1024,512]{1,0:T(8,128)(2,1)S(1)}, bf16[1024,512]{1,0:T(8,128)(2,1)S(1)}, u32[]{:S(2)}, u32[]{:S(2)}) collective-permute-start(bf16[1024,512]{1,0:T(8,128)(2,1)S(1)} %shard_map.61), channel_id=1, source_target_pairs={{0,4},{4,0},{8,12},{12,8},{16,20},{20,16},{24,28},{28,24},{32,36},... | collective-permute-start | bytes 3145736 | tf_op jit(solution)/shard_map/ppermute | solution.py:351
  76.9 6.3 %collective-permute-start.13 = (bf16[1040,512]{1,0:T(8,128)(2,1)S(1)}, bf16[1040,512]{1,0:T(8,128)(2,1)S(1)}, u32[]{:S(2)}, u32[]{:S(2)}) collective-permute-start(bf16[1040,512]{1,0:T(8,128)(2,1)S(1)} %shard_map.58), channel_id=1, source_target_pairs={{0,4},{4,0},{8,12},{12,8},{16,20},{20,16},{24,28},{28,24},{32,36},... | collective-permute-start | bytes 3194888 | tf_op jit(solution)/shard_map/ppermute | solution.py:351
  80.5 8.0 %collective-permute-start.24 = (bf16[512,128]{1,0:T(8,128)(2,1)S(1)}, bf16[512,128]{1,0:T(8,128)(2,1)S(1)}, u32[]{:S(2)}, u32[]{:S(2)}) collective-permute-start(bf16[512,128]{1,0:T(8,128)(2,1)S(1)} %get-tuple-element.56), channel_id=1, source_target_pairs={{0,1},{1,2},{2,3},{3,0},{4,5},{5,6},{6,7},{7,4},{8,9},{9,10},{10,1... | collective-permute-start | bytes 393224 | tf_op jit(solution)/shard_map/ppermute | solution.py:319
  81.8 6.7 %collective-permute-start.25 = (bf16[512,128]{1,0:T(8,128)(2,1)S(1)}, bf16[512,128]{1,0:T(8,128)(2,1)S(1)}, u32[]{:S(2)}, u32[]{:S(2)}) collective-permute-start(bf16[512,128]{1,0:T(8,128)(2,1)S(1)} %get-tuple-element.57), channel_id=1, source_target_pairs={{0,3},{1,0},{2,1},{3,2},{4,7},{5,4},{6,5},{7,6},{8,11},{9,8},{10,9... | collective-permute-start | bytes 393224 | tf_op jit(solution)/shard_map/ppermute | solution.py:319
  85.5 5.9 %collective-permute-start.14 = (bf16[512,128]{1,0:T(8,128)(2,1)S(1)}, bf16[512,128]{1,0:T(8,128)(2,1)S(1)}, u32[]{:S(2)}, u32[]{:S(2)}) collective-permute-start(bf16[512,128]{1,0:T(8,128)(2,1)S(1)} %get-tuple-element.47), channel_id=1, source_target_pairs={{0,1},{1,2},{2,3},{3,0},{4,5},{5,6},{6,7},{7,4},{8,9},{9,10},{10,1... | collective-permute-start | bytes 393224 | tf_op jit(solution)/shard_map/ppermute | solution.py:319
  88.6 7.9 %collective-permute-start.26 = (bf16[1024,128]{1,0:T(8,128)(2,1)S(1)}, bf16[1024,128]{1,0:T(8,128)(2,1)S(1)}, u32[]{:S(2)}, u32[]{:S(2)}) collective-permute-start(bf16[1024,128]{1,0:T(8,128)(2,1)S(1)} %get-tuple-element.58), channel_id=1, source_target_pairs={{0,1},{1,2},{2,3},{3,0},{4,5},{5,6},{6,7},{7,4},{8,9},{9,10},{10,1... | collective-permute-start | bytes 786440 | tf_op jit(solution)/shard_map/ppermute | solution.py:319
  88.7 7.8 %collective-permute-start.27 = (bf16[1024,128]{1,0:T(8,128)(2,1)S(1)}, bf16[1024,128]{1,0:T(8,128)(2,1)S(1)}, u32[]{:S(2)}, u32[]{:S(2)}) collective-permute-start(bf16[1024,128]{1,0:T(8,128)(2,1)S(1)} %get-tuple-element.59), channel_id=1, source_target_pairs={{0,3},{1,0},{2,1},{3,2},{4,7},{5,4},{6,5},{7,6},{8,11},{9,8},{10,9... | collective-permute-start | bytes 786440 | tf_op jit(solution)/shard_map/ppermute | solution.py:319
  91.5 10.6 %collective-permute-start.16 = (bf16[1024,128]{1,0:T(8,128)(2,1)S(1)}, bf16[1024,128]{1,0:T(8,128)(2,1)S(1)}, u32[]{:S(2)}, u32[]{:S(2)}) collective-permute-start(bf16[1024,128]{1,0:T(8,128)(2,1)S(1)} %get-tuple-element.49), channel_id=1, source_target_pairs={{0,1},{1,2},{2,3},{3,0},{4,5},{5,6},{6,7},{7,4},{8,9},{9,10},{10,1... | collective-permute-start | bytes 786440 | tf_op jit(solution)/shard_map/ppermute | solution.py:319
  91.6 10.5 %collective-permute-start.17 = (bf16[1024,128]{1,0:T(8,128)(2,1)S(1)}, bf16[1024,128]{1,0:T(8,128)(2,1)S(1)}, u32[]{:S(2)}, u32[]{:S(2)}) collective-permute-start(bf16[1024,128]{1,0:T(8,128)(2,1)S(1)} %get-tuple-element.50), channel_id=1, source_target_pairs={{0,3},{1,0},{2,1},{3,2},{4,7},{5,4},{6,5},{7,6},{8,11},{9,8},{10,9... | collective-permute-start | bytes 786440 | tf_op jit(solution)/shard_map/ppermute | solution.py:319
  103.2 29.1 %all-to-all-start.1 = ((bf16[64,32,128]{2,1,0:T(8,128)(2,1)}), bf16[64,32,128]{2,1,0:T(8,128)(2,1)S(1)}, u32[]{:S(2)}, u32[]{:S(2)}) async-start(bf16[64,32,128]{2,1,0:T(8,128)(2,1)} %bitcast.10), calls=%async_computation.1 | async-start | bytes 1048576 | tf_op jit(solution)/shard_map/all_to_all | solution.py:360
  115.1 5.9 %collective-permute-start.28 = (bf16[32,2048]{1,0:T(8,128)(2,1)S(1)}, bf16[32,2048]{1,0:T(8,128)(2,1)S(1)}, u32[]{:S(2)}, u32[]{:S(2)}) collective-permute-start(bf16[32,2048]{1,0:T(8,128)(2,1)S(1)} %get-tuple-element.62), channel_id=1, source_target_pairs={{0,64},{64,128},{128,192},{192,0},{1,65},{65,129},{129,193},{193,1... | collective-permute-start | bytes 393224 | tf_op jit(solution)/shard_map/ppermute | solution.py:319
  115.5 8.6 %collective-permute-start.29 = (bf16[32,2048]{1,0:T(8,128)(2,1)S(1)}, bf16[32,2048]{1,0:T(8,128)(2,1)S(1)}, u32[]{:S(2)}, u32[]{:S(2)}) collective-permute-start(bf16[32,2048]{1,0:T(8,128)(2,1)S(1)} %get-tuple-element.63), channel_id=1, source_target_pairs={{0,128},{64,192},{128,0},{192,64},{1,129},{65,193},{129,1},{193,65... | collective-permute-start | bytes 393224 | tf_op jit(solution)/shard_map/ppermute | solution.py:319
  118.2 6.0 %collective-permute-start.30 = (bf16[32,2048]{1,0:T(8,128)(2,1)S(1)}, bf16[32,2048]{1,0:T(8,128)(2,1)S(1)}, u32[]{:S(2)}, u32[]{:S(2)}) collective-permute-start(bf16[32,2048]{1,0:T(8,128)(2,1)S(1)} %get-tuple-element.64), channel_id=1, source_target_pairs={{0,192},{64,0},{128,64},{192,128},{1,193},{65,1},{129,65},{193,129... | collective-permute-start | bytes 393224 | tf_op jit(solution)/shard_map/ppermute | solution.py:319
  (3 other events, 32.7 us)

commit v4 on v3

--- a/solution.py
+++ b/solution.py
@@ -325,20 +325,28 @@
     b_send = prep_b(response.reshape(512, 512), response_mask.reshape(4, 4))
 
     b_own = lax.all_to_all(b_send, "col", 0, 0)
-
     gathered = [{0: chunk} for chunk in chunks]
-    for step in range(1, 5):
-        if step == 2:
-            gathered[1][1], gathered[1][7], b_own = lax.optimization_barrier((gathered[1][1], gathered[1][7], b_own))
-        for q in range(NQ):
-            got = gathered[q]
-            if step < 4 or q % 2 == 0:
-                got[step] = turn_z(got[step - 1], 1)
-            if step < 4 or q % 2 == 1:
-                got[8 - step] = turn_z(got[(9 - step) % 8], -1)
-
+
+    def ring(q, step):
+        got = gathered[q]
+        if step < 4 or q % 2 == 0:
+            got[step] = turn_z(got[step - 1], 1)
+        if step < 4 or q % 2 == 1:
+            got[8 - step] = turn_z(got[(9 - step) % 8], -1)
+
+    ring(0, 1)
+    ring(1, 1)
+    (gathered[1][1], gathered[1][7], b_own) = lax.optimization_barrier((gathered[1][1], gathered[1][7], b_own))
     behind, ahead = turn(b_own, "row", 1), turn(b_own, "row", -1)
+    ring(0, 2)
+    ring(1, 2)
+    (gathered[1][2], gathered[1][6], behind, ahead) = lax.optimization_barrier((gathered[1][2], gathered[1][6], behind, ahead))
     bs = [b_own, behind, ahead, turn(behind[:8], "row", 1), turn(ahead[8:], "row", -1)]
+    ring(0, 3)
+    ring(1, 3)
+    ring(0, 4)
+    ring(1, 4)
+
     bs = [value.reshape(-1, 4, 2, 32, 256) for value in bs]
 
     kept_b, sent_b = arrange(bs)

time: 134 us -> 132 us (0.985)
  starting transfers between devices: 66.6 us -> 63 us
    ppermute x14, starting transfers between devices: 17.9 us -> 13.5 us  [turn_z(): return lax.ppermute(value, 'col', pairs)]
    ppermute x15, starting transfers between devices: 20.5 us -> 23.1 us  [turn(): return lax.ppermute(value, axis, [(i, (i + shift) % 4) for i in range(4)])]
    all_to_all x1, starting transfers between devices: 11.9 us -> 10.4 us  [per_device(): own = lax.all_to_all(product.reshape(64, 32, 128), ('col', 'layer'), 0, 0)]
  transfers between devices with their start and end apart: 33 -> 33, of which waited for: 15 -> 12; matrix products, arithmetic and copies ran while one was open for 0% -> 0% of each run, Pallas kernels for 7% -> 7%
where the time goes in v4:
time: 132 us; the launch traced here: 131 us
  starting transfers between devices  63 us (48%)
  waiting for transfers between devices  52 us (39%)
  Pallas kernels  16.1 us (12%)
    ppermute x14, waiting for transfers between devices, turn_z(): return lax.ppermute(value, 'col', pairs)  30.7 us
    ppermute x15, starting transfers between devices, turn(): return lax.ppermute(value, axis, [(i, (i + shift) % 4) for i in range(4)])  23.1 us
    ppermute x15, waiting for transfers between devices, turn(): return lax.ppermute(value, axis, [(i, (i + shift) % 4) for i in range(4)])  13.9 us
    ppermute x14, starting transfers between devices, turn_z(): return lax.ppermute(value, 'col', pairs)  13.5 us
    all_to_all x1, starting transfers between devices, per_device(): own = lax.all_to_all(product.reshape(64, 32, 128), ('col', 'layer'), 0, 0)  10.4 us
    all_to_all x1, starting transfers between devices, per_device(): b_own = lax.all_to_all(b_send, 'col', 0, 0)  9.99 us
    all_to_all x1, waiting for transfers between devices, per_device(): own = lax.all_to_all(product.reshape(64, 32, 128), ('col', 'layer'), 0, 0)  7.4 us
    ppermute x2, starting transfers between devices, per_device(): received = lax.ppermute(other, 'col', [(i, i ^ 1) for i in range(16)])  6 us
  transfers between devices with their start and end apart: 33, of which 12 were waited for; matrix products, arithmetic and copies ran while one was open for 0% of the time, Pallas kernels for 7%

profile of v4, /device:TPU:1, one launch (start us, length us, event | category | flops | bytes accessed | tf_op | source)
XLA Modules:
  0.0 131.3 jit_solution(6137423976980002895)
XLA Ops:
  0.0 2.0 %shard_map.55 = (bf16[1040,128]{1,0:T(8,128)(2,1)}, bf16[1024,128]{1,0:T(8,128)(2,1)}) custom-call(s32[1,16]{1,0:T(1,128)} %bitcast.21, bf16[2048,128]{1,0:T(8,128)(2,1)} %bitcast.17, s32[4,16]{1,0:T(4,128)} %bitcast.19), custom_call_target="tpu_custom_call" | custom-call | flops 262144 | bytes 1048576 | tf_op jit(solution)/shard_map/pallas_call | solution.py:63
  2.0 2.1 %shard_map.56 = bf16[16,64,256]{2,1,0:T(8,128)(2,1)} custom-call(s32[4,4]{1,0:T(4,128)} %bitcast.20, bf16[512,512]{1,0:T(8,128)(2,1)} %bitcast.18), custom_call_target="tpu_custom_call" | custom-call | flops 262144 | bytes 1048576 | tf_op jit(solution)/shard_map/pallas_call | solution.py:93
  4.1 10.0 %all-to-all-start = ((bf16[16,64,256]{2,1,0:T(8,128)(2,1)}), bf16[16,64,256]{2,1,0:T(8,128)(2,1)S(1)}, u32[]{:S(2)}, u32[]{:S(2)}) async-start(bf16[16,64,256]{2,1,0:T(8,128)(2,1)} %shard_map.56), calls=%async_computation | async-start | bytes 1048576 | tf_op jit(solution)/shard_map/all_to_all | solution.py:327
  14.1 1.5 %collective-permute-start.7 = (bf16[1024,128]{1,0:T(8,128)(2,1)S(1)}, bf16[1024,128]{1,0:T(8,128)(2,1)S(1)}, u32[]{:S(2)}, u32[]{:S(2)}) collective-permute-start(bf16[1024,128]{1,0:T(8,128)(2,1)S(1)} %copy-done.1), channel_id=1, source_target_pairs={{0,8},{4,12},{8,16},{12,20},{16,24},{20,28},{24,32},{28,36},{32,40... | collective-permute-start | bytes 786440 | tf_op jit(solution)/shard_map/ppermute | solution.py:315
  17.1 2.5 %collective-permute-start.4 = (bf16[1040,128]{1,0:T(8,128)(2,1)S(1)}, bf16[1040,128]{1,0:T(8,128)(2,1)S(1)}, u32[]{:S(2)}, u32[]{:S(2)}) collective-permute-start(bf16[1040,128]{1,0:T(8,128)(2,1)S(1)} %copy-done), channel_id=1, source_target_pairs={{0,56},{4,60},{8,0},{12,4},{16,8},{20,12},{24,16},{28,20},{32,24},... | collective-permute-start | bytes 798728 | tf_op jit(solution)/shard_map/ppermute | solution.py:315
  19.6 15.0 %collective-permute-done.7.refs_1_ = bf16[1024,128]{1,0:T(8,128)(2,1)S(1)} collective-permute-done((bf16[1024,128]{1,0:T(8,128)(2,1)S(1)}, bf16[1024,128]{1,0:T(8,128)(2,1)S(1)}, u32[]{:S(2)}, u32[]{:S(2)}) %collective-permute-start.7) | collective-permute-done | bytes 262176 | tf_op jit(solution)/shard_map/ppermute | solution.py:315
  35.8 1.5 %collective-permute-start.12 = (bf16[16,64,256]{2,1,0:T(8,128)(2,1)S(1)}, bf16[16,64,256]{2,1,0:T(8,128)(2,1)S(1)}, u32[]{:S(2)}, u32[]{:S(2)}) collective-permute-start(bf16[16,64,256]{2,1,0:T(8,128)(2,1)S(1)} %all-to-all-done), channel_id=1, source_target_pairs={{0,192},{64,0},{128,64},{192,128},{1,193},{65,1},{129,65},{193,129... | collective-permute-start | bytes 1572872 | tf_op jit(solution)/shard_map/ppermute | solution.py:319
  37.4 2.9 %collective-permute-done.refs_1_ = bf16[1040,128]{1,0:T(8,128)(2,1)S(1)} collective-permute-done((bf16[1040,128]{1,0:T(8,128)(2,1)S(1)}, bf16[1040,128]{1,0:T(8,128)(2,1)S(1)}, u32[]{:S(2)}, u32[]{:S(2)}) %collective-permute-start) | collective-permute-done | bytes 266272 | tf_op jit(solution)/shard_map/ppermute | solution.py:315
  40.3 2.7 %collective-permute-start.10 = (bf16[1024,128]{1,0:T(8,128)(2,1)S(1)}, bf16[1024,128]{1,0:T(8,128)(2,1)S(1)}, u32[]{:S(2)}, u32[]{:S(2)}) collective-permute-start(bf16[1024,128]{1,0:T(8,128)(2,1)S(1)} %collective-permute-done.8.refs_7_), channel_id=1, source_target_pairs={{0,56},{4,60},{8,0},{12,4},{16,8},{20,12},{24,16},{28,20},{32,24},... | collective-permute-start | bytes 786440 | tf_op jit(solution)/shard_map/ppermute | solution.py:315
  42.9 5.6 %collective-permute-done.1.refs_2_ = bf16[1040,128]{1,0:T(8,128)(2,1)S(1)} collective-permute-done((bf16[1040,128]{1,0:T(8,128)(2,1)S(1)}, bf16[1040,128]{1,0:T(8,128)(2,1)S(1)}, u32[]{:S(2)}, u32[]{:S(2)}) %collective-permute-start.1) | collective-permute-done | bytes 266272 | tf_op jit(solution)/shard_map/ppermute | solution.py:315
  48.5 1.5 %collective-permute-start.2 = (bf16[1040,128]{1,0:T(8,128)(2,1)S(1)}, bf16[1040,128]{1,0:T(8,128)(2,1)S(1)}, u32[]{:S(2)}, u32[]{:S(2)}) collective-permute-start(bf16[1040,128]{1,0:T(8,128)(2,1)S(1)} %collective-permute-done.1.refs_2_), channel_id=1, source_target_pairs={{0,8},{4,12},{8,16},{12,20},{16,24},{20,28},{24,32},{28,36},{32,40... | collective-permute-start | bytes 798728 | tf_op jit(solution)/shard_map/ppermute | solution.py:315
  50.0 4.1 %collective-permute-done.9.refs_2_ = bf16[1024,128]{1,0:T(8,128)(2,1)S(1)} collective-permute-done((bf16[1024,128]{1,0:T(8,128)(2,1)S(1)}, bf16[1024,128]{1,0:T(8,128)(2,1)S(1)}, u32[]{:S(2)}, u32[]{:S(2)}) %collective-permute-start.9) | collective-permute-done | bytes 262176 | tf_op jit(solution)/shard_map/ppermute | solution.py:315
  54.1 1.4 %collective-permute-start.13 = (bf16[8,64,256]{2,1,0:T(8,128)(2,1)S(1)}, bf16[8,64,256]{2,1,0:T(8,128)(2,1)S(1)}, u32[]{:S(2)}, u32[]{:S(2)}) collective-permute-start(bf16[8,64,256]{2,1,0:T(8,128)(2,1)S(1)} %slice.6), channel_id=1, source_target_pairs={{0,64},{64,128},{128,192},{192,0},{1,65},{65,129},{129,193},{193,1... | collective-permute-start | bytes 786440 | tf_op jit(solution)/shard_map/ppermute | solution.py:319
  56.7 3.1 %collective-permute-done.2.refs_3_ = bf16[1040,128]{1,0:T(8,128)(2,1)S(1)} collective-permute-done((bf16[1040,128]{1,0:T(8,128)(2,1)S(1)}, bf16[1040,128]{1,0:T(8,128)(2,1)S(1)}, u32[]{:S(2)}, u32[]{:S(2)}) %collective-permute-start.2) | collective-permute-done | bytes 266272 | tf_op jit(solution)/shard_map/ppermute | solution.py:315
  59.8 3.0 %collective-permute-start.14 = (bf16[8,64,256]{2,1,0:T(8,128)(2,1)S(1)}, bf16[8,64,256]{2,1,0:T(8,128)(2,1)S(1)}, u32[]{:S(2)}, u32[]{:S(2)}) collective-permute-start(bf16[8,64,256]{2,1,0:T(8,128)(2,1)S(1)} %slice.7), channel_id=1, source_target_pairs={{0,192},{64,0},{128,64},{192,128},{1,193},{65,1},{129,65},{193,129... | collective-permute-start | bytes 786440 | tf_op jit(solution)/shard_map/ppermute | solution.py:319
  62.9 2.7 %collective-permute-start.22 = (bf16[1024,128]{1,0:T(8,128)(2,1)S(1)}, bf16[1024,128]{1,0:T(8,128)(2,1)S(1)}, u32[]{:S(2)}, u32[]{:S(2)}) collective-permute-start(bf16[1024,128]{1,0:T(8,128)(2,1)S(1)} %collective-permute-done.21.refs_5_), channel_id=1, source_target_pairs={{0,56},{4,60},{8,0},{12,4},{16,8},{20,12},{24,16},{28,20},{32,24},... | collective-permute-start | bytes 786440 | tf_op jit(solution)/shard_map/ppermute | solution.py:315
  67.5 2.2 %shard_map.58 = bf16[1040,512]{1,0:T(8,128)(2,1)S(1)} custom-call(bf16[1040,128]{1,0:T(8,128)(2,1)S(1)} %copy-done, bf16[1040,128]{1,0:T(8,128)(2,1)S(1)} %collective-permute-done.refs_1_, bf16[1040,128]{1,0:T(8,128)(2,1)S(1)} %collective-permute-done.1.refs_2_, bf16[1040,128]{1,0:T(8,128)(2,1)S(1)} %collective-permute-done.2.refs_3_, ...), custom_call_target="tpu_custom_call" | custom-call | flops 1073741824 | bytes 3145728 | tf_op jit(solution)/shard_map/pallas_call | solution.py:183
  69.6 5.4 %collective-permute-start.15 = (bf16[1040,512]{1,0:T(8,128)(2,1)S(1)}, bf16[1040,512]{1,0:T(8,128)(2,1)S(1)}, u32[]{:S(2)}, u32[]{:S(2)}) collective-permute-start(bf16[1040,512]{1,0:T(8,128)(2,1)S(1)} %shard_map.58), channel_id=1, source_target_pairs={{0,4},{4,0},{8,12},{12,8},{16,20},{20,16},{24,28},{28,24},{32,36},... | collective-permute-start | bytes 3194888 | tf_op jit(solution)/shard_map/ppermute | solution.py:359
  75.0 2.1 %shard_map.61 = bf16[1024,512]{1,0:T(8,128)(2,1)S(1)} custom-call(bf16[1024,128]{1,0:T(8,128)(2,1)S(1)} %copy-done.1, bf16[1024,128]{1,0:T(8,128)(2,1)S(1)} %collective-permute-done.7.refs_1_, bf16[1024,128]{1,0:T(8,128)(2,1)S(1)} %collective-permute-done.9.refs_2_, bf16[1024,128]{1,0:T(8,128)(2,1)S(1)} %collective-permute-done.20.refs_3_, ...), custom_call_target="tpu_custom_call" | custom-call | flops 1073741824 | bytes 3145728 | tf_op jit(solution)/shard_map/pallas_call | solution.py:183
  77.8 2.2 %shard_map.59 = (f32[1024,128]{1,0:T(8,128)S(1)}, f32[1024,128]{1,0:T(8,128)S(1)}, f32[1024,128]{1,0:T(8,128)S(1)}, bf16[512,128]{1,0:T(8,128)(2,1)S(1)}, bf16[5...) custom-call(bf16[1040,128]{1,0:T(8,128)(2,1)S(1)} %copy-done, bf16[1040,128]{1,0:T(8,128)(2,1)S(1)} %collective-permute-done.refs_1_, ...), custom_call_target="tpu_custom_call" | custom-call | flops 1073741824 | bytes 4194304 | tf_op jit(solution)/shard_map/pallas_call | solution.py:219
  81.3 1.5 %collective-permute-start.17 = (bf16[512,128]{1,0:T(8,128)(2,1)S(1)}, bf16[512,128]{1,0:T(8,128)(2,1)S(1)}, u32[]{:S(2)}, u32[]{:S(2)}) collective-permute-start(bf16[512,128]{1,0:T(8,128)(2,1)S(1)} %get-tuple-element.56), channel_id=1, source_target_pairs={{0,3},{1,0},{2,1},{3,2},{4,7},{5,4},{6,5},{7,6},{8,11},{9,8},{10,9... | collective-permute-start | bytes 393224 | tf_op jit(solution)/shard_map/ppermute | solution.py:319
  82.8 2.2 %shard_map.62 = (f32[1024,128]{1,0:T(8,128)S(1)}, f32[1024,128]{1,0:T(8,128)S(1)}, f32[1024,128]{1,0:T(8,128)S(1)}, bf16[512,128]{1,0:T(8,128)(2,1)S(1)}, bf16[512,128]{1,0:T(8,128)(2,1)S(1)}) custom-call(bf16[1024,128]{1,0:T(8,128)(2,1)S(1)} %copy-done.1, bf16[1024,128]{1,0:T(8,128)(2,1)S(1)} %collective-permute-done.7.refs_1_, ...), custom_call_target="tpu_custom_call" | custom-call | flops 1073741824 | bytes 4194304 | tf_op jit(solution)/shard_map/pallas_call | solution.py:219
  85.0 2.7 %collective-permute-start.25 = (bf16[512,128]{1,0:T(8,128)(2,1)S(1)}, bf16[512,128]{1,0:T(8,128)(2,1)S(1)}, u32[]{:S(2)}, u32[]{:S(2)}) collective-permute-start(bf16[512,128]{1,0:T(8,128)(2,1)S(1)} %get-tuple-element.65), channel_id=1, source_target_pairs={{0,3},{1,0},{2,1},{3,2},{4,7},{5,4},{6,5},{7,6},{8,11},{9,8},{10,9... | collective-permute-start | bytes 393224 | tf_op jit(solution)/shard_map/ppermute | solution.py:319
  87.9 2.7 %collective-permute-start.19 = (bf16[1024,128]{1,0:T(8,128)(2,1)S(1)}, bf16[1024,128]{1,0:T(8,128)(2,1)S(1)}, u32[]{:S(2)}, u32[]{:S(2)}) collective-permute-start(bf16[1024,128]{1,0:T(8,128)(2,1)S(1)} %get-tuple-element.58), channel_id=1, source_target_pairs={{0,3},{1,0},{2,1},{3,2},{4,7},{5,4},{6,5},{7,6},{8,11},{9,8},{10,9... | collective-permute-start | bytes 786440 | tf_op jit(solution)/shard_map/ppermute | solution.py:319
  90.8 2.7 %collective-permute-start.27 = (bf16[1024,128]{1,0:T(8,128)(2,1)S(1)}, bf16[1024,128]{1,0:T(8,128)(2,1)S(1)}, u32[]{:S(2)}, u32[]{:S(2)}) collective-permute-start(bf16[1024,128]{1,0:T(8,128)(2,1)S(1)} %get-tuple-element.67), channel_id=1, source_target_pairs={{0,3},{1,0},{2,1},{3,2},{4,7},{5,4},{6,5},{7,6},{8,11},{9,8},{10,9... | collective-permute-start | bytes 786440 | tf_op jit(solution)/shard_map/ppermute | solution.py:319
  93.5 2.2 %collective-permute-done.18.refs_2_ = bf16[1024,128]{1,0:T(8,128)(2,1)S(1)} collective-permute-done((bf16[1024,128]{1,0:T(8,128)(2,1)S(1)}, bf16[1024,128]{1,0:T(8,128)(2,1)S(1)}, u32[]{:S(2)}, u32[]{:S(2)}) %collective-permute-start.18) | collective-permute-done | bytes 262176 | tf_op jit(solution)/shard_map/ppermute | solution.py:319
  95.7 5.6 %collective-permute-done.26.refs_5_ = bf16[1024,128]{1,0:T(8,128)(2,1)S(1)} collective-permute-done((bf16[1024,128]{1,0:T(8,128)(2,1)S(1)}, bf16[1024,128]{1,0:T(8,128)(2,1)S(1)}, u32[]{:S(2)}, u32[]{:S(2)}) %collective-permute-start.26) | collective-permute-done | bytes 262176 | tf_op jit(solution)/shard_map/ppermute | solution.py:319
  102.4 10.4 %all-to-all-start.1 = ((bf16[64,32,128]{2,1,0:T(8,128)(2,1)}), bf16[64,32,128]{2,1,0:T(8,128)(2,1)S(1)}, u32[]{:S(2)}, u32[]{:S(2)}) async-start(bf16[64,32,128]{2,1,0:T(8,128)(2,1)} %bitcast.10), calls=%async_computation.1 | async-start | bytes 1048576 | tf_op jit(solution)/shard_map/all_to_all | solution.py:368
  112.8 1.4 %collective-permute-start.28 = (bf16[32,2048]{1,0:T(8,128)(2,1)S(1)}, bf16[32,2048]{1,0:T(8,128)(2,1)S(1)}, u32[]{:S(2)}, u32[]{:S(2)}) collective-permute-start(bf16[32,2048]{1,0:T(8,128)(2,1)S(1)} %get-tuple-element.70), channel_id=1, source_target_pairs={{0,64},{64,128},{128,192},{192,0},{1,65},{65,129},{129,193},{193,1... | collective-permute-start | bytes 393224 | tf_op jit(solution)/shard_map/ppermute | solution.py:319
  114.2 2.5 %collective-permute-start.29 = (bf16[32,2048]{1,0:T(8,128)(2,1)S(1)}, bf16[32,2048]{1,0:T(8,128)(2,1)S(1)}, u32[]{:S(2)}, u32[]{:S(2)}) collective-permute-start(bf16[32,2048]{1,0:T(8,128)(2,1)S(1)} %get-tuple-element.71), channel_id=1, source_target_pairs={{0,128},{64,192},{128,0},{192,64},{1,129},{65,193},{129,1},{193,65... | collective-permute-start | bytes 393224 | tf_op jit(solution)/shard_map/ppermute | solution.py:319
  118.7 3.9 %collective-permute-done.29.refs_2_ = bf16[32,2048]{1,0:T(8,128)(2,1)S(1)} collective-permute-done((bf16[32,2048]{1,0:T(8,128)(2,1)S(1)}, bf16[32,2048]{1,0:T(8,128)(2,1)S(1)}, u32[]{:S(2)}, u32[]{:S(2)}) %collective-permute-start.29) | collective-permute-done | bytes 131104 | tf_op jit(solution)/shard_map/ppermute | solution.py:319
  122.6 7.4 %all-to-all-done.1.own = bf16[64,32,128]{2,1,0:T(8,128)(2,1)S(1)} async-done(((bf16[64,32,128]{2,1,0:T(8,128)(2,1)}), bf16[64,32,128]{2,1,0:T(8,128)(2,1)S(1)}, u32[]{:S(2)}, u32[]{:S(2)}) %all-to-all-start.1) | async-done | bytes 524320 | tf_op jit(solution)/shard_map/all_to_all | solution.py:368
  (51 shorter events, 12.7 us)
Async XLA Ops:
  4.1 30.4 %all-to-all-start = ((bf16[16,64,256]{2,1,0:T(8,128)(2,1)}), bf16[16,64,256]{2,1,0:T(8,128)(2,1)S(1)}, u32[]{:S(2)}, u32[]{:S(2)}) async-start(bf16[16,64,256]{2,1,0:T(8,128)(2,1)} %shard_map.56), calls=%async_computation | async-start | bytes 1048576 | tf_op jit(solution)/shard_map/all_to_all | solution.py:327
  14.1 20.4 %collective-permute-start.7 = (bf16[1024,128]{1,0:T(8,128)(2,1)S(1)}, bf16[1024,128]{1,0:T(8,128)(2,1)S(1)}, u32[]{:S(2)}, u32[]{:S(2)}) collective-permute-start(bf16[1024,128]{1,0:T(8,128)(2,1)S(1)} %copy-done.1), channel_id=1, source_target_pairs={{0,8},{4,12},{8,16},{12,20},{16,24},{20,28},{24,32},{28,36},{32,40... | collective-permute-start | bytes 786440 | tf_op jit(solution)/shard_map/ppermute | solution.py:315
  15.6 19.0 %collective-permute-start.8 = (bf16[1024,128]{1,0:T(8,128)(2,1)S(1)}, bf16[1024,128]{1,0:T(8,128)(2,1)S(1)}, u32[]{:S(2)}, u32[]{:S(2)}) collective-permute-start(bf16[1024,128]{1,0:T(8,128)(2,1)S(1)} %copy-done.1), channel_id=1, source_target_pairs={{0,56},{4,60},{8,0},{12,4},{16,8},{20,12},{24,16},{28,20},{32,24},... | collective-permute-start | bytes 786440 | tf_op jit(solution)/shard_map/ppermute | solution.py:315
  16.9 23.3 %collective-permute-start = (bf16[1040,128]{1,0:T(8,128)(2,1)S(1)}, bf16[1040,128]{1,0:T(8,128)(2,1)S(1)}, u32[]{:S(2)}, u32[]{:S(2)}) collective-permute-start(bf16[1040,128]{1,0:T(8,128)(2,1)S(1)} %copy-done), channel_id=1, source_target_pairs={{0,8},{4,12},{8,16},{12,20},{16,24},{20,28},{24,32},{28,36},{32,40... | collective-permute-start | bytes 798728 | tf_op jit(solution)/shard_map/ppermute | solution.py:315
  17.1 25.9 %collective-permute-start.4 = (bf16[1040,128]{1,0:T(8,128)(2,1)S(1)}, bf16[1040,128]{1,0:T(8,128)(2,1)S(1)}, u32[]{:S(2)}, u32[]{:S(2)}) collective-permute-start(bf16[1040,128]{1,0:T(8,128)(2,1)S(1)} %copy-done), channel_id=1, source_target_pairs={{0,56},{4,60},{8,0},{12,4},{16,8},{20,12},{24,16},{28,20},{32,24},... | collective-permute-start | bytes 798728 | tf_op jit(solution)/shard_map/ppermute | solution.py:315
  34.5 19.6 %collective-permute-start.11 = (bf16[16,64,256]{2,1,0:T(8,128)(2,1)S(1)}, bf16[16,64,256]{2,1,0:T(8,128)(2,1)S(1)}, u32[]{:S(2)}, u32[]{:S(2)}) collective-permute-start(bf16[16,64,256]{2,1,0:T(8,128)(2,1)S(1)} %all-to-all-done), channel_id=1, source_target_pairs={{0,64},{64,128},{128,192},{192,0},{1,65},{65,129},{129,193},{193,1... | collective-permute-start | bytes 1572872 | tf_op jit(solution)/shard_map/ppermute | solution.py:319
  35.8 18.3 %collective-permute-start.12 = (bf16[16,64,256]{2,1,0:T(8,128)(2,1)S(1)}, bf16[16,64,256]{2,1,0:T(8,128)(2,1)S(1)}, u32[]{:S(2)}, u32[]{:S(2)}) collective-permute-start(bf16[16,64,256]{2,1,0:T(8,128)(2,1)S(1)} %all-to-all-done), channel_id=1, source_target_pairs={{0,192},{64,0},{128,64},{192,128},{1,193},{65,1},{129,65},{193,129... | collective-permute-start | bytes 1572872 | tf_op jit(solution)/shard_map/ppermute | solution.py:319
  40.2 8.2 %collective-permute-start.1 = (bf16[1040,128]{1,0:T(8,128)(2,1)S(1)}, bf16[1040,128]{1,0:T(8,128)(2,1)S(1)}, u32[]{:S(2)}, u32[]{:S(2)}) collective-permute-start(bf16[1040,128]{1,0:T(8,128)(2,1)S(1)} %collective-permute-done.refs_1_), channel_id=1, source_target_pairs={{0,8},{4,12},{8,16},{12,20},{16,24},{20,28},{24,32},{28,36},{32,40... | collective-permute-start | bytes 798728 | tf_op jit(solution)/shard_map/ppermute | solution.py:315
  40.3 8.3 %collective-permute-start.10 = (bf16[1024,128]{1,0:T(8,128)(2,1)S(1)}, bf16[1024,128]{1,0:T(8,128)(2,1)S(1)}, u32[]{:S(2)}, u32[]{:S(2)}) collective-permute-start(bf16[1024,128]{1,0:T(8,128)(2,1)S(1)} %collective-permute-done.8.refs_7_), channel_id=1, source_target_pairs={{0,56},{4,60},{8,0},{12,4},{16,8},{20,12},{24,16},{28,20},{32,24},... | collective-permute-start | bytes 786440 | tf_op jit(solution)/shard_map/ppermute | solution.py:315
  42.9 11.2 %collective-permute-start.9 = (bf16[1024,128]{1,0:T(8,128)(2,1)S(1)}, bf16[1024,128]{1,0:T(8,128)(2,1)S(1)}, u32[]{:S(2)}, u32[]{:S(2)}) collective-permute-start(bf16[1024,128]{1,0:T(8,128)(2,1)S(1)} %collective-permute-done.7.refs_1_), channel_id=1, source_target_pairs={{0,8},{4,12},{8,16},{12,20},{16,24},{20,28},{24,32},{28,36},{32,40... | collective-permute-start | bytes 786440 | tf_op jit(solution)/shard_map/ppermute | solution.py:315
  48.5 7.0 %collective-permute-start.5 = (bf16[1040,128]{1,0:T(8,128)(2,1)S(1)}, bf16[1040,128]{1,0:T(8,128)(2,1)S(1)}, u32[]{:S(2)}, u32[]{:S(2)}) collective-permute-start(bf16[1040,128]{1,0:T(8,128)(2,1)S(1)} %collective-permute-done.4.refs_7_), channel_id=1, source_target_pairs={{0,56},{4,60},{8,0},{12,4},{16,8},{20,12},{24,16},{28,20},{32,24},... | collective-permute-start | bytes 798728 | tf_op jit(solution)/shard_map/ppermute | solution.py:315
  48.5 11.3 %collective-permute-start.2 = (bf16[1040,128]{1,0:T(8,128)(2,1)S(1)}, bf16[1040,128]{1,0:T(8,128)(2,1)S(1)}, u32[]{:S(2)}, u32[]{:S(2)}) collective-permute-start(bf16[1040,128]{1,0:T(8,128)(2,1)S(1)} %collective-permute-done.1.refs_2_), channel_id=1, source_target_pairs={{0,8},{4,12},{8,16},{12,20},{16,24},{20,28},{24,32},{28,36},{32,40... | collective-permute-start | bytes 798728 | tf_op jit(solution)/shard_map/ppermute | solution.py:315
  54.1 8.7 %collective-permute-start.13 = (bf16[8,64,256]{2,1,0:T(8,128)(2,1)S(1)}, bf16[8,64,256]{2,1,0:T(8,128)(2,1)S(1)}, u32[]{:S(2)}, u32[]{:S(2)}) collective-permute-start(bf16[8,64,256]{2,1,0:T(8,128)(2,1)S(1)} %slice.6), channel_id=1, source_target_pairs={{0,64},{64,128},{128,192},{192,0},{1,65},{65,129},{129,193},{193,1... | collective-permute-start | bytes 786440 | tf_op jit(solution)/shard_map/ppermute | solution.py:319
  55.5 7.3 %collective-permute-start.21 = (bf16[1024,128]{1,0:T(8,128)(2,1)S(1)}, bf16[1024,128]{1,0:T(8,128)(2,1)S(1)}, u32[]{:S(2)}, u32[]{:S(2)}) collective-permute-start(bf16[1024,128]{1,0:T(8,128)(2,1)S(1)} %collective-permute-done.10.refs_6_), channel_id=1, source_target_pairs={{0,56},{4,60},{8,0},{12,4},{16,8},{20,12},{24,16},{28,20},{32,24},... | collective-permute-start | bytes 786440 | tf_op jit(solution)/shard_map/ppermute | solution.py:315
  55.5 11.9 %collective-permute-start.6 = (bf16[1040,128]{1,0:T(8,128)(2,1)S(1)}, bf16[1040,128]{1,0:T(8,128)(2,1)S(1)}, u32[]{:S(2)}, u32[]{:S(2)}) collective-permute-start(bf16[1040,128]{1,0:T(8,128)(2,1)S(1)} %collective-permute-done.5.refs_6_), channel_id=1, source_target_pairs={{0,56},{4,60},{8,0},{12,4},{16,8},{20,12},{24,16},{28,20},{32,24},... | collective-permute-start | bytes 798728 | tf_op jit(solution)/shard_map/ppermute | solution.py:315
  59.8 7.6 %collective-permute-start.3 = (bf16[1040,128]{1,0:T(8,128)(2,1)S(1)}, bf16[1040,128]{1,0:T(8,128)(2,1)S(1)}, u32[]{:S(2)}, u32[]{:S(2)}) collective-permute-start(bf16[1040,128]{1,0:T(8,128)(2,1)S(1)} %collective-permute-done.2.refs_3_), channel_id=1, source_target_pairs={{0,8},{4,12},{8,16},{12,20},{16,24},{20,28},{24,32},{28,36},{32,40... | collective-permute-start | bytes 798728 | tf_op jit(solution)/shard_map/ppermute | solution.py:315
  59.8 6.8 %collective-permute-start.14 = (bf16[8,64,256]{2,1,0:T(8,128)(2,1)S(1)}, bf16[8,64,256]{2,1,0:T(8,128)(2,1)S(1)}, u32[]{:S(2)}, u32[]{:S(2)}) collective-permute-start(bf16[8,64,256]{2,1,0:T(8,128)(2,1)S(1)} %slice.7), channel_id=1, source_target_pairs={{0,192},{64,0},{128,64},{192,128},{1,193},{65,1},{129,65},{193,129... | collective-permute-start | bytes 786440 | tf_op jit(solution)/shard_map/ppermute | solution.py:319
  62.8 12.2 %collective-permute-start.20 = (bf16[1024,128]{1,0:T(8,128)(2,1)S(1)}, bf16[1024,128]{1,0:T(8,128)(2,1)S(1)}, u32[]{:S(2)}, u32[]{:S(2)}) collective-permute-start(bf16[1024,128]{1,0:T(8,128)(2,1)S(1)} %collective-permute-done.9.refs_2_), channel_id=1, source_target_pairs={{0,8},{4,12},{8,16},{12,20},{16,24},{20,28},{24,32},{28,36},{32,40... | collective-permute-start | bytes 786440 | tf_op jit(solution)/shard_map/ppermute | solution.py:315
  62.9 12.2 %collective-permute-start.22 = (bf16[1024,128]{1,0:T(8,128)(2,1)S(1)}, bf16[1024,128]{1,0:T(8,128)(2,1)S(1)}, u32[]{:S(2)}, u32[]{:S(2)}) collective-permute-start(bf16[1024,128]{1,0:T(8,128)(2,1)S(1)} %collective-permute-done.21.refs_5_), channel_id=1, source_target_pairs={{0,56},{4,60},{8,0},{12,4},{16,8},{20,12},{24,16},{28,20},{32,24},... | collective-permute-start | bytes 786440 | tf_op jit(solution)/shard_map/ppermute | solution.py:315
  69.6 8.1 %collective-permute-start.15 = (bf16[1040,512]{1,0:T(8,128)(2,1)S(1)}, bf16[1040,512]{1,0:T(8,128)(2,1)S(1)}, u32[]{:S(2)}, u32[]{:S(2)}) collective-permute-start(bf16[1040,512]{1,0:T(8,128)(2,1)S(1)} %shard_map.58), channel_id=1, source_target_pairs={{0,4},{4,0},{8,12},{12,8},{16,20},{20,16},{24,28},{28,24},{32,36},... | collective-permute-start | bytes 3194888 | tf_op jit(solution)/shard_map/ppermute | solution.py:359
  80.0 7.7 %collective-permute-start.16 = (bf16[512,128]{1,0:T(8,128)(2,1)S(1)}, bf16[512,128]{1,0:T(8,128)(2,1)S(1)}, u32[]{:S(2)}, u32[]{:S(2)}) collective-permute-start(bf16[512,128]{1,0:T(8,128)(2,1)S(1)} %get-tuple-element.55), channel_id=1, source_target_pairs={{0,1},{1,2},{2,3},{3,0},{4,5},{5,6},{6,7},{7,4},{8,9},{9,10},{10,1... | collective-permute-start | bytes 393224 | tf_op jit(solution)/shard_map/ppermute | solution.py:319
  81.3 6.4 %collective-permute-start.17 = (bf16[512,128]{1,0:T(8,128)(2,1)S(1)}, bf16[512,128]{1,0:T(8,128)(2,1)S(1)}, u32[]{:S(2)}, u32[]{:S(2)}) collective-permute-start(bf16[512,128]{1,0:T(8,128)(2,1)S(1)} %get-tuple-element.56), channel_id=1, source_target_pairs={{0,3},{1,0},{2,1},{3,2},{4,7},{5,4},{6,5},{7,6},{8,11},{9,8},{10,9... | collective-permute-start | bytes 393224 | tf_op jit(solution)/shard_map/ppermute | solution.py:319
  85.0 5.7 %collective-permute-start.24 = (bf16[512,128]{1,0:T(8,128)(2,1)S(1)}, bf16[512,128]{1,0:T(8,128)(2,1)S(1)}, u32[]{:S(2)}, u32[]{:S(2)}) collective-permute-start(bf16[512,128]{1,0:T(8,128)(2,1)S(1)} %get-tuple-element.64), channel_id=1, source_target_pairs={{0,1},{1,2},{2,3},{3,0},{4,5},{5,6},{6,7},{7,4},{8,9},{9,10},{10,1... | collective-permute-start | bytes 393224 | tf_op jit(solution)/shard_map/ppermute | solution.py:319
  85.0 5.6 %collective-permute-start.25 = (bf16[512,128]{1,0:T(8,128)(2,1)S(1)}, bf16[512,128]{1,0:T(8,128)(2,1)S(1)}, u32[]{:S(2)}, u32[]{:S(2)}) collective-permute-start(bf16[512,128]{1,0:T(8,128)(2,1)S(1)} %get-tuple-element.65), channel_id=1, source_target_pairs={{0,3},{1,0},{2,1},{3,2},{4,7},{5,4},{6,5},{7,6},{8,11},{9,8},{10,9... | collective-permute-start | bytes 393224 | tf_op jit(solution)/shard_map/ppermute | solution.py:319
  87.8 7.9 %collective-permute-start.18 = (bf16[1024,128]{1,0:T(8,128)(2,1)S(1)}, bf16[1024,128]{1,0:T(8,128)(2,1)S(1)}, u32[]{:S(2)}, u32[]{:S(2)}) collective-permute-start(bf16[1024,128]{1,0:T(8,128)(2,1)S(1)} %get-tuple-element.57), channel_id=1, source_target_pairs={{0,1},{1,2},{2,3},{3,0},{4,5},{5,6},{6,7},{7,4},{8,9},{9,10},{10,1... | collective-permute-start | bytes 786440 | tf_op jit(solution)/shard_map/ppermute | solution.py:319
  87.9 7.8 %collective-permute-start.19 = (bf16[1024,128]{1,0:T(8,128)(2,1)S(1)}, bf16[1024,128]{1,0:T(8,128)(2,1)S(1)}, u32[]{:S(2)}, u32[]{:S(2)}) collective-permute-start(bf16[1024,128]{1,0:T(8,128)(2,1)S(1)} %get-tuple-element.58), channel_id=1, source_target_pairs={{0,3},{1,0},{2,1},{3,2},{4,7},{5,4},{6,5},{7,6},{8,11},{9,8},{10,9... | collective-permute-start | bytes 786440 | tf_op jit(solution)/shard_map/ppermute | solution.py:319
  90.8 10.6 %collective-permute-start.26 = (bf16[1024,128]{1,0:T(8,128)(2,1)S(1)}, bf16[1024,128]{1,0:T(8,128)(2,1)S(1)}, u32[]{:S(2)}, u32[]{:S(2)}) collective-permute-start(bf16[1024,128]{1,0:T(8,128)(2,1)S(1)} %get-tuple-element.66), channel_id=1, source_target_pairs={{0,1},{1,2},{2,3},{3,0},{4,5},{5,6},{6,7},{7,4},{8,9},{9,10},{10,1... | collective-permute-start | bytes 786440 | tf_op jit(solution)/shard_map/ppermute | solution.py:319
  90.8 10.5 %collective-permute-start.27 = (bf16[1024,128]{1,0:T(8,128)(2,1)S(1)}, bf16[1024,128]{1,0:T(8,128)(2,1)S(1)}, u32[]{:S(2)}, u32[]{:S(2)}) collective-permute-start(bf16[1024,128]{1,0:T(8,128)(2,1)S(1)} %get-tuple-element.67), channel_id=1, source_target_pairs={{0,3},{1,0},{2,1},{3,2},{4,7},{5,4},{6,5},{7,6},{8,11},{9,8},{10,9... | collective-permute-start | bytes 786440 | tf_op jit(solution)/shard_map/ppermute | solution.py:319
  102.4 27.6 %all-to-all-start.1 = ((bf16[64,32,128]{2,1,0:T(8,128)(2,1)}), bf16[64,32,128]{2,1,0:T(8,128)(2,1)S(1)}, u32[]{:S(2)}, u32[]{:S(2)}) async-start(bf16[64,32,128]{2,1,0:T(8,128)(2,1)} %bitcast.10), calls=%async_computation.1 | async-start | bytes 1048576 | tf_op jit(solution)/shard_map/all_to_all | solution.py:368
  112.8 5.9 %collective-permute-start.28 = (bf16[32,2048]{1,0:T(8,128)(2,1)S(1)}, bf16[32,2048]{1,0:T(8,128)(2,1)S(1)}, u32[]{:S(2)}, u32[]{:S(2)}) collective-permute-start(bf16[32,2048]{1,0:T(8,128)(2,1)S(1)} %get-tuple-element.70), channel_id=1, source_target_pairs={{0,64},{64,128},{128,192},{192,0},{1,65},{65,129},{129,193},{193,1... | collective-permute-start | bytes 393224 | tf_op jit(solution)/shard_map/ppermute | solution.py:319
  114.2 8.5 %collective-permute-start.29 = (bf16[32,2048]{1,0:T(8,128)(2,1)S(1)}, bf16[32,2048]{1,0:T(8,128)(2,1)S(1)}, u32[]{:S(2)}, u32[]{:S(2)}) collective-permute-start(bf16[32,2048]{1,0:T(8,128)(2,1)S(1)} %get-tuple-element.71), channel_id=1, source_target_pairs={{0,128},{64,192},{128,0},{192,64},{1,129},{65,193},{129,1},{193,65... | collective-permute-start | bytes 393224 | tf_op jit(solution)/shard_map/ppermute | solution.py:319
  116.7 6.0 %collective-permute-start.30 = (bf16[32,2048]{1,0:T(8,128)(2,1)S(1)}, bf16[32,2048]{1,0:T(8,128)(2,1)S(1)}, u32[]{:S(2)}, u32[]{:S(2)}) collective-permute-start(bf16[32,2048]{1,0:T(8,128)(2,1)S(1)} %get-tuple-element.72), channel_id=1, source_target_pairs={{0,192},{64,0},{128,64},{192,128},{1,193},{65,1},{129,65},{193,129... | collective-permute-start | bytes 393224 | tf_op jit(solution)/shard_map/ppermute | solution.py:319
  (3 other events, 32.7 us)

commit v5 on v4

--- a/solution.py
+++ b/solution.py
@@ -336,7 +336,6 @@
 
     ring(0, 1)
     ring(1, 1)
-    (gathered[1][1], gathered[1][7], b_own) = lax.optimization_barrier((gathered[1][1], gathered[1][7], b_own))
     behind, ahead = turn(b_own, "row", 1), turn(b_own, "row", -1)
     ring(0, 2)
     ring(1, 2)

time: 132 us -> 129 us (0.977)
  waiting for transfers between devices: 52 us -> 44.2 us
  starting transfers between devices: 63 us -> 68.2 us
    ppermute x14, waiting for transfers between devices: 30.7 us -> 12 us  [turn_z(): return lax.ppermute(value, 'col', pairs)]
    all_to_all x1, waiting for transfers between devices: 0.01 us -> 11.9 us  [per_device(): b_own = lax.all_to_all(b_send, 'col', 0, 0)]
    ppermute x14, starting transfers between devices: 13.5 us -> 17.4 us  [turn_z(): return lax.ppermute(value, 'col', pairs)]
where the time goes in v5:
time: 129 us
  starting transfers between devices  68.2 us (53%)
  waiting for transfers between devices  44.2 us (34%)
  Pallas kernels  16.1 us (12%)
    ppermute x15, starting transfers between devices, turn(): return lax.ppermute(value, axis, [(i, (i + shift) % 4) for i in range(4)])  24.3 us
    ppermute x14, starting transfers between devices, turn_z(): return lax.ppermute(value, 'col', pairs)  17.4 us
    ppermute x15, waiting for transfers between devices, turn(): return lax.ppermute(value, axis, [(i, (i + shift) % 4) for i in range(4)])  12.8 us
    ppermute x14, waiting for transfers between devices, turn_z(): return lax.ppermute(value, 'col', pairs)  12 us
    all_to_all x1, waiting for transfers between devices, per_device(): b_own = lax.all_to_all(b_send, 'col', 0, 0)  11.9 us
    all_to_all x1, starting transfers between devices, per_device(): own = lax.all_to_all(product.reshape(64, 32, 128), ('col', 'layer'), 0, 0)  10.7 us
    all_to_all x1, starting transfers between devices, per_device(): b_own = lax.all_to_all(b_send, 'col', 0, 0)  9.99 us
    all_to_all x1, waiting for transfers between devices, per_device(): own = lax.all_to_all(product.reshape(64, 32, 128), ('col', 'layer'), 0, 0)  7.43 us
  transfers between devices with their start and end apart: 33, of which 12 were waited for; matrix products, arithmetic and copies ran while one was open for 0% of the time, Pallas kernels for 7%

profile of v5, /device:TPU:1, one launch (start us, length us, event | category | flops | bytes accessed | tf_op | source)
XLA Modules:
  0.0 128.7 jit_solution(12314026810263052565)
XLA Ops:
  0.0 2.0 %shard_map.55 = (bf16[1040,128]{1,0:T(8,128)(2,1)}, bf16[1024,128]{1,0:T(8,128)(2,1)}) custom-call(s32[1,16]{1,0:T(1,128)} %bitcast.21, bf16[2048,128]{1,0:T(8,128)(2,1)} %bitcast.17, s32[4,16]{1,0:T(4,128)} %bitcast.19), custom_call_target="tpu_custom_call" | custom-call | flops 262144 | bytes 1048576 | tf_op jit(solution)/shard_map/pallas_call | solution.py:63
  2.0 2.1 %shard_map.56 = bf16[16,64,256]{2,1,0:T(8,128)(2,1)} custom-call(s32[4,4]{1,0:T(4,128)} %bitcast.20, bf16[512,512]{1,0:T(8,128)(2,1)} %bitcast.18), custom_call_target="tpu_custom_call" | custom-call | flops 262144 | bytes 1048576 | tf_op jit(solution)/shard_map/pallas_call | solution.py:93
  4.1 10.0 %all-to-all-start = ((bf16[16,64,256]{2,1,0:T(8,128)(2,1)}), bf16[16,64,256]{2,1,0:T(8,128)(2,1)S(1)}, u32[]{:S(2)}, u32[]{:S(2)}) async-start(bf16[16,64,256]{2,1,0:T(8,128)(2,1)} %shard_map.56), calls=%async_computation | async-start | bytes 1048576 | tf_op jit(solution)/shard_map/all_to_all | solution.py:327
  14.1 2.7 %collective-permute-start.9 = (bf16[1024,128]{1,0:T(8,128)(2,1)S(1)}, bf16[1024,128]{1,0:T(8,128)(2,1)S(1)}, u32[]{:S(2)}, u32[]{:S(2)}) collective-permute-start(bf16[1024,128]{1,0:T(8,128)(2,1)S(1)} %copy-done.1), channel_id=1, source_target_pairs={{0,56},{4,60},{8,0},{12,4},{16,8},{20,12},{24,16},{28,20},{32,24},... | collective-permute-start | bytes 786440 | tf_op jit(solution)/shard_map/ppermute | solution.py:315
  17.1 2.5 %collective-permute-start.4 = (bf16[1040,128]{1,0:T(8,128)(2,1)S(1)}, bf16[1040,128]{1,0:T(8,128)(2,1)S(1)}, u32[]{:S(2)}, u32[]{:S(2)}) collective-permute-start(bf16[1040,128]{1,0:T(8,128)(2,1)S(1)} %copy-done), channel_id=1, source_target_pairs={{0,56},{4,60},{8,0},{12,4},{16,8},{20,12},{24,16},{28,20},{32,24},... | collective-permute-start | bytes 798728 | tf_op jit(solution)/shard_map/ppermute | solution.py:315
  19.5 11.9 %all-to-all-done = bf16[16,64,256]{2,1,0:T(8,128)(2,1)S(1)} async-done(((bf16[16,64,256]{2,1,0:T(8,128)(2,1)}), bf16[16,64,256]{2,1,0:T(8,128)(2,1)S(1)}, u32[]{:S(2)}, u32[]{:S(2)}) %all-to-all-start) | async-done | bytes 524320 | tf_op jit(solution)/shard_map/all_to_all | solution.py:327
  33.4 2.7 %collective-permute-start.12 = (bf16[16,64,256]{2,1,0:T(8,128)(2,1)S(1)}, bf16[16,64,256]{2,1,0:T(8,128)(2,1)S(1)}, u32[]{:S(2)}, u32[]{:S(2)}) collective-permute-start(bf16[16,64,256]{2,1,0:T(8,128)(2,1)S(1)} %all-to-all-done), channel_id=1, source_target_pairs={{0,192},{64,0},{128,64},{192,128},{1,193},{65,1},{129,65},{193,129... | collective-permute-start | bytes 1572872 | tf_op jit(solution)/shard_map/ppermute | solution.py:319
  37.3 2.9 %collective-permute-done.7.refs_1_ = bf16[1024,128]{1,0:T(8,128)(2,1)S(1)} collective-permute-done((bf16[1024,128]{1,0:T(8,128)(2,1)S(1)}, bf16[1024,128]{1,0:T(8,128)(2,1)S(1)}, u32[]{:S(2)}, u32[]{:S(2)}) %collective-permute-start.7) | collective-permute-done | bytes 262176 | tf_op jit(solution)/shard_map/ppermute | solution.py:315
  41.7 5.0 %collective-permute-done.10.refs_6_ = bf16[1024,128]{1,0:T(8,128)(2,1)S(1)} collective-permute-done((bf16[1024,128]{1,0:T(8,128)(2,1)S(1)}, bf16[1024,128]{1,0:T(8,128)(2,1)S(1)}, u32[]{:S(2)}, u32[]{:S(2)}) %collective-permute-start.10) | collective-permute-done | bytes 262176 | tf_op jit(solution)/shard_map/ppermute | solution.py:315
  46.7 2.4 %collective-permute-start.5 = (bf16[1040,128]{1,0:T(8,128)(2,1)S(1)}, bf16[1040,128]{1,0:T(8,128)(2,1)S(1)}, u32[]{:S(2)}, u32[]{:S(2)}) collective-permute-start(bf16[1040,128]{1,0:T(8,128)(2,1)S(1)} %collective-permute-done.4.refs_7_), channel_id=1, source_target_pairs={{0,56},{4,60},{8,0},{12,4},{16,8},{20,12},{24,16},{28,20},{32,24},... | collective-permute-start | bytes 798728 | tf_op jit(solution)/shard_map/ppermute | solution.py:315
  49.1 1.9 %collective-permute-done.8.refs_2_ = bf16[1024,128]{1,0:T(8,128)(2,1)S(1)} collective-permute-done((bf16[1024,128]{1,0:T(8,128)(2,1)S(1)}, bf16[1024,128]{1,0:T(8,128)(2,1)S(1)}, u32[]{:S(2)}, u32[]{:S(2)}) %collective-permute-start.8) | collective-permute-done | bytes 262176 | tf_op jit(solution)/shard_map/ppermute | solution.py:315
  51.1 1.3 %collective-permute-start.13 = (bf16[8,64,256]{2,1,0:T(8,128)(2,1)S(1)}, bf16[8,64,256]{2,1,0:T(8,128)(2,1)S(1)}, u32[]{:S(2)}, u32[]{:S(2)}) collective-permute-start(bf16[8,64,256]{2,1,0:T(8,128)(2,1)S(1)} %slice.6), channel_id=1, source_target_pairs={{0,64},{64,128},{128,192},{192,0},{1,65},{65,129},{129,193},{193,1... | collective-permute-start | bytes 786440 | tf_op jit(solution)/shard_map/ppermute | solution.py:319
  52.4 1.8 %collective-permute-start.21 = (bf16[1024,128]{1,0:T(8,128)(2,1)S(1)}, bf16[1024,128]{1,0:T(8,128)(2,1)S(1)}, u32[]{:S(2)}, u32[]{:S(2)}) collective-permute-start(bf16[1024,128]{1,0:T(8,128)(2,1)S(1)} %collective-permute-done.10.refs_6_), channel_id=1, source_target_pairs={{0,56},{4,60},{8,0},{12,4},{16,8},{20,12},{24,16},{28,20},{32,24},... | collective-permute-start | bytes 786440 | tf_op jit(solution)/shard_map/ppermute | solution.py:315
  54.2 1.8 %collective-permute-start.6 = (bf16[1040,128]{1,0:T(8,128)(2,1)S(1)}, bf16[1040,128]{1,0:T(8,128)(2,1)S(1)}, u32[]{:S(2)}, u32[]{:S(2)}) collective-permute-start(bf16[1040,128]{1,0:T(8,128)(2,1)S(1)} %collective-permute-done.5.refs_6_), channel_id=1, source_target_pairs={{0,56},{4,60},{8,0},{12,4},{16,8},{20,12},{24,16},{28,20},{32,24},... | collective-permute-start | bytes 798728 | tf_op jit(solution)/shard_map/ppermute | solution.py:315
  56.0 3.0 %collective-permute-start.14 = (bf16[8,64,256]{2,1,0:T(8,128)(2,1)S(1)}, bf16[8,64,256]{2,1,0:T(8,128)(2,1)S(1)}, u32[]{:S(2)}, u32[]{:S(2)}) collective-permute-start(bf16[8,64,256]{2,1,0:T(8,128)(2,1)S(1)} %slice.7), channel_id=1, source_target_pairs={{0,192},{64,0},{128,64},{192,128},{1,193},{65,1},{129,65},{193,129... | collective-permute-start | bytes 786440 | tf_op jit(solution)/shard_map/ppermute | solution.py:319
  59.2 3.1 %collective-permute-start.22 = (bf16[1024,128]{1,0:T(8,128)(2,1)S(1)}, bf16[1024,128]{1,0:T(8,128)(2,1)S(1)}, u32[]{:S(2)}, u32[]{:S(2)}) collective-permute-start(bf16[1024,128]{1,0:T(8,128)(2,1)S(1)} %collective-permute-done.21.refs_5_), channel_id=1, source_target_pairs={{0,56},{4,60},{8,0},{12,4},{16,8},{20,12},{24,16},{28,20},{32,24},... | collective-permute-start | bytes 786440 | tf_op jit(solution)/shard_map/ppermute | solution.py:315
  63.1 1.5 %collective-permute-done.6.refs_5_ = bf16[1040,128]{1,0:T(8,128)(2,1)S(1)} collective-permute-done((bf16[1040,128]{1,0:T(8,128)(2,1)S(1)}, bf16[1040,128]{1,0:T(8,128)(2,1)S(1)}, u32[]{:S(2)}, u32[]{:S(2)}) %collective-permute-start.6) | collective-permute-done | bytes 266272 | tf_op jit(solution)/shard_map/ppermute | solution.py:315
  64.6 2.2 %shard_map.58 = bf16[1040,512]{1,0:T(8,128)(2,1)S(1)} custom-call(bf16[1040,128]{1,0:T(8,128)(2,1)S(1)} %copy-done, bf16[1040,128]{1,0:T(8,128)(2,1)S(1)} %collective-permute-done.refs_1_, bf16[1040,128]{1,0:T(8,128)(2,1)S(1)} %collective-permute-done.1.refs_2_, bf16[1040,128]{1,0:T(8,128)(2,1)S(1)} %collective-permute-done.2.refs_3_, ...), custom_call_target="tpu_custom_call" | custom-call | flops 1073741824 | bytes 3145728 | tf_op jit(solution)/shard_map/pallas_call | solution.py:183
  66.8 4.7 %collective-permute-start.15 = (bf16[1040,512]{1,0:T(8,128)(2,1)S(1)}, bf16[1040,512]{1,0:T(8,128)(2,1)S(1)}, u32[]{:S(2)}, u32[]{:S(2)}) collective-permute-start(bf16[1040,512]{1,0:T(8,128)(2,1)S(1)} %shard_map.58), channel_id=1, source_target_pairs={{0,4},{4,0},{8,12},{12,8},{16,20},{20,16},{24,28},{28,24},{32,36},... | collective-permute-start | bytes 3194888 | tf_op jit(solution)/shard_map/ppermute | solution.py:358
  71.5 2.1 %shard_map.61 = bf16[1024,512]{1,0:T(8,128)(2,1)S(1)} custom-call(bf16[1024,128]{1,0:T(8,128)(2,1)S(1)} %copy-done.1, bf16[1024,128]{1,0:T(8,128)(2,1)S(1)} %collective-permute-done.7.refs_1_, bf16[1024,128]{1,0:T(8,128)(2,1)S(1)} %collective-permute-done.8.refs_2_, bf16[1024,128]{1,0:T(8,128)(2,1)S(1)} %collective-permute-done.20.refs_3_, ...), custom_call_target="tpu_custom_call" | custom-call | flops 1073741824 | bytes 3145728 | tf_op jit(solution)/shard_map/pallas_call | solution.py:183
  74.9 2.2 %shard_map.59 = (f32[1024,128]{1,0:T(8,128)S(1)}, f32[1024,128]{1,0:T(8,128)S(1)}, f32[1024,128]{1,0:T(8,128)S(1)}, bf16[512,128]{1,0:T(8,128)(2,1)S(1)}, bf16[5...) custom-call(bf16[1040,128]{1,0:T(8,128)(2,1)S(1)} %copy-done, bf16[1040,128]{1,0:T(8,128)(2,1)S(1)} %collective-permute-done.refs_1_, ...), custom_call_target="tpu_custom_call" | custom-call | flops 1073741824 | bytes 4194304 | tf_op jit(solution)/shard_map/pallas_call | solution.py:219
  78.4 1.5 %collective-permute-start.17 = (bf16[512,128]{1,0:T(8,128)(2,1)S(1)}, bf16[512,128]{1,0:T(8,128)(2,1)S(1)}, u32[]{:S(2)}, u32[]{:S(2)}) collective-permute-start(bf16[512,128]{1,0:T(8,128)(2,1)S(1)} %get-tuple-element.50), channel_id=1, source_target_pairs={{0,3},{1,0},{2,1},{3,2},{4,7},{5,4},{6,5},{7,6},{8,11},{9,8},{10,9... | collective-permute-start | bytes 393224 | tf_op jit(solution)/shard_map/ppermute | solution.py:319
  79.9 2.2 %shard_map.62 = (f32[1024,128]{1,0:T(8,128)S(1)}, f32[1024,128]{1,0:T(8,128)S(1)}, f32[1024,128]{1,0:T(8,128)S(1)}, bf16[512,128]{1,0:T(8,128)(2,1)S(1)}, bf16[512,128]{1,0:T(8,128)(2,1)S(1)}) custom-call(bf16[1024,128]{1,0:T(8,128)(2,1)S(1)} %copy-done.1, bf16[1024,128]{1,0:T(8,128)(2,1)S(1)} %collective-permute-done.7.refs_1_, ...), custom_call_target="tpu_custom_call" | custom-call | flops 1073741824 | bytes 4194304 | tf_op jit(solution)/shard_map/pallas_call | solution.py:219
  82.1 2.7 %collective-permute-start.25 = (bf16[512,128]{1,0:T(8,128)(2,1)S(1)}, bf16[512,128]{1,0:T(8,128)(2,1)S(1)}, u32[]{:S(2)}, u32[]{:S(2)}) collective-permute-start(bf16[512,128]{1,0:T(8,128)(2,1)S(1)} %get-tuple-element.59), channel_id=1, source_target_pairs={{0,3},{1,0},{2,1},{3,2},{4,7},{5,4},{6,5},{7,6},{8,11},{9,8},{10,9... | collective-permute-start | bytes 393224 | tf_op jit(solution)/shard_map/ppermute | solution.py:319
  85.0 2.7 %collective-permute-start.19 = (bf16[1024,128]{1,0:T(8,128)(2,1)S(1)}, bf16[1024,128]{1,0:T(8,128)(2,1)S(1)}, u32[]{:S(2)}, u32[]{:S(2)}) collective-permute-start(bf16[1024,128]{1,0:T(8,128)(2,1)S(1)} %get-tuple-element.52), channel_id=1, source_target_pairs={{0,3},{1,0},{2,1},{3,2},{4,7},{5,4},{6,5},{7,6},{8,11},{9,8},{10,9... | collective-permute-start | bytes 786440 | tf_op jit(solution)/shard_map/ppermute | solution.py:319
  87.9 2.7 %collective-permute-start.27 = (bf16[1024,128]{1,0:T(8,128)(2,1)S(1)}, bf16[1024,128]{1,0:T(8,128)(2,1)S(1)}, u32[]{:S(2)}, u32[]{:S(2)}) collective-permute-start(bf16[1024,128]{1,0:T(8,128)(2,1)S(1)} %get-tuple-element.61), channel_id=1, source_target_pairs={{0,3},{1,0},{2,1},{3,2},{4,7},{5,4},{6,5},{7,6},{8,11},{9,8},{10,9... | collective-permute-start | bytes 786440 | tf_op jit(solution)/shard_map/ppermute | solution.py:319
  90.6 2.2 %collective-permute-done.18.refs_2_ = bf16[1024,128]{1,0:T(8,128)(2,1)S(1)} collective-permute-done((bf16[1024,128]{1,0:T(8,128)(2,1)S(1)}, bf16[1024,128]{1,0:T(8,128)(2,1)S(1)}, u32[]{:S(2)}, u32[]{:S(2)}) %collective-permute-start.18) | collective-permute-done | bytes 262176 | tf_op jit(solution)/shard_map/ppermute | solution.py:319
  92.8 5.6 %collective-permute-done.26.refs_5_ = bf16[1024,128]{1,0:T(8,128)(2,1)S(1)} collective-permute-done((bf16[1024,128]{1,0:T(8,128)(2,1)S(1)}, bf16[1024,128]{1,0:T(8,128)(2,1)S(1)}, u32[]{:S(2)}, u32[]{:S(2)}) %collective-permute-start.26) | collective-permute-done | bytes 262176 | tf_op jit(solution)/shard_map/ppermute | solution.py:319
  99.5 10.7 %all-to-all-start.1 = ((bf16[64,32,128]{2,1,0:T(8,128)(2,1)}), bf16[64,32,128]{2,1,0:T(8,128)(2,1)S(1)}, u32[]{:S(2)}, u32[]{:S(2)}) async-start(bf16[64,32,128]{2,1,0:T(8,128)(2,1)} %bitcast.10), calls=%async_computation.1 | async-start | bytes 1048576 | tf_op jit(solution)/shard_map/all_to_all | solution.py:367
  111.4 2.6 %collective-permute-start.29 = (bf16[32,2048]{1,0:T(8,128)(2,1)S(1)}, bf16[32,2048]{1,0:T(8,128)(2,1)S(1)}, u32[]{:S(2)}, u32[]{:S(2)}) collective-permute-start(bf16[32,2048]{1,0:T(8,128)(2,1)S(1)} %get-tuple-element.65), channel_id=1, source_target_pairs={{0,128},{64,192},{128,0},{192,64},{1,129},{65,193},{129,1},{193,65... | collective-permute-start | bytes 393224 | tf_op jit(solution)/shard_map/ppermute | solution.py:319
  116.1 3.9 %collective-permute-done.29.refs_2_ = bf16[32,2048]{1,0:T(8,128)(2,1)S(1)} collective-permute-done((bf16[32,2048]{1,0:T(8,128)(2,1)S(1)}, bf16[32,2048]{1,0:T(8,128)(2,1)S(1)}, u32[]{:S(2)}, u32[]{:S(2)}) %collective-permute-start.29) | collective-permute-done | bytes 131104 | tf_op jit(solution)/shard_map/ppermute | solution.py:319
  120.0 7.4 %all-to-all-done.1.own = bf16[64,32,128]{2,1,0:T(8,128)(2,1)S(1)} async-done(((bf16[64,32,128]{2,1,0:T(8,128)(2,1)}), bf16[64,32,128]{2,1,0:T(8,128)(2,1)S(1)}, u32[]{:S(2)}, u32[]{:S(2)}) %all-to-all-start.1) | async-done | bytes 524320 | tf_op jit(solution)/shard_map/all_to_all | solution.py:367
  (51 shorter events, 14.7 us)
Async XLA Ops:
  4.1 27.3 %all-to-all-start = ((bf16[16,64,256]{2,1,0:T(8,128)(2,1)}), bf16[16,64,256]{2,1,0:T(8,128)(2,1)S(1)}, u32[]{:S(2)}, u32[]{:S(2)}) async-start(bf16[16,64,256]{2,1,0:T(8,128)(2,1)} %shard_map.56), calls=%async_computation | async-start | bytes 1048576 | tf_op jit(solution)/shard_map/all_to_all | solution.py:327
  14.1 19.2 %collective-permute-start.9 = (bf16[1024,128]{1,0:T(8,128)(2,1)S(1)}, bf16[1024,128]{1,0:T(8,128)(2,1)S(1)}, u32[]{:S(2)}, u32[]{:S(2)}) collective-permute-start(bf16[1024,128]{1,0:T(8,128)(2,1)S(1)} %copy-done.1), channel_id=1, source_target_pairs={{0,56},{4,60},{8,0},{12,4},{16,8},{20,12},{24,16},{28,20},{32,24},... | collective-permute-start | bytes 786440 | tf_op jit(solution)/shard_map/ppermute | solution.py:315
  16.8 19.3 %collective-permute-start = (bf16[1040,128]{1,0:T(8,128)(2,1)S(1)}, bf16[1040,128]{1,0:T(8,128)(2,1)S(1)}, u32[]{:S(2)}, u32[]{:S(2)}) collective-permute-start(bf16[1040,128]{1,0:T(8,128)(2,1)S(1)} %copy-done), channel_id=1, source_target_pairs={{0,8},{4,12},{8,16},{12,20},{16,24},{20,28},{24,32},{28,36},{32,40... | collective-permute-start | bytes 798728 | tf_op jit(solution)/shard_map/ppermute | solution.py:315
  16.8 23.4 %collective-permute-start.7 = (bf16[1024,128]{1,0:T(8,128)(2,1)S(1)}, bf16[1024,128]{1,0:T(8,128)(2,1)S(1)}, u32[]{:S(2)}, u32[]{:S(2)}) collective-permute-start(bf16[1024,128]{1,0:T(8,128)(2,1)S(1)} %copy-done.1), channel_id=1, source_target_pairs={{0,8},{4,12},{8,16},{12,20},{16,24},{20,28},{24,32},{28,36},{32,40... | collective-permute-start | bytes 786440 | tf_op jit(solution)/shard_map/ppermute | solution.py:315
  17.1 24.4 %collective-permute-start.4 = (bf16[1040,128]{1,0:T(8,128)(2,1)S(1)}, bf16[1040,128]{1,0:T(8,128)(2,1)S(1)}, u32[]{:S(2)}, u32[]{:S(2)}) collective-permute-start(bf16[1040,128]{1,0:T(8,128)(2,1)S(1)} %copy-done), channel_id=1, source_target_pairs={{0,56},{4,60},{8,0},{12,4},{16,8},{20,12},{24,16},{28,20},{32,24},... | collective-permute-start | bytes 798728 | tf_op jit(solution)/shard_map/ppermute | solution.py:315
  31.5 19.6 %collective-permute-start.11 = (bf16[16,64,256]{2,1,0:T(8,128)(2,1)S(1)}, bf16[16,64,256]{2,1,0:T(8,128)(2,1)S(1)}, u32[]{:S(2)}, u32[]{:S(2)}) collective-permute-start(bf16[16,64,256]{2,1,0:T(8,128)(2,1)S(1)} %all-to-all-done), channel_id=1, source_target_pairs={{0,64},{64,128},{128,192},{192,0},{1,65},{65,129},{129,193},{193,1... | collective-permute-start | bytes 1572872 | tf_op jit(solution)/shard_map/ppermute | solution.py:319
  33.4 17.7 %collective-permute-start.12 = (bf16[16,64,256]{2,1,0:T(8,128)(2,1)S(1)}, bf16[16,64,256]{2,1,0:T(8,128)(2,1)S(1)}, u32[]{:S(2)}, u32[]{:S(2)}) collective-permute-start(bf16[16,64,256]{2,1,0:T(8,128)(2,1)S(1)} %all-to-all-done), channel_id=1, source_target_pairs={{0,192},{64,0},{128,64},{192,128},{1,193},{65,1},{129,65},{193,129... | collective-permute-start | bytes 1572872 | tf_op jit(solution)/shard_map/ppermute | solution.py:319
  36.1 13.0 %collective-permute-start.1 = (bf16[1040,128]{1,0:T(8,128)(2,1)S(1)}, bf16[1040,128]{1,0:T(8,128)(2,1)S(1)}, u32[]{:S(2)}, u32[]{:S(2)}) collective-permute-start(bf16[1040,128]{1,0:T(8,128)(2,1)S(1)} %collective-permute-done.refs_1_), channel_id=1, source_target_pairs={{0,8},{4,12},{8,16},{12,20},{16,24},{20,28},{24,32},{28,36},{32,40... | collective-permute-start | bytes 798728 | tf_op jit(solution)/shard_map/ppermute | solution.py:315
  40.2 6.5 %collective-permute-start.10 = (bf16[1024,128]{1,0:T(8,128)(2,1)S(1)}, bf16[1024,128]{1,0:T(8,128)(2,1)S(1)}, u32[]{:S(2)}, u32[]{:S(2)}) collective-permute-start(bf16[1024,128]{1,0:T(8,128)(2,1)S(1)} %collective-permute-done.9.refs_7_), channel_id=1, source_target_pairs={{0,56},{4,60},{8,0},{12,4},{16,8},{20,12},{24,16},{28,20},{32,24},... | collective-permute-start | bytes 786440 | tf_op jit(solution)/shard_map/ppermute | solution.py:315
  41.4 9.6 %collective-permute-start.8 = (bf16[1024,128]{1,0:T(8,128)(2,1)S(1)}, bf16[1024,128]{1,0:T(8,128)(2,1)S(1)}, u32[]{:S(2)}, u32[]{:S(2)}) collective-permute-start(bf16[1024,128]{1,0:T(8,128)(2,1)S(1)} %collective-permute-done.7.refs_1_), channel_id=1, source_target_pairs={{0,8},{4,12},{8,16},{12,20},{16,24},{20,28},{24,32},{28,36},{32,40... | collective-permute-start | bytes 786440 | tf_op jit(solution)/shard_map/ppermute | solution.py:315
  46.7 7.5 %collective-permute-start.5 = (bf16[1040,128]{1,0:T(8,128)(2,1)S(1)}, bf16[1040,128]{1,0:T(8,128)(2,1)S(1)}, u32[]{:S(2)}, u32[]{:S(2)}) collective-permute-start(bf16[1040,128]{1,0:T(8,128)(2,1)S(1)} %collective-permute-done.4.refs_7_), channel_id=1, source_target_pairs={{0,56},{4,60},{8,0},{12,4},{16,8},{20,12},{24,16},{28,20},{32,24},... | collective-permute-start | bytes 798728 | tf_op jit(solution)/shard_map/ppermute | solution.py:315
  49.1 6.8 %collective-permute-start.2 = (bf16[1040,128]{1,0:T(8,128)(2,1)S(1)}, bf16[1040,128]{1,0:T(8,128)(2,1)S(1)}, u32[]{:S(2)}, u32[]{:S(2)}) collective-permute-start(bf16[1040,128]{1,0:T(8,128)(2,1)S(1)} %collective-permute-done.1.refs_2_), channel_id=1, source_target_pairs={{0,8},{4,12},{8,16},{12,20},{16,24},{20,28},{24,32},{28,36},{32,40... | collective-permute-start | bytes 798728 | tf_op jit(solution)/shard_map/ppermute | solution.py:315
  51.1 7.9 %collective-permute-start.13 = (bf16[8,64,256]{2,1,0:T(8,128)(2,1)S(1)}, bf16[8,64,256]{2,1,0:T(8,128)(2,1)S(1)}, u32[]{:S(2)}, u32[]{:S(2)}) collective-permute-start(bf16[8,64,256]{2,1,0:T(8,128)(2,1)S(1)} %slice.6), channel_id=1, source_target_pairs={{0,64},{64,128},{128,192},{192,0},{1,65},{65,129},{129,193},{193,1... | collective-permute-start | bytes 786440 | tf_op jit(solution)/shard_map/ppermute | solution.py:319
  52.4 6.9 %collective-permute-start.21 = (bf16[1024,128]{1,0:T(8,128)(2,1)S(1)}, bf16[1024,128]{1,0:T(8,128)(2,1)S(1)}, u32[]{:S(2)}, u32[]{:S(2)}) collective-permute-start(bf16[1024,128]{1,0:T(8,128)(2,1)S(1)} %collective-permute-done.10.refs_6_), channel_id=1, source_target_pairs={{0,56},{4,60},{8,0},{12,4},{16,8},{20,12},{24,16},{28,20},{32,24},... | collective-permute-start | bytes 786440 | tf_op jit(solution)/shard_map/ppermute | solution.py:315
  54.2 10.4 %collective-permute-start.6 = (bf16[1040,128]{1,0:T(8,128)(2,1)S(1)}, bf16[1040,128]{1,0:T(8,128)(2,1)S(1)}, u32[]{:S(2)}, u32[]{:S(2)}) collective-permute-start(bf16[1040,128]{1,0:T(8,128)(2,1)S(1)} %collective-permute-done.5.refs_6_), channel_id=1, source_target_pairs={{0,56},{4,60},{8,0},{12,4},{16,8},{20,12},{24,16},{28,20},{32,24},... | collective-permute-start | bytes 798728 | tf_op jit(solution)/shard_map/ppermute | solution.py:315
  55.9 8.7 %collective-permute-start.3 = (bf16[1040,128]{1,0:T(8,128)(2,1)S(1)}, bf16[1040,128]{1,0:T(8,128)(2,1)S(1)}, u32[]{:S(2)}, u32[]{:S(2)}) collective-permute-start(bf16[1040,128]{1,0:T(8,128)(2,1)S(1)} %collective-permute-done.2.refs_3_), channel_id=1, source_target_pairs={{0,8},{4,12},{8,16},{12,20},{16,24},{20,28},{24,32},{28,36},{32,40... | collective-permute-start | bytes 798728 | tf_op jit(solution)/shard_map/ppermute | solution.py:315
  56.0 6.4 %collective-permute-start.14 = (bf16[8,64,256]{2,1,0:T(8,128)(2,1)S(1)}, bf16[8,64,256]{2,1,0:T(8,128)(2,1)S(1)}, u32[]{:S(2)}, u32[]{:S(2)}) collective-permute-start(bf16[8,64,256]{2,1,0:T(8,128)(2,1)S(1)} %slice.7), channel_id=1, source_target_pairs={{0,192},{64,0},{128,64},{192,128},{1,193},{65,1},{129,65},{193,129... | collective-permute-start | bytes 786440 | tf_op jit(solution)/shard_map/ppermute | solution.py:319
  59.0 12.5 %collective-permute-start.20 = (bf16[1024,128]{1,0:T(8,128)(2,1)S(1)}, bf16[1024,128]{1,0:T(8,128)(2,1)S(1)}, u32[]{:S(2)}, u32[]{:S(2)}) collective-permute-start(bf16[1024,128]{1,0:T(8,128)(2,1)S(1)} %collective-permute-done.8.refs_2_), channel_id=1, source_target_pairs={{0,8},{4,12},{8,16},{12,20},{16,24},{20,28},{24,32},{28,36},{32,40... | collective-permute-start | bytes 786440 | tf_op jit(solution)/shard_map/ppermute | solution.py:315
  59.2 12.3 %collective-permute-start.22 = (bf16[1024,128]{1,0:T(8,128)(2,1)S(1)}, bf16[1024,128]{1,0:T(8,128)(2,1)S(1)}, u32[]{:S(2)}, u32[]{:S(2)}) collective-permute-start(bf16[1024,128]{1,0:T(8,128)(2,1)S(1)} %collective-permute-done.21.refs_5_), channel_id=1, source_target_pairs={{0,56},{4,60},{8,0},{12,4},{16,8},{20,12},{24,16},{28,20},{32,24},... | collective-permute-start | bytes 786440 | tf_op jit(solution)/shard_map/ppermute | solution.py:315
  66.8 8.1 %collective-permute-start.15 = (bf16[1040,512]{1,0:T(8,128)(2,1)S(1)}, bf16[1040,512]{1,0:T(8,128)(2,1)S(1)}, u32[]{:S(2)}, u32[]{:S(2)}) collective-permute-start(bf16[1040,512]{1,0:T(8,128)(2,1)S(1)} %shard_map.58), channel_id=1, source_target_pairs={{0,4},{4,0},{8,12},{12,8},{16,20},{20,16},{24,28},{28,24},{32,36},... | collective-permute-start | bytes 3194888 | tf_op jit(solution)/shard_map/ppermute | solution.py:358
  73.6 6.2 %collective-permute-start.23 = (bf16[1024,512]{1,0:T(8,128)(2,1)S(1)}, bf16[1024,512]{1,0:T(8,128)(2,1)S(1)}, u32[]{:S(2)}, u32[]{:S(2)}) collective-permute-start(bf16[1024,512]{1,0:T(8,128)(2,1)S(1)} %shard_map.61), channel_id=1, source_target_pairs={{0,4},{4,0},{8,12},{12,8},{16,20},{20,16},{24,28},{28,24},{32,36},... | collective-permute-start | bytes 3145736 | tf_op jit(solution)/shard_map/ppermute | solution.py:358
  77.1 7.7 %collective-permute-start.16 = (bf16[512,128]{1,0:T(8,128)(2,1)S(1)}, bf16[512,128]{1,0:T(8,128)(2,1)S(1)}, u32[]{:S(2)}, u32[]{:S(2)}) collective-permute-start(bf16[512,128]{1,0:T(8,128)(2,1)S(1)} %get-tuple-element.49), channel_id=1, source_target_pairs={{0,1},{1,2},{2,3},{3,0},{4,5},{5,6},{6,7},{7,4},{8,9},{9,10},{10,1... | collective-permute-start | bytes 393224 | tf_op jit(solution)/shard_map/ppermute | solution.py:319
  78.4 6.4 %collective-permute-start.17 = (bf16[512,128]{1,0:T(8,128)(2,1)S(1)}, bf16[512,128]{1,0:T(8,128)(2,1)S(1)}, u32[]{:S(2)}, u32[]{:S(2)}) collective-permute-start(bf16[512,128]{1,0:T(8,128)(2,1)S(1)} %get-tuple-element.50), channel_id=1, source_target_pairs={{0,3},{1,0},{2,1},{3,2},{4,7},{5,4},{6,5},{7,6},{8,11},{9,8},{10,9... | collective-permute-start | bytes 393224 | tf_op jit(solution)/shard_map/ppermute | solution.py:319
  82.0 5.7 %collective-permute-start.24 = (bf16[512,128]{1,0:T(8,128)(2,1)S(1)}, bf16[512,128]{1,0:T(8,128)(2,1)S(1)}, u32[]{:S(2)}, u32[]{:S(2)}) collective-permute-start(bf16[512,128]{1,0:T(8,128)(2,1)S(1)} %get-tuple-element.58), channel_id=1, source_target_pairs={{0,1},{1,2},{2,3},{3,0},{4,5},{5,6},{6,7},{7,4},{8,9},{9,10},{10,1... | collective-permute-start | bytes 393224 | tf_op jit(solution)/shard_map/ppermute | solution.py:319
  84.9 7.9 %collective-permute-start.18 = (bf16[1024,128]{1,0:T(8,128)(2,1)S(1)}, bf16[1024,128]{1,0:T(8,128)(2,1)S(1)}, u32[]{:S(2)}, u32[]{:S(2)}) collective-permute-start(bf16[1024,128]{1,0:T(8,128)(2,1)S(1)} %get-tuple-element.51), channel_id=1, source_target_pairs={{0,1},{1,2},{2,3},{3,0},{4,5},{5,6},{6,7},{7,4},{8,9},{9,10},{10,1... | collective-permute-start | bytes 786440 | tf_op jit(solution)/shard_map/ppermute | solution.py:319
  85.0 7.8 %collective-permute-start.19 = (bf16[1024,128]{1,0:T(8,128)(2,1)S(1)}, bf16[1024,128]{1,0:T(8,128)(2,1)S(1)}, u32[]{:S(2)}, u32[]{:S(2)}) collective-permute-start(bf16[1024,128]{1,0:T(8,128)(2,1)S(1)} %get-tuple-element.52), channel_id=1, source_target_pairs={{0,3},{1,0},{2,1},{3,2},{4,7},{5,4},{6,5},{7,6},{8,11},{9,8},{10,9... | collective-permute-start | bytes 786440 | tf_op jit(solution)/shard_map/ppermute | solution.py:319
  87.8 10.6 %collective-permute-start.26 = (bf16[1024,128]{1,0:T(8,128)(2,1)S(1)}, bf16[1024,128]{1,0:T(8,128)(2,1)S(1)}, u32[]{:S(2)}, u32[]{:S(2)}) collective-permute-start(bf16[1024,128]{1,0:T(8,128)(2,1)S(1)} %get-tuple-element.60), channel_id=1, source_target_pairs={{0,1},{1,2},{2,3},{3,0},{4,5},{5,6},{6,7},{7,4},{8,9},{9,10},{10,1... | collective-permute-start | bytes 786440 | tf_op jit(solution)/shard_map/ppermute | solution.py:319
  87.9 10.5 %collective-permute-start.27 = (bf16[1024,128]{1,0:T(8,128)(2,1)S(1)}, bf16[1024,128]{1,0:T(8,128)(2,1)S(1)}, u32[]{:S(2)}, u32[]{:S(2)}) collective-permute-start(bf16[1024,128]{1,0:T(8,128)(2,1)S(1)} %get-tuple-element.61), channel_id=1, source_target_pairs={{0,3},{1,0},{2,1},{3,2},{4,7},{5,4},{6,5},{7,6},{8,11},{9,8},{10,9... | collective-permute-start | bytes 786440 | tf_op jit(solution)/shard_map/ppermute | solution.py:319
  99.5 27.9 %all-to-all-start.1 = ((bf16[64,32,128]{2,1,0:T(8,128)(2,1)}), bf16[64,32,128]{2,1,0:T(8,128)(2,1)S(1)}, u32[]{:S(2)}, u32[]{:S(2)}) async-start(bf16[64,32,128]{2,1,0:T(8,128)(2,1)} %bitcast.10), calls=%async_computation.1 | async-start | bytes 1048576 | tf_op jit(solution)/shard_map/all_to_all | solution.py:367
  110.2 5.9 %collective-permute-start.28 = (bf16[32,2048]{1,0:T(8,128)(2,1)S(1)}, bf16[32,2048]{1,0:T(8,128)(2,1)S(1)}, u32[]{:S(2)}, u32[]{:S(2)}) collective-permute-start(bf16[32,2048]{1,0:T(8,128)(2,1)S(1)} %get-tuple-element.64), channel_id=1, source_target_pairs={{0,64},{64,128},{128,192},{192,0},{1,65},{65,129},{129,193},{193,1... | collective-permute-start | bytes 393224 | tf_op jit(solution)/shard_map/ppermute | solution.py:319
  111.4 8.6 %collective-permute-start.29 = (bf16[32,2048]{1,0:T(8,128)(2,1)S(1)}, bf16[32,2048]{1,0:T(8,128)(2,1)S(1)}, u32[]{:S(2)}, u32[]{:S(2)}) collective-permute-start(bf16[32,2048]{1,0:T(8,128)(2,1)S(1)} %get-tuple-element.65), channel_id=1, source_target_pairs={{0,128},{64,192},{128,0},{192,64},{1,129},{65,193},{129,1},{193,65... | collective-permute-start | bytes 393224 | tf_op jit(solution)/shard_map/ppermute | solution.py:319
  114.0 6.0 %collective-permute-start.30 = (bf16[32,2048]{1,0:T(8,128)(2,1)S(1)}, bf16[32,2048]{1,0:T(8,128)(2,1)S(1)}, u32[]{:S(2)}, u32[]{:S(2)}) collective-permute-start(bf16[32,2048]{1,0:T(8,128)(2,1)S(1)} %get-tuple-element.66), channel_id=1, source_target_pairs={{0,192},{64,0},{128,64},{192,128},{1,193},{65,1},{129,65},{193,129... | collective-permute-start | bytes 393224 | tf_op jit(solution)/shard_map/ppermute | solution.py:319
  (3 other events, 32.6 us)
